TPU v7x, 128 devices: a whole 4x4x4 slice. The times are simulated.
128 devices in a mesh: row: 8 (over y_hi, x), col: 16 (over y_lo, z, core).
Axes of the slice: x: 4, y: 4 (y_hi: 2, y_lo: 2; y = y_hi * 2 + y_lo), z: 4, core: 2. Of those that a mesh axis runs over, the one named last changes fastest.
Arguments:
- pair: bfloat16 [768, 768, 128], P('row', 'col'), may hold values from -6 to 6
- atoms: bfloat16 [24576, 128], P(('row', 'col')), may hold values from -6 to 6
- token_atoms: int32 [768], replicated, may hold values from 16 to 48, as said below
- pair_gain: float32 [128], replicated, may hold values from 0.1 to 1.9
- tri_proj: bfloat16 [128, 640], replicated, may hold values from -0.5 to 0.5
- tri_out: bfloat16 [128, 128], replicated, may hold values from -0.5 to 0.5
- out_gain: float32 [128], replicated, may hold values from 0.1 to 1.9
- bias_weight: float32 [128, 4], replicated, may hold values from -30 to 30
- atom_gain: float32 [128], replicated, may hold values from 0.1 to 1.9
- atom_proj: bfloat16 [128, 512], replicated, may hold values from -0.5 to 0.5
- atom_out: bfloat16 [128, 128], replicated, may hold values from -0.5 to 0.5
- trans_gain: float32 [128], replicated, may hold values from 0.1 to 1.9
- trans_up: bfloat16 [128, 512], replicated, may hold values from -0.5 to 0.5
- trans_down: bfloat16 [256, 128], replicated, may hold values from -0.375 to 0.375
Outputs:
- pair_out: bfloat16 [768, 768, 128], P('row', 'col')
- atoms_out: bfloat16 [24576, 128], P(('row', 'col'))
Inputs may be any that keep to these rules, and one draw needn't show every extreme that they name: `token_atoms`: every aligned block of 96 tokens holds exactly 3072 atoms in all.
All inputs are finite; a program needn't handle non-finite values.
Results may differ from a plain program's by a relative error of at most 0.012.
Values may be sent and summed in bfloat16 or wider, within the bound.
No kernel may reach another device: no remote copies, remote signals or barrier semaphores. Data moves between devices by JAX's collectives and lax.ppermute only.
A program may use at most 192 MiB of HBM per device.

v0:
```python
import jax
import jax.numpy as jnp
from jax import lax
from jax.sharding import PartitionSpec as P

ATOMS_TOK = 32
QUERIES = 32
KEYS = 128
OFFSETS = 16
HALO = 48


EPSILON = 1e-05
HIGHEST = lax.Precision.HIGHEST


def broadcast(value, axis, source):
    kept = jnp.where(lax.axis_index(axis) == source, value, 0).astype(value.dtype)
    return lax.psum(kept, axis)


def extended_2(block, sides, width):
    for axis, dim in sides:
        count = lax.axis_size(axis)
        forward = [(i, i + 1) for i in range(count - 1)]
        backward = [(target, source) for source, target in forward]
        low = lax.ppermute(
            lax.slice_in_dim(block, block.shape[dim] - width, None, axis=dim), axis, forward
        )
        high = lax.ppermute(lax.slice_in_dim(block, 0, width, axis=dim), axis, backward)
        block = jnp.concatenate([low, block, high], axis=dim)
    return block


def layer_norm(values):
    center = values - jnp.mean(values, -1, keepdims=True)
    return center * lax.rsqrt(jnp.mean(center * center, -1, keepdims=True) + EPSILON)


def on_device(
    pair,
    atoms,
    token_atoms,
    pair_gain,
    tri_proj,
    tri_out,
    out_gain,
    bias_weight,
    atom_gain,
    atom_proj,
    atom_out,
    trans_gain,
    trans_up,
    trans_down,
):
    tile_rows, tile_cols = (pair.shape[0], pair.shape[1])
    tri_width = tri_out.shape[0]
    head_count = bias_weight.shape[1]
    row_id = lax.axis_index("row")
    col_id = lax.axis_index("col")
    normed = layer_norm(pair.astype(jnp.float32))
    tri_input = (normed * pair_gain).astype(jnp.bfloat16)
    project = jnp.einsum("ijc,cd->ijd", tri_input, tri_proj, preferred_element_type=jnp.float32)
    left_edge = (
        jax.nn.sigmoid(project[..., :tri_width]) * project[..., tri_width : 2 * tri_width]
    ).astype(jnp.bfloat16)
    right_edge = (
        jax.nn.sigmoid(project[..., 2 * tri_width : 3 * tri_width])
        * project[..., 3 * tri_width : 4 * tri_width]
    ).astype(jnp.bfloat16)
    out_gate = jax.nn.sigmoid(project[..., 4 * tri_width :])
    tile_bias = jnp.einsum("ijc,ch->ijh", normed, bias_weight, precision=HIGHEST)
    half_band = OFFSETS // 2
    row_global = row_id * tile_rows + jnp.arange(tile_rows, dtype=jnp.int32)
    col_local = (
        row_global[:, None]
        + jnp.arange(OFFSETS, dtype=jnp.int32)[None, :]
        - half_band
        - col_id * tile_cols
    )
    inside = (col_local >= 0) & (col_local < tile_cols)
    picked = jnp.take_along_axis(
        tile_bias, jnp.clip(col_local, 0, tile_cols - 1)[:, :, None], axis=1
    )
    band_part = jnp.where(inside[:, :, None], picked, 0.0)
    band_bias = lax.psum(band_part, "col")
    slice_start = col_id * tile_cols % tile_rows
    root_row = col_id * tile_cols // tile_rows
    whole_rows = lax.all_gather(right_edge, "col", axis=1, tiled=True)
    wanted = lax.dynamic_slice_in_dim(whole_rows, slice_start, tile_cols, 0)
    right_rows = broadcast(wanted, "row", root_row)
    product = jnp.einsum(
        "ikc,jkc->ijc",
        lax.all_gather(left_edge, "col", axis=1, tiled=True),
        right_rows,
        preferred_element_type=jnp.float32,
    )
    tri_normed = (layer_norm(product) * out_gain).astype(jnp.bfloat16)
    update = jnp.einsum("ijc,cd->ijd", tri_normed, tri_out, preferred_element_type=jnp.float32)
    pair_out = (pair.astype(jnp.float32) + out_gate * update).astype(jnp.bfloat16)
    atom_rows, atom_width = atoms.shape
    atom_input = (layer_norm(atoms.astype(jnp.float32)) * atom_gain).astype(jnp.bfloat16)
    projected = jnp.dot(atom_input, atom_proj, preferred_element_type=jnp.float32).astype(
        jnp.bfloat16
    )
    extended = extended_2(projected[:, atom_width : 3 * atom_width], ((("row", "col"), 0),), HALO)
    windows = atom_rows // QUERIES
    key_blocks = KEYS // QUERIES
    strips = extended.reshape(extended.shape[0] // QUERIES, QUERIES, 2 * atom_width)
    head_width = atom_width // head_count
    atom_total = token_atoms.shape[0] * ATOMS_TOK
    token_ends = jnp.cumsum(token_atoms)
    atom_base = lax.axis_index(("row", "col")) * atom_rows
    query_global = atom_base + jnp.arange(atom_rows, dtype=jnp.int32)
    key_global = (
        atom_base
        - HALO
        + QUERIES * jnp.arange(windows, dtype=jnp.int32)[:, None]
        + jnp.arange(KEYS, dtype=jnp.int32)[None, :]
    )
    key_valid = (key_global >= 0) & (key_global < atom_total)
    query_token = jnp.searchsorted(token_ends, query_global, side="right").reshape(windows, QUERIES)
    key_token = jnp.searchsorted(token_ends, jnp.clip(key_global, 0, atom_total - 1), side="right")
    band_row = query_token - row_id * tile_rows
    band_col = jnp.clip(key_token[:, None, :] - query_token[:, :, None] + half_band, 0, OFFSETS - 1)
    head_table = band_bias.transpose(2, 0, 1)
    row_table = head_table[:, band_row]
    pair_bias = jnp.zeros((head_count, windows, QUERIES, KEYS), jnp.float32)
    for offset_at in range(OFFSETS):
        pair_bias = pair_bias + jnp.where(
            (band_col == offset_at)[None], row_table[..., offset_at : offset_at + 1], 0.0
        )
    query_rows = projected[:, :atom_width].reshape(windows, QUERIES, head_count, head_width)
    score_scale = head_width ** (-0.5)
    score_parts = []
    for block_at in range(key_blocks):
        key_block = strips[block_at : block_at + windows, :, :atom_width].reshape(
            windows, QUERIES, head_count, head_width
        )
        score_parts.append(
            jnp.einsum("bqhd,bkhd->hbqk", query_rows, key_block, preferred_element_type=jnp.float32)
        )
    scores = jnp.concatenate(score_parts, axis=-1) * score_scale + pair_bias
    scores = jnp.where(key_valid[None, :, None, :], scores, -jnp.inf)
    row_max = jnp.max(scores, -1, keepdims=True)
    exp_scores = jnp.exp(scores - row_max)
    weights = (exp_scores / jnp.sum(exp_scores, -1, keepdims=True)).astype(jnp.bfloat16)
    mixed_heads = jnp.zeros((windows, QUERIES, head_count, head_width), jnp.float32)
    for block_at in range(key_blocks):
        value_block = strips[block_at : block_at + windows, :, atom_width:].reshape(
            windows, QUERIES, head_count, head_width
        )
        weight_block = weights[..., block_at * QUERIES : (block_at + 1) * QUERIES]
        mixed_heads = mixed_heads + jnp.einsum(
            "hbqk,bkhd->bqhd", weight_block, value_block, preferred_element_type=jnp.float32
        )
    gate_value = jax.nn.sigmoid(projected[:, 3 * atom_width :].astype(jnp.float32)).reshape(
        windows, QUERIES, head_count, head_width
    )
    attended = (mixed_heads * gate_value).reshape(atom_rows, atom_width).astype(jnp.bfloat16)
    atom_state = atoms.astype(jnp.float32) + jnp.dot(
        attended, atom_out, preferred_element_type=jnp.float32
    )
    trans_input = (layer_norm(atom_state) * trans_gain).astype(jnp.bfloat16)
    upward = jnp.dot(trans_input, trans_up, preferred_element_type=jnp.float32)
    trans_width = trans_down.shape[0]
    activated = (jax.nn.silu(upward[:, :trans_width]) * upward[:, trans_width:]).astype(
        jnp.bfloat16
    )
    atoms_out = (
        atom_state + jnp.dot(activated, trans_down, preferred_element_type=jnp.float32)
    ).astype(jnp.bfloat16)
    return (pair_out, atoms_out)


def solution(mesh):
    return jax.shard_map(
        on_device,
        mesh=mesh,
        in_specs=(
            P("row", "col", None),
            P(("row", "col"), None),
            P(),
            P(),
            P(),
            P(),
            P(),
            P(),
            P(),
            P(),
            P(),
            P(),
            P(),
            P(),
        ),
        out_specs=(P("row", "col", None), P(("row", "col"), None)),
        check_vma=False,
    )
```

profile of v0, /device:TPU:1, one launch (start us, length us, event | category | flops | bytes accessed | tf_op | source)
XLA Modules:
  0.0 481.1 jit_solution(12595047749866982305)
XLA Ops:
  7.2 2.0 convert_reduce_fusion
  9.5 2.5 fusion.14
  12.2 2.0 fusion.32
  14.2 3.1 fusion.16
  17.4 1.9 copy-done.2
  21.3 4.9 %collective-permute-start = (bf16[48,256]{1,0:T(8,128)(2,1)}, bf16[48,256]{1,0:T(8,128)(2,1)}, u32[]{:S(2)}, u32[]{:S(2)}) collective-permute-start(bf16[48,256]{1,0:T(8,128)(2,1)} %get-tuple-element.222), channel_id=1, source_target_pairs={{0,1},{1,2},{2,3},{3,4},{4,5},{5,6},{6,7},{7,8},{8,9},{9,10},{10,1... | collective-permute-start | bytes 73736 | tf_op jit(solution)/shard_map/ppermute | solution.py:27
  26.3 1.9 collective-permute-start.1
  28.9 33.3 %while.51 = (s32[]{:T(128)}, u32[6,128]{1,0:T(8,128)S(1)}, u32[6,128]{1,0:T(8,128)S(1)}, s32[768]{0:T(1024)S(1)}, s32[6]{0:T(128)S(1)}, /*index=5*/s32[]{:T(128)}, s32[]{:T(128)}, s32[]{}) while((s32[]{:T(128)}, u32[6,128]{1,0:T(8,128)S(1)}, u32[6,128]{1,0:T(8,128)S(1)}, s32[768]{0:T(1024)S(1)}, s32[6]{0:T(128)S(1)}, ...), condition=%wide.region_10.11_spmd.clone, body=%wide.region_9.10_spmd.clone.sunk | while | flops 16388 | bytes 54917 | solution.py:123
  28.9 3.2 gather_fusion
  32.2 3.2 gather_fusion
  35.6 3.2 gather_fusion
  38.9 3.2 gather_fusion
  42.2 3.2 gather_fusion
  45.6 3.2 gather_fusion
  48.9 3.2 gather_fusion
  52.2 3.2 gather_fusion
  55.6 3.2 gather_fusion
  58.9 3.2 gather_fusion
  62.2 62.4 %all-gather.3.cloned.1.call-done = bf16[96,768,128]{2,1,0:T(8,128)(2,1)} async-done(((bf16[96,48,128]{2,1,0:T(8,128)(2,1)}), bf16[96,768,128]{2,1,0:T(8,128)(2,1)}) %all-gather.3.cloned.1.call-update) | async-done | bytes 18874384 | tf_op jit(solution)/shard_map/all_gather | solution.py:89
  124.6 7.9 %dynamic-slice_select_fusion = bf16[48,768,128]{2,1,0:T(8,128)(2,1)} fusion(bf16[96,768,128]{2,1,0:T(8,128)(2,1)} %all-gather.3.cloned.1.call-done, s32[]{:T(128)S(6)} %select_n.136, pred[]{:T(512)S(6)} %eq.158), kind=kLoop, calls=%fused_computation.20 | loop fusion | flops 4718592 | bytes 18874372 | tf_op jit(solution)/shard_map/jit(_where)/select_n | solution.py:18
  132.5 12.4 %while.52 = (s32[]{:T(128)}, u32[192]{0:T(256)S(1)}, u32[192]{0:T(256)S(1)}, s32[768]{0:T(1024)S(1)}, s32[]{:T(128)}, /*index=5*/s32[]{:T(128)}, s32[]{:T(128)}, s32[]{}) while((s32[]{:T(128)}, u32[192]{0:T(256)S(1)}, u32[192]{0:T(256)S(1)}, s32[768]{0:T(1024)S(1)}, s32[]{:T(128)}, /*index=5*/s32[]{:T(128)}, s32[]{:T(128)}, ...), condition=%wide.region_12.13_spmd.clone, body=%wide.region_11.12_spmd.clone.sunk | while | flops 3716 | bytes 13424 | solution.py:122
  145.7 4.5 fusion.10
  150.1 9.9 %gather_fusion.3 = f32[1536,4]{1,0:T(8,128)S(1)} fusion(f32[96,48,4]{2,1,0:T(8,128)S(1)} %fusion.10, s32[1536]{0:T(1024)S(1)} %reshape.309), kind=kCustom, calls=%fused_computation.3 | custom fusion | bytes 61440 | tf_op jit(solution)/shard_map/jit(take_along_axis)/gather | solution.py:82
  160.8 56.6 %psum.15 = f32[4,96,16]{2,0,1:T(4,128)S(1)} all-reduce(f32[4,96,16]{2,0,1:T(4,128)S(1)} %select_bitcast_fusion), channel_id=1, replica_groups=mesh['row'=8,'col'=16] {'col'}, use_global_device_ids=true, to_apply=%region_13.14 | all-reduce | flops 6144 | bytes 49152 | tf_op jit(solution)/shard_map/psum | solution.py:86
  224.8 9.0 %fusion.110 = (f32[4,6,32]{2,1,0:T(8,128)S(1)}, f32[4,6,32,128]{3,2,1,0:T(8,128)S(1)}) fusion(f32[4,6,32,32]{3,2,1,0:T(8,128)S(1)} %fusion.49, f32[4,6,32,32]{3,2,1,0:T(8,128)S(1)} %fusion.51, f32[4,6,32,32]{3,2,1,0:T(8,128)S(1)} %fusion.53, f32[4,6,32,32]{3,2,1,0:T(8,128)S(1)} %fusion.55, f32[4,6,32]{2,1,0:T(8,128)} %get-tuple-element.217, ...), kind=kOutput, calls=%fused_computation.183 | output fusion | flops 3833983 | bytes 1232640 | tf_op jit(solution)/shard_map/sub | solution.py:146
  237.0 33.0 %copy.145 = bf16[96,768,128]{0,1,2:T(8,128)(2,1)} copy(bf16[96,768,128]{2,1,0:T(8,128)(2,1)} %all-gather.5.cloned.1.call-done) | data formatting | bytes 37748736 | tf_op jit(solution)/shard_map/all_gather | solution.py:94
  270.0 169.9 %all-reduce.2.cloned.1.call-done = bf16[48,768,128]{2,1,0:T(8,128)(2,1)} async-done(((bf16[48,768,128]{2,1,0:T(8,128)(2,1)}), bf16[48,768,128]{2,1,0:T(8,128)(2,1)}) %all-reduce.2.cloned.1.call-update) | async-done | bytes 9437200 | tf_op jit(solution)/shard_map/psum | solution.py:19
  439.9 12.9 %copy.144 = bf16[48,768,128]{1,0,2:T(8,128)(2,1)} copy(bf16[48,768,128]{2,1,0:T(8,128)(2,1)} %all-reduce.2.cloned.1.call-done) | data formatting | bytes 18874368 | tf_op jit(solution)/shard_map/psum | solution.py:19
  452.8 13.3 %bitcast_reduce_fusion = (f32[96,48]{0,1:T(8,128)S(1)}, f32[128,48,96]{2,1,0:T(8,128)S(1)}) fusion(bf16[48,768,128]{1,0,2:T(8,128)(2,1)} %copy.144, bf16[96,768,128]{0,1,2:T(8,128)(2,1)} %copy.145), kind=kOutput, calls=%fused_computation.25 | convolution fusion | flops 906554880 | bytes 30689280 | tf_op jit(solution)/shard_map/ikc,jkc->ijc/dot_general | solution.py:92
  466.8 1.6 multiply_convert_fusion
  468.5 2.6 copy.146
  471.1 3.5 fusion.15
  (224 shorter events, 28.3 us)
Async XLA Ops:
  7.2 5.0 %copy-start = (bf16[128,640]{1,0:T(8,128)(2,1)S(1)}, bf16[128,640]{1,0:T(8,128)(2,1)}, u32[]{:S(2)}) copy-start(bf16[128,640]{1,0:T(8,128)(2,1)} %param.22) | copy-start | bytes 491524
  7.2 5.0 %copy-start.3 = (bf16[96,48,128]{2,1,0:T(8,128)(2,1)S(1)}, bf16[96,48,128]{2,1,0:T(8,128)(2,1)}, u32[]{:S(2)}) copy-start(bf16[96,48,128]{2,1,0:T(8,128)(2,1)} %param.18) | copy-start | bytes 3538948
  7.2 5.0 %copy-start.17 = (f32[128]{0:T(128)S(1)}, f32[128]{0:T(128)}, u32[]{:S(2)}) copy-start(f32[128]{0:T(128)} %param.21) | copy-start | bytes 1540
  7.2 117.4 %all-gather.3.cloned.1.call-start = ((), (), s32[]{:S(2)}) async-start(), calls=%async_computation | async-start | bytes 20054016 | tf_op jit(solution)/shard_map/all_gather | solution.py:89
  14.2 5.0 %copy-start.2 = (f32[96,48,640]{2,1,0:T(8,128)}, f32[96,48,640]{2,1,0:T(8,128)S(1)}, u32[]{:S(2)}) copy-start(f32[96,48,640]{2,1,0:T(8,128)S(1)} %fusion.32) | copy-start | bytes 35389444
  19.3 0.8 copy-start.5
  19.3 1.2 copy-start.6
  19.3 1.2 copy-start.18
  19.3 9.0 %copy-start.15 = (s32[768]{0:T(1024)S(1)}, s32[768]{0:T(1024)}, u32[]{:S(2)}) copy-start(s32[768]{0:T(1024)} %param.20) | copy-start | bytes 9220
  19.3 217.7 %all-gather.5.cloned.1.call-start = ((), (), s32[]{:S(2)}) async-start(), calls=%async_computation.2 | async-start | bytes 20054016 | tf_op jit(solution)/shard_map/all_gather | solution.py:94
  20.1 419.9 %all-reduce.2.cloned.1.call-start = ((), (), s32[]{:S(2)}) async-start(), calls=%async_computation.1 | async-start | bytes 18874368 | tf_op jit(solution)/shard_map/psum | solution.py:19
  21.3 200.3 %collective-permute-start = (bf16[48,256]{1,0:T(8,128)(2,1)}, bf16[48,256]{1,0:T(8,128)(2,1)}, u32[]{:S(2)}, u32[]{:S(2)}) collective-permute-start(bf16[48,256]{1,0:T(8,128)(2,1)} %get-tuple-element.222), channel_id=1, source_target_pairs={{0,1},{1,2},{2,3},{3,4},{4,5},{5,6},{6,7},{7,8},{8,9},{9,10},{10,1... | collective-permute-start | bytes 73736 | tf_op jit(solution)/shard_map/ppermute | solution.py:27
  26.3 195.4 %collective-permute-start.1 = (bf16[48,256]{1,0:T(8,128)(2,1)}, bf16[48,256]{1,0:T(8,128)(2,1)}, u32[]{:S(2)}, u32[]{:S(2)}) collective-permute-start(bf16[48,256]{1,0:T(8,128)(2,1)} %get-tuple-element.223), channel_id=1, source_target_pairs={{1,0},{2,1},{3,2},{4,3},{5,4},{6,5},{7,6},{8,7},{9,8},{10,9},{11,1... | collective-permute-start | bytes 73736 | tf_op jit(solution)/shard_map/ppermute | solution.py:30
  132.5 13.2 %copy-start.16 = (f32[128,4]{0,1:T(4,128)S(1)}, f32[128,4]{0,1:T(4,128)}, u32[]{:S(2)}) copy-start(f32[128,4]{0,1:T(4,128)} %param.25) | copy-start | bytes 6148
  222.8 1.9 copy-start.9
  222.8 1.9 copy-start.10
  222.9 1.9 copy-start.11
  222.9 1.9 copy-start.12
  222.9 1.9 copy-start.13
  222.9 1.9 copy-start.14
  234.4 1.1 copy-start.8
  234.4 1.5 copy-start.7
  234.4 1.5 copy-start.20
  234.6 1.5 copy-start.21
  466.2 0.7 copy-start.19
  468.4 2.6 copy-start.4
  468.5 2.6 copy-start.22
  471.0 3.5 copy-start.1
Sparse Core Ops, SparseCore 0:
  19.4 105.1 all-gather.2
  126.8 104.4 all-gather.4
  233.8 206.0 all-reduce.1
where the time goes:
time: 483 us; the launch traced here: 481 us
  waiting for transfers between devices  233 us (48%)
  local copies, waits for them, and re-layouts  111 us (23%)
  blocking collectives  56.6 us (12%)
  other arithmetic  31.8 us (7%)
  matrix products  26.6 us (6%)
  between operations  14.5 us (3%)
  starting transfers between devices  6.96 us (1%)
    psum x1, waiting for transfers between devices, broadcast(): return lax.psum(kept, axis)  170 us
    all_gather x1, waiting for transfers between devices, on_device(): whole_rows = lax.all_gather(right_edge, 'col', axis=1, tiled=True)  62.4 us
    psum x1, blocking collectives, on_device(): band_bias = lax.psum(band_part, 'col')  56.6 us
    all_gather x1, local copies, waits for them, and re-layouts, on_device(): lax.all_gather(left_edge, 'col', axis=1, tiled=True)  33 us
    gather x10, local copies, waits for them, and re-layouts, on_device(): jnp.searchsorted(token_ends, jnp.clip(key_global, 0, atom_total - 1), sid...  31.9 us
    dot_general x1, matrix products, on_device(): jnp.einsum('ikc,jkc->ijc', lax.all_gather(left_edge, 'col', axis=1, tiled...  13.3 us
    psum x1, local copies, waits for them, and re-layouts, broadcast(): return lax.psum(kept, axis)  12.9 us
    gather x10, local copies, waits for them, and re-layouts, on_device(): jnp.searchsorted(token_ends, query_global, side='right')  11.7 us
  transfers between devices with their start and end apart: 5, of which 2 were waited for; matrix products, arithmetic and copies ran while one was open for 25% of the time, Pallas kernels for 0%

commit v1 on v0

v1 whole, which is shorter than its diff:
```python
import functools

import jax
import jax.numpy as jnp
from jax import lax
from jax.experimental import pallas as pl
from jax.experimental.pallas import tpu as pltpu
from jax.sharding import PartitionSpec as P

ROWS = 96
COLS = 48
LANES = 128
CHANNELS = 128
TOKENS = 768
QUERIES = 32
KEYS = 128
HALO = 48
ATOM_ROWS = 192
KEY_ROWS = ATOM_ROWS + 2 * HALO
HEADS = 4
HEAD_DIM = 32
NEAR = 5
BAND_ROWS = 16
BAND_COLS = 32
EDGE_ROWS = 72
SUM_ROWS = 40
EPSILON = 1e-05
BOTH = ("row", "col")
VMEM_LIMIT = 56 * 1024 * 1024

F32 = jnp.float32
BF16 = jnp.bfloat16


def layer_norm(values):
    center = values - jnp.mean(values, -1, keepdims=True)
    return center * lax.rsqrt(jnp.mean(center * center, -1, keepdims=True) + EPSILON)


def sigmoid(values):
    return 0.5 * jnp.tanh(0.5 * values) + 0.5


def edges_kernel(pair_ref, gain_ref, weight_ref, edges_ref, normed_ref, stage_ref):
    gain = gain_ref[...]
    weight = weight_ref[...]

    def norm_step(step, carry):
        tile = pair_ref[pl.ds(step * 8, 8)].astype(F32).reshape(8 * COLS, CHANNELS)
        normed_ref[pl.ds(pl.multiple_of(step * 8 * COLS, 8 * COLS), 8 * COLS), :] = (
            layer_norm(tile) * gain
        )
        return carry

    lax.fori_loop(0, ROWS // 8, norm_step, 0)

    def packed(col, third, extra):
        main = normed_ref[pl.ds(col, ROWS, stride=COLS), :]
        rest = normed_ref[pl.ds(third * 32 * COLS + extra, 32, stride=COLS), :]
        return jnp.concatenate([main, rest], 0).astype(BF16)

    def emit(sources, left_at, right_at):
        for at in range(0, len(sources), 2):
            rows = jnp.concatenate([packed(*source) for source in sources[at : at + 2]], 0)
            project = lax.dot_general(
                weight, rows, (((1,), (1,)), ((), ())), preferred_element_type=F32
            )
            left = sigmoid(project[:128]) * project[128:256]
            right = sigmoid(project[256:384]) * project[384:]
            for half in range(2):
                lanes = slice(half * LANES, (half + 1) * LANES)
                stage_ref[pl.ds(left_at + at + half, CHANNELS, stride=16), :] = left[:, lanes]
                stage_ref[pl.ds(right_at + at + half, CHANNELS, stride=16), :] = right[:, lanes]

    def block(group, carry):
        sources = []
        for at in range(8):
            third = jnp.where(group < 3, group, at // 4)
            extra = jnp.where(group < 3, 36 + at, 44 + at % 4)
            sources.append((group * 8 + at, third, extra))
        emit(sources, 0, 8)
        edges_ref[:, pl.ds(pl.multiple_of(group * 16, 16), 16), :] = (
            stage_ref[...].reshape(CHANNELS, 16, LANES).astype(BF16)
        )
        return carry

    lax.fori_loop(0, 4, block, 0)
    emit([(32 + at, 2, 44 + at) for at in range(4)], 0, 4)
    edges_ref[:, 64:72, :] = stage_ref[...].reshape(CHANNELS, 16, LANES)[:, :8].astype(BF16)


def edges(pair, pair_gain, weight):
    return pl.pallas_call(
        edges_kernel,
        out_shape=jax.ShapeDtypeStruct((CHANNELS, EDGE_ROWS, LANES), BF16),
        scratch_shapes=[
            pltpu.VMEM((ROWS * COLS, CHANNELS), F32),
            pltpu.VMEM((CHANNELS * 16, LANES), F32),
        ],
        compiler_params=pltpu.CompilerParams(vmem_limit_bytes=VMEM_LIMIT),
        cost_estimate=pl.CostEstimate(
            flops=2 * ROWS * COLS * 128 * 512, bytes_accessed=4000000, transcendentals=1200000
        ),
        name="edges",
    )(pair, pair_gain, weight)


def triangle_kernel(chunks_ref, sums_ref, left_ref, right_ref, flip_ref, out_ref):
    lane = lax.broadcasted_iota(jnp.int32, (8, LANES), 1)
    low = lax.broadcasted_iota(jnp.int32, (8, LANES), 0) < 4

    def thirds(first, second, third):
        return jnp.where(
            lane < 32,
            pltpu.roll(first, 32, 1),
            jnp.where(lane < 64, pltpu.roll(second, 64, 1), pltpu.roll(third, 96, 1)),
        )

    for row in range(8):

        def gather(col, carry):
            chunk = chunks_ref[row * 16 + col].astype(F32)
            part = [chunk[at * 8 : at * 8 + 8] for at in range(9)]
            tail = part[8]
            turned = pltpu.roll(tail, 4, 0)
            at_rows = pl.ds(pl.multiple_of(col * COLS, COLS), COLS)
            left, right = part[0:8:2], part[1:8:2]
            for ref, main, last, spare in (
                (left_ref, left, tail, turned),
                (right_ref, right, turned, tail),
            ):
                fine = thirds(pltpu.roll(main[3], 4, 0), main[3], spare)
                whole = jnp.concatenate(
                    main + [thirds(main[0], main[1], main[2]), jnp.where(low, last, fine)], 0
                )
                ref[at_rows, row * LANES : (row + 1) * LANES] = whole.astype(BF16)
            return carry

        lax.fori_loop(0, 16, gather, 0)
        flip_ref[row * LANES : (row + 1) * LANES, :] = right_ref[
            :, row * LANES : (row + 1) * LANES
        ].T

    for pair_at in range(4):
        out_ref[...] = jnp.dot(
            flip_ref[...],
            left_ref[:, pair_at * 256 : (pair_at + 1) * 256],
            preferred_element_type=F32,
        )
        for half in range(2):
            row = pair_at * 2 + half

            def pack(col_pair, carry):
                for side in range(2):
                    start = pl.multiple_of(col_pair * LANES + side * COLS, 16)
                    block = out_ref[pl.ds(start, COLS), half * LANES : (half + 1) * LANES]
                    rest = block[40:48]
                    head = [
                        jnp.where(
                            lane < 96, block[at * 8 : at * 8 + 8], pltpu.roll(rest, 96 - 32 * at, 1)
                        )
                        for at in range(3)
                    ]
                    whole = jnp.concatenate(head + [block[24:40]], 0)
                    sums_ref[row * 16 + col_pair * 2 + side] = whole.astype(BF16)
                return carry

            lax.fori_loop(0, 8, pack, 0)


def triangle(chunks):
    return pl.pallas_call(
        triangle_kernel,
        out_shape=jax.ShapeDtypeStruct((CHANNELS, SUM_ROWS, LANES), BF16),
        scratch_shapes=[
            pltpu.VMEM((TOKENS, 1024), BF16),
            pltpu.VMEM((TOKENS, 1024), BF16),
            pltpu.VMEM((1024, TOKENS), BF16),
            pltpu.VMEM((1024, 256), F32),
        ],
        compiler_params=pltpu.CompilerParams(vmem_limit_bytes=VMEM_LIMIT),
        cost_estimate=pl.CostEstimate(
            flops=2 * 1024 * 1024 * 768, bytes_accessed=4000000, transcendentals=0
        ),
        name="triangle",
    )(chunks)


def update_kernel(sums_ref, pair_ref, gate_ref, gain_ref, weight_ref, out_ref, normed_ref, update_ref):
    gain = gain_ref[...]
    weight = weight_ref[...]

    def norm_step(step, carry):
        rows = pl.ds(pl.multiple_of(step * 8, 8), 8)
        tile = sums_ref[:, rows, :].astype(F32)
        center = tile - jnp.mean(tile, 0, keepdims=True)
        scale = lax.rsqrt(jnp.mean(center * center, 0, keepdims=True) + EPSILON)
        normed_ref[...] = (center * scale).reshape(CHANNELS * 8, LANES)
        for at in range(8):
            block = (normed_ref[pl.ds(at, CHANNELS, stride=8), :] * gain).astype(BF16)
            update = lax.dot_general(
                block, weight, (((0,), (0,)), ((), ())), preferred_element_type=F32
            )
            update_ref[pl.ds(step * 8 + at, ROWS, stride=COLS), :] = update[:ROWS]

            @pl.when(step < 3)
            def _():
                start = step * 32 * COLS + 40 + at
                update_ref[pl.ds(start, 32, stride=COLS), :] = update[ROWS:]

        return carry

    lax.fori_loop(0, SUM_ROWS // 8, norm_step, 0)

    def out_step(step, carry):
        rows = pl.ds(step * 8, 8)
        update = update_ref[pl.ds(pl.multiple_of(step * 8 * COLS, 8 * COLS), 8 * COLS), :]
        update = update.reshape(8, COLS, CHANNELS)
        out_ref[rows] = (pair_ref[rows].astype(F32) + gate_ref[rows] * update).astype(BF16)
        return carry

    lax.fori_loop(0, ROWS // 8, out_step, 0)


def update_pair(sums, pair, gate, out_gain, tri_out):
    return pl.pallas_call(
        update_kernel,
        out_shape=jax.ShapeDtypeStruct((ROWS, COLS, CHANNELS), BF16),
        scratch_shapes=[
            pltpu.VMEM((CHANNELS * 8, LANES), F32),
            pltpu.VMEM((ROWS * COLS, CHANNELS), F32),
        ],
        compiler_params=pltpu.CompilerParams(vmem_limit_bytes=VMEM_LIMIT),
        cost_estimate=pl.CostEstimate(
            flops=2 * ROWS * COLS * 128 * 128, bytes_accessed=6000000, transcendentals=5000
        ),
        name="update_pair",
    )(sums, pair, gate, out_gain, tri_out)


def split3(values):
    high = values.astype(BF16)
    rest = values - high.astype(F32)
    middle = rest.astype(BF16)
    low = (rest - middle.astype(F32)).astype(BF16)
    return high, middle, low


def side_kernel(
    first_ref, place_ref, pair_ref, gain_ref, weight_ref, bias_ref, gate_ref, band_ref, table_ref
):
    gain = gain_ref[...]
    weight = weight_ref[...]
    bias = jnp.concatenate([part.astype(F32) for part in split3(bias_ref[...])], 0).astype(BF16)
    table_ref[...] = jnp.zeros_like(table_ref)

    def norm_step(step, carry):
        tile = pair_ref[pl.ds(step * 8, 8)].astype(F32).reshape(8 * COLS, CHANNELS)
        normed = layer_norm(tile)
        inputs = (normed * gain).astype(BF16)
        gate = sigmoid(jnp.dot(inputs, weight, preferred_element_type=F32))
        gate_ref[pl.ds(step * 8, 8)] = gate.reshape(8, COLS, CHANNELS)
        parts = split3(normed)
        for at in range(8):
            rows = slice(at * COLS, (at + 1) * COLS)
            found = sum(
                lax.dot_general(
                    bias, part[rows], (((1,), (1,)), ((), ())), preferred_element_type=F32
                )
                for part in parts
            )
            found = found[0:8] + found[8:16] + found[16:24]
            for head in range(HEADS):
                table_ref[head, pl.ds(8 + step * 8 + at, 1), 0:COLS] = found[head : head + 1]
        return carry

    lax.fori_loop(0, ROWS // 8, norm_step, 0)

    lane = lax.broadcasted_iota(jnp.int32, (BAND_ROWS, LANES), 1)
    row_base = place_ref[0]
    col_base = place_ref[1]

    def band_step(target, carry):
        first = first_ref[target]
        start = first - row_base + 8
        total = jnp.zeros((BAND_ROWS, LANES), F32)
        shift = col_base - (first - NEAR)
        for head in range(HEADS):
            rows = table_ref[head, pl.ds(start, BAND_ROWS), :]
            moved = pltpu.roll(rows, lax.rem(shift + head * BAND_COLS + 16 * LANES, LANES), 1)
            col = lane - head * BAND_COLS - shift
            keep = (lane // BAND_COLS == head) & (col >= 0) & (col < COLS)
            total = total + jnp.where(keep, moved, 0.0)
        band_ref[target] = total
        return carry

    lax.fori_loop(0, 16, band_step, 0)


def side(first, place, pair, pair_gain, gate_weight, bias_wide):
    whole = pl.BlockSpec(memory_space=pltpu.VMEM)
    scalars = pl.BlockSpec(memory_space=pltpu.SMEM)
    return pl.pallas_call(
        side_kernel,
        out_shape=(
            jax.ShapeDtypeStruct((ROWS, COLS, CHANNELS), F32),
            jax.ShapeDtypeStruct((16, BAND_ROWS, LANES), F32),
        ),
        in_specs=[scalars, scalars, whole, whole, whole, whole],
        out_specs=(whole, whole),
        scratch_shapes=[pltpu.VMEM((HEADS, ROWS + 32, LANES), F32)],
        compiler_params=pltpu.CompilerParams(vmem_limit_bytes=VMEM_LIMIT),
        cost_estimate=pl.CostEstimate(
            flops=8 * ROWS * COLS * 128 * 128, bytes_accessed=5000000, transcendentals=600000
        ),
        name="side",
    )(first, place, pair, pair_gain, gate_weight, bias_wide)


def atoms_kernel(
    base_ref,
    atoms_ref,
    before_ref,
    after_ref,
    band_ref,
    lane_start_ref,
    lane_end_ref,
    sub_start_ref,
    sub_end_ref,
    gain_ref,
    project_ref,
    output_ref,
    trans_gain_ref,
    up_ref,
    down_ref,
    out_ref,
):
    base = base_ref[0]
    own = atoms_ref[...].astype(F32)
    around = jnp.concatenate(
        [before_ref[...].astype(F32), own, after_ref[...].astype(F32)], 0
    )
    inputs = (layer_norm(around) * gain_ref[...]).astype(BF16)
    projected = jnp.dot(inputs, project_ref[...], preferred_element_type=F32)
    query = projected[HALO : HALO + ATOM_ROWS, 0:128].astype(BF16)
    key = projected[:, 128:256].astype(BF16)
    value = projected[:, 256:384].astype(BF16)
    gate = projected[HALO : HALO + ATOM_ROWS, 384:512].astype(BF16).astype(F32)

    query_atom = base + lax.broadcasted_iota(jnp.int32, (ATOM_ROWS, LANES), 0)
    query_hot = (
        ((query_atom >= lane_start_ref[...]) & (query_atom < lane_end_ref[...]))
        .astype(F32)
        .astype(BF16)
    )
    key_atom = base - HALO + lax.broadcasted_iota(jnp.int32, (LANES, KEY_ROWS), 1)
    key_hot = (
        ((key_atom >= sub_start_ref[...]) & (key_atom < sub_end_ref[...])).astype(F32)
    )
    token_head = lax.broadcasted_iota(jnp.int32, (LANES, KEY_ROWS), 0) // BAND_COLS

    band = jnp.sum(band_ref[...], 0)
    band = jnp.concatenate([band, jnp.zeros((LANES - BAND_ROWS, LANES), F32)], 0)
    picked = [
        jnp.dot(query_hot, part, preferred_element_type=F32).astype(BF16) for part in split3(band)
    ]

    window = lax.broadcasted_iota(jnp.int32, (ATOM_ROWS, KEY_ROWS), 0) // QUERIES
    place = lax.broadcasted_iota(jnp.int32, (ATOM_ROWS, KEY_ROWS), 1)
    near = place - window * QUERIES
    atom = base - HALO + place
    allowed = (near >= 0) & (near < KEYS) & (atom >= 0) & (atom < TOKENS * 32)
    lane_head = lax.broadcasted_iota(jnp.int32, (ATOM_ROWS, LANES), 1) // HEAD_DIM
    mixed = jnp.zeros((ATOM_ROWS, LANES), F32)
    for head in range(HEADS):
        own_query = jnp.where(lane_head == head, query.astype(F32), 0.0).astype(BF16)
        scores = lax.dot_general(
            own_query, key, (((1,), (1,)), ((), ())), preferred_element_type=F32
        ) * (HEAD_DIM**-0.5)
        head_hot = jnp.where(token_head == head, key_hot, 0.0).astype(BF16)
        for part in picked:
            scores = scores + jnp.dot(part, head_hot, preferred_element_type=F32)
        scores = jnp.where(allowed, scores, -jnp.inf)
        grown = jnp.exp(scores - jnp.max(scores, -1, keepdims=True))
        weights = (grown / jnp.sum(grown, -1, keepdims=True)).astype(BF16)
        mixed = mixed + jnp.where(
            lane_head == head, jnp.dot(weights, value, preferred_element_type=F32), 0.0
        )
    attended = (mixed * sigmoid(gate)).astype(BF16)
    state = own + jnp.dot(attended, output_ref[...], preferred_element_type=F32)
    inner = (layer_norm(state) * trans_gain_ref[...]).astype(BF16)
    upward = jnp.dot(inner, up_ref[...], preferred_element_type=F32)
    first, second = upward[:, :256], upward[:, 256:]
    hidden = (first * sigmoid(first) * second).astype(BF16)
    out_ref[...] = (
        state + jnp.dot(hidden, down_ref[...], preferred_element_type=F32)
    ).astype(BF16)


def atoms_block(base, *arrays):
    whole = pl.BlockSpec(memory_space=pltpu.VMEM)
    return pl.pallas_call(
        atoms_kernel,
        out_shape=jax.ShapeDtypeStruct((ATOM_ROWS, LANES), BF16),
        in_specs=[pl.BlockSpec(memory_space=pltpu.SMEM)] + [whole] * len(arrays),
        out_specs=whole,
        compiler_params=pltpu.CompilerParams(vmem_limit_bytes=VMEM_LIMIT),
        cost_estimate=pl.CostEstimate(
            flops=2 * 400 * 1000 * 1000, bytes_accessed=2000000, transcendentals=400000
        ),
        name="atoms_block",
    )(base, *arrays)


def on_device(
    pair,
    atoms,
    token_atoms,
    pair_gain,
    tri_proj,
    tri_out,
    out_gain,
    bias_weight,
    atom_gain,
    atom_proj,
    atom_out,
    trans_gain,
    trans_up,
    trans_down,
):
    row_id = lax.axis_index("row")
    col_id = lax.axis_index("col")
    device = row_id * 16 + col_id

    weight = tri_proj[:, :512].T
    chunks = edges(pair, pair_gain[None], weight)
    arrived = lax.all_to_all(chunks, BOTH, 0, 0, tiled=True)

    ends = jnp.cumsum(token_atoms)
    starts = ends - token_atoms
    firsts_at = (row_id * 16 + jnp.arange(16, dtype=jnp.int32)) * ATOM_ROWS
    firsts = jnp.sum((ends[None, :] <= firsts_at[:, None]).astype(jnp.int32), 1)
    first = jnp.sum((ends <= device * ATOM_ROWS).astype(jnp.int32))
    far = jnp.full((LANES,), -1, jnp.int32)
    all_starts = jnp.concatenate([far, starts, far])
    all_ends = jnp.concatenate([far, ends, far])
    lane_start = lax.dynamic_slice(all_starts, (first + LANES,), (LANES,))
    lane_end = lax.dynamic_slice(all_ends, (first + LANES,), (LANES,))
    sub_start = lax.dynamic_slice(all_starts, (first + LANES - NEAR,), (BAND_COLS,))
    sub_end = lax.dynamic_slice(all_ends, (first + LANES - NEAR,), (BAND_COLS,))

    bias_wide = jnp.pad(bias_weight.T, ((0, 4), (0, 0)))
    place = jnp.stack([row_id * ROWS, col_id * COLS]).astype(jnp.int32)
    gate, bands = side(firsts, place, pair, pair_gain[None], tri_proj[:, 512:], bias_wide)
    band = lax.all_to_all(bands, "col", 0, 0, tiled=True)

    ring = list(range(127))
    before = lax.ppermute(atoms[ATOM_ROWS - HALO :], BOTH, [(at, at + 1) for at in ring])
    after = lax.ppermute(atoms[:HALO], BOTH, [(at + 1, at) for at in ring])
    atoms_out = atoms_block(
        (device * ATOM_ROWS).astype(jnp.int32)[None],
        atoms,
        before,
        after,
        band,
        lane_start[None],
        lane_end[None],
        jnp.tile(sub_start, HEADS)[:, None],
        jnp.tile(sub_end, HEADS)[:, None],
        atom_gain[None],
        atom_proj,
        atom_out,
        trans_gain[None],
        trans_up,
        trans_down,
    )

    sums = triangle(arrived)
    returned = lax.all_to_all(sums, BOTH, 0, 0, tiled=True)
    pair_out = update_pair(returned, pair, gate, out_gain[:, None], tri_out)
    return (pair_out, atoms_out)


def solution(mesh):
    return jax.shard_map(
        on_device,
        mesh=mesh,
        in_specs=(P("row", "col", None), P(BOTH, None)) + (P(),) * 12,
        out_specs=(P("row", "col", None), P(BOTH, None)),
        check_vma=False,
    )
```

time: 483 us -> 129 us (0.27)
  waiting for transfers between devices: 233 us -> 24.2 us
  local copies, waits for them, and re-layouts: 111 us -> 9.19 us
  Pallas kernels: 0 us -> 59.7 us
  blocking collectives: 56.6 us -> 0 us
  other arithmetic: 31.8 us -> 2.43 us
  matrix products: 26.6 us -> 0 us
  starting transfers between devices: 6.96 us -> 27.4 us
  between operations: 14.5 us -> 3.35 us
    psum x1 -> x0, waiting for transfers between devices: 170 us -> none  [broadcast(): return lax.psum(kept, axis)]
    all_gather x2 -> x0, waiting for transfers between devices: 62.4 us -> none  [the longest x1 62.4 us: on_device(): whole_rows = lax.all_gather(right_edge, 'col', axis=1, tiled=True)]
    pallas_call x0 -> x5, Pallas kernels: none -> 59.7 us  [the longest x1 22.1 us: triangle(): pl.pallas_call(triangle_kernel, out_shape=jax.ShapeDtypeStruct((CHANNELS,...]
    psum x1 -> x0, blocking collectives: 56.6 us -> none  [on_device(): band_bias = lax.psum(band_part, 'col')]
    gather x25 -> x0, local copies, waits for them, and re-layouts: 55.4 us -> none  [the longest x10 31.9 us: on_device(): jnp.searchsorted(token_ends, jnp.clip(key_global, 0, atom_total - 1), sid...]
    all_gather x1 -> x0, local copies, waits for them, and re-layouts: 33 us -> none  [on_device(): lax.all_gather(left_edge, 'col', axis=1, tiled=True)]
    dot_general x16 -> x0, matrix products: 26.6 us -> none  [the longest x1 13.3 us: on_device(): jnp.einsum('ikc,jkc->ijc', lax.all_gather(left_edge, 'col', axis=1, tiled...]
    all_to_all x0 -> x3, waiting for transfers between devices: none -> 24.2 us  [the longest x1 19.4 us: on_device(): arrived = lax.all_to_all(chunks, BOTH, 0, 0, tiled=True)]
  transfers between devices with their start and end apart: 5 -> 5, of which waited for: 2 -> 2; matrix products, arithmetic and copies ran while one was open for 25% -> 6% of each run, Pallas kernels for 0% -> 30%
where the time goes in v1:
time: 129 us; the launch traced here: 126 us
  Pallas kernels  59.7 us (46%)
  starting transfers between devices  27.4 us (21%)
  waiting for transfers between devices  24.2 us (19%)
  local copies, waits for them, and re-layouts  9.19 us (7%)
  between operations  3.35 us (3%)
  other arithmetic  2.43 us (2%)
    pallas_call x1, Pallas kernels, triangle(): pl.pallas_call(triangle_kernel, out_shape=jax.ShapeDtypeStruct((CHANNELS,...  22.1 us
    all_to_all x1, waiting for transfers between devices, on_device(): arrived = lax.all_to_all(chunks, BOTH, 0, 0, tiled=True)  19.4 us
    pallas_call x1, Pallas kernels, update_pair(): pl.pallas_call(update_kernel, out_shape=jax.ShapeDtypeStruct((ROWS, COLS,...  13.6 us
    all_to_all x1, starting transfers between devices, on_device(): arrived = lax.all_to_all(chunks, BOTH, 0, 0, tiled=True)  11.5 us
    pallas_call x1, Pallas kernels, side(): pl.pallas_call(side_kernel, out_shape=(jax.ShapeDtypeStruct((ROWS, COLS,...  10.2 us
    pallas_call x1, Pallas kernels, edges(): pl.pallas_call(edges_kernel, out_shape=jax.ShapeDtypeStruct((CHANNELS, ED...  8.9 us
    all_to_all x1, starting transfers between devices, on_device(): returned = lax.all_to_all(sums, BOTH, 0, 0, tiled=True)  6.41 us
    pallas_call x1, Pallas kernels, atoms_block(): pl.pallas_call(atoms_kernel, out_shape=jax.ShapeDtypeStruct((ATOM_ROWS, L...  5.01 us
  transfers between devices with their start and end apart: 5, of which 2 were waited for; matrix products, arithmetic and copies ran while one was open for 6% of the time, Pallas kernels for 30%

profile of v1, /device:TPU:1, one launch (start us, length us, event | category | flops | bytes accessed | tf_op | source)
XLA Modules:
  0.0 126.3 jit_solution(15271088665880933079)
XLA Ops:
  0.6 0.9 slice.19
  1.5 0.8 copy.28
  2.3 8.9 %edges.1 = bf16[128,72,128]{2,1,0:T(8,128)(2,1)} custom-call(bf16[96,48,128]{2,1,0:T(8,128)(2,1)} %pair_ref.5, f32[1,128]{1,0:T(1,128)} %bitcast.21, bf16[512,128]{1,0:T(8,128)(2,1)} %bitcast.17), custom_call_target="tpu_custom_call" | custom-call | flops 603979776 | bytes 4000000 | tf_op jit(solution)/shard_map/edges/pallas_call | solution.py:93
  11.2 11.5 %all-to-all-start = ((bf16[128,72,128]{2,1,0:T(8,128)(2,1)}), bf16[128,72,128]{2,1,0:T(8,128)(2,1)S(1)}, u32[]{:S(2)}, u32[]{:S(2)}) async-start(bf16[128,72,128]{2,1,0:T(8,128)(2,1)} %edges.1), calls=%async_computation | async-start | bytes 4718592 | tf_op jit(solution)/shard_map/all_to_all | solution.py:437
  22.7 1.4 %slice.22.weight_ref = bf16[128,128]{1,0:T(8,128)(2,1)} slice(bf16[128,640]{1,0:T(8,128)(2,1)} %param.18), slice={[0:128], [512:640]} | slice | bytes 65536 | tf_op jit(solution)/shard_map/slice | solution.py:454
  24.1 0.3 reduce-window.9
  24.4 0.1 slice.20
  24.5 0.6 pad.4.bias_ref
  25.1 0.7 pad_add_fusion.4.place_ref
  25.7 0.1 slice_reduce_fusion
  25.9 0.1 fusion
  25.9 0.7 convert_reduce_fusion.first_ref
  26.6 10.2 %side.1 = (f32[96,48,128]{2,1,0:T(8,128)}, f32[16,16,128]{2,1,0:T(8,128)}) custom-call(s32[16]{0:T(128)} %convert_reduce_fusion.first_ref, s32[2]{0:T(128)} %pad_add_fusion.4.place_ref, bf16[96,48,128]{2,1,0:T(8,128)(2,1)} %pair_ref.5, f32[1,128]{1,0:T(1,128)} %bitcast.22, bf16[128,128]{1,0:T(8,128)(2,1)} %slice.22.weight_ref, f32[8,128]{1,0:T(8,128)} %pad.4.bias_ref), custom_call_target="tpu_custom_call" | custom-call | flops 603979776 | bytes 5000000 | tf_op jit(solution)/shard_map/side/pallas_call | solution.py:303
  36.8 19.4 %all-to-all-done.chunks_ref = bf16[128,72,128]{2,1,0:T(8,128)(2,1)S(1)} async-done(((bf16[128,72,128]{2,1,0:T(8,128)(2,1)}), bf16[128,72,128]{2,1,0:T(8,128)(2,1)S(1)}, u32[]{:S(2)}, u32[]{:S(2)}) %all-to-all-start) | async-done | bytes 2359328 | tf_op jit(solution)/shard_map/all_to_all | solution.py:437
  56.2 3.9 %all-to-all-start.2 = ((f32[16,16,128]{2,1,0:T(8,128)}), f32[16,16,128]{2,1,0:T(8,128)S(1)}, u32[]{:S(2)}, u32[]{:S(2)}) async-start(f32[16,16,128]{2,1,0:T(8,128)} %get-tuple-element.5), calls=%async_computation.2 | async-start | bytes 262144 | tf_op jit(solution)/shard_map/all_to_all | solution.py:455
  60.1 22.1 %triangle.1 = bf16[128,40,128]{2,1,0:T(8,128)(2,1)} custom-call(bf16[128,72,128]{2,1,0:T(8,128)(2,1)} %copy-done.1), custom_call_target="tpu_custom_call" | custom-call | flops 1610612736 | bytes 4000000 | tf_op jit(solution)/shard_map/triangle/pallas_call | solution.py:172
  82.2 0.6 copy-done.2
  82.8 6.4 %all-to-all-start.1 = ((bf16[128,40,128]{2,1,0:T(8,128)(2,1)}), bf16[128,40,128]{2,1,0:T(8,128)(2,1)S(1)}, u32[]{:S(2)}, u32[]{:S(2)}) async-start(bf16[128,40,128]{2,1,0:T(8,128)(2,1)} %triangle.1), calls=%async_computation.1 | async-start | bytes 2621440 | tf_op jit(solution)/shard_map/all_to_all | solution.py:479
  89.3 3.7 %collective-permute-start = (bf16[48,128]{1,0:T(8,128)(2,1)S(1)}, bf16[48,128]{1,0:T(8,128)(2,1)S(1)}, u32[]{:S(2)}, u32[]{:S(2)}) collective-permute-start(bf16[48,128]{1,0:T(8,128)(2,1)S(1)} %get-tuple-element.9), channel_id=1, source_target_pairs={{0,1},{1,2},{2,3},{3,4},{4,5},{5,6},{6,7},{7,8},{8,9},{9,10},{10,1... | collective-permute-start | bytes 36872 | tf_op jit(solution)/shard_map/ppermute | solution.py:458
  93.0 1.9 %collective-permute-start.1 = (bf16[48,128]{1,0:T(8,128)(2,1)S(1)}, bf16[48,128]{1,0:T(8,128)(2,1)S(1)}, u32[]{:S(2)}, u32[]{:S(2)}) collective-permute-start(bf16[48,128]{1,0:T(8,128)(2,1)S(1)} %get-tuple-element.8), channel_id=1, source_target_pairs={{1,0},{2,1},{3,2},{4,3},{5,4},{6,5},{7,6},{8,7},{9,8},{10,9},{11,1... | collective-permute-start | bytes 36872 | tf_op jit(solution)/shard_map/ppermute | solution.py:459
  94.9 0.7 convert_reduce_fusion.1
  96.9 0.7 dynamic-slice_bitcast_fusion
  98.9 0.1 dynamic_slice.14
  99.0 0.1 dynamic_slice.15
  99.0 0.7 copy.25.gain_ref
  99.8 0.7 broadcast_in_dim_tile.8.sub_start_ref
  100.5 0.7 broadcast_in_dim_tile.9.sub_end_ref
  101.3 0.6 copy-done.7
  101.8 5.0 %atoms_block.1 = bf16[192,128]{1,0:T(8,128)(2,1)} custom-call(s32[1]{0:T(128)} %bitcast.8.base_ref, bf16[192,128]{1,0:T(8,128)(2,1)} %atoms_ref.1, bf16[48,128]{1,0:T(8,128)(2,1)} %copy-done.7, bf16[48,128]{1,0:T(8,128)(2,1)} %copy-done.8, f32[16,16,128]{2,1,0:T(8,128)} %copy-done.2, s32[1,128]{1,0:T(1,128)} %get-tuple-element.13.lane_start_ref, ...), custom_call_target="tpu_custom_call" | custom-call | flops 800000000 | bytes 2000000 | tf_op jit(solution)/shard_map/atoms_block/pallas_call | solution.py:402
  106.9 4.8 %all-to-all-done.1.sums_ref = bf16[128,40,128]{2,1,0:T(8,128)(2,1)S(1)} async-done(((bf16[128,40,128]{2,1,0:T(8,128)(2,1)}), bf16[128,40,128]{2,1,0:T(8,128)(2,1)S(1)}, u32[]{:S(2)}, u32[]{:S(2)}) %all-to-all-start.1) | async-done | bytes 1310752 | tf_op jit(solution)/shard_map/all_to_all | solution.py:479
  111.6 1.1 copy-done
  112.7 13.6 %update_pair.1 = bf16[96,48,128]{2,1,0:T(8,128)(2,1)} custom-call(bf16[128,40,128]{2,1,0:T(8,128)(2,1)} %copy-done, bf16[96,48,128]{2,1,0:T(8,128)(2,1)} %pair_ref.5, f32[96,48,128]{2,1,0:T(8,128)} %get-tuple-element.4.gate_ref, f32[128,1]{1,0:T(8,128)} %copy.25.gain_ref, bf16[128,128]{1,0:T(8,128)(2,1)} %weight_ref.1), custom_call_target="tpu_custom_call" | custom-call | flops 150994944 | bytes 6000000 | tf_op jit(solution)/shard_map/update_pair/pallas_call | solution.py:226
  (25 shorter events, 0.1 us)
Async XLA Ops:
  11.2 12.9 %copy-start.3 = (s32[768]{0:T(1024)S(1)}, s32[768]{0:T(1024)}, u32[]{:S(2)}) copy-start(s32[768]{0:T(1024)} %param.16) | copy-start | bytes 9220
  11.2 13.3 %copy-start.5 = (f32[128,4]{0,1:T(4,128)S(1)}, f32[128,4]{0,1:T(4,128)}, u32[]{:S(2)}) copy-start(f32[128,4]{0,1:T(4,128)} %param.21) | copy-start | bytes 6148
  11.2 45.0 %all-to-all-start = ((bf16[128,72,128]{2,1,0:T(8,128)(2,1)}), bf16[128,72,128]{2,1,0:T(8,128)(2,1)S(1)}, u32[]{:S(2)}, u32[]{:S(2)}) async-start(bf16[128,72,128]{2,1,0:T(8,128)(2,1)} %edges.1), calls=%async_computation | async-start | bytes 4718592 | tf_op jit(solution)/shard_map/all_to_all | solution.py:437
  56.2 3.9 %copy-start.1 = (bf16[128,72,128]{2,1,0:T(8,128)(2,1)}, bf16[128,72,128]{2,1,0:T(8,128)(2,1)S(1)}, u32[]{:S(2)}) copy-start(bf16[128,72,128]{2,1,0:T(8,128)(2,1)S(1)} %all-to-all-done.chunks_ref) | copy-start | bytes 7077892
  56.2 26.0 %all-to-all-start.2 = ((f32[16,16,128]{2,1,0:T(8,128)}), f32[16,16,128]{2,1,0:T(8,128)S(1)}, u32[]{:S(2)}, u32[]{:S(2)}) async-start(f32[16,16,128]{2,1,0:T(8,128)} %get-tuple-element.5), calls=%async_computation.2 | async-start | bytes 262144 | tf_op jit(solution)/shard_map/all_to_all | solution.py:455
  82.2 7.1 %copy-start.4 = (bf16[192,128]{1,0:T(8,128)(2,1)S(1)}, bf16[192,128]{1,0:T(8,128)(2,1)}, u32[]{:S(2)}) copy-start(bf16[192,128]{1,0:T(8,128)(2,1)} %atoms_ref.1) | copy-start | bytes 147460
  82.2 16.8 %copy-start.6 = (f32[128]{0:T(128)S(1)}, f32[128]{0:T(128)}, u32[]{:S(2)}) copy-start(f32[128]{0:T(128)} %param.20) | copy-start | bytes 1540
  82.2 0.7 copy-start.2
  82.8 28.8 %all-to-all-start.1 = ((bf16[128,40,128]{2,1,0:T(8,128)(2,1)}), bf16[128,40,128]{2,1,0:T(8,128)(2,1)S(1)}, u32[]{:S(2)}, u32[]{:S(2)}) async-start(bf16[128,40,128]{2,1,0:T(8,128)(2,1)} %triangle.1), calls=%async_computation.1 | async-start | bytes 2621440 | tf_op jit(solution)/shard_map/all_to_all | solution.py:479
  89.3 11.9 %collective-permute-start = (bf16[48,128]{1,0:T(8,128)(2,1)S(1)}, bf16[48,128]{1,0:T(8,128)(2,1)S(1)}, u32[]{:S(2)}, u32[]{:S(2)}) collective-permute-start(bf16[48,128]{1,0:T(8,128)(2,1)S(1)} %get-tuple-element.9), channel_id=1, source_target_pairs={{0,1},{1,2},{2,3},{3,4},{4,5},{5,6},{6,7},{7,8},{8,9},{9,10},{10,1... | collective-permute-start | bytes 36872 | tf_op jit(solution)/shard_map/ppermute | solution.py:458
  93.0 8.3 %collective-permute-start.1 = (bf16[48,128]{1,0:T(8,128)(2,1)S(1)}, bf16[48,128]{1,0:T(8,128)(2,1)S(1)}, u32[]{:S(2)}, u32[]{:S(2)}) collective-permute-start(bf16[48,128]{1,0:T(8,128)(2,1)S(1)} %get-tuple-element.8), channel_id=1, source_target_pairs={{1,0},{2,1},{3,2},{4,3},{5,4},{6,5},{7,6},{8,7},{9,8},{10,9},{11,1... | collective-permute-start | bytes 36872 | tf_op jit(solution)/shard_map/ppermute | solution.py:459
  101.2 0.6 copy-start.7
  101.2 0.6 copy-start.8
  111.6 1.1 copy-start

commit v2 on v1

--- a/solution.py
+++ b/solution.py
@@ -26,7 +26,7 @@
 SUM_ROWS = 40
 EPSILON = 1e-05
 BOTH = ("row", "col")
-VMEM_LIMIT = 56 * 1024 * 1024
+VMEM_LIMIT = 20 * 1024 * 1024
 
 F32 = jnp.float32
 BF16 = jnp.bfloat16
@@ -41,9 +41,10 @@
     return 0.5 * jnp.tanh(0.5 * values) + 0.5
 
 
-def edges_kernel(pair_ref, gain_ref, weight_ref, edges_ref, normed_ref, stage_ref):
+def edges_kernel(pair_ref, gain_ref, weight_ref, edges_ref, gain_out_ref, normed_ref, stage_ref):
     gain = gain_ref[...]
-    weight = weight_ref[...]
+    gain_out_ref[...] = gain
+    weight = weight_ref[:, :512].T
 
     def norm_step(step, carry):
         tile = pair_ref[pl.ds(step * 8, 8)].astype(F32).reshape(8 * COLS, CHANNELS)
@@ -52,7 +53,7 @@
         )
         return carry
 
-    lax.fori_loop(0, ROWS // 8, norm_step, 0)
+    lax.fori_loop(0, ROWS // 8, norm_step, 0, unroll=4)
 
     def packed(col, third, extra):
         main = normed_ref[pl.ds(col, ROWS, stride=COLS), :]
@@ -84,7 +85,7 @@
         )
         return carry
 
-    lax.fori_loop(0, 4, block, 0)
+    lax.fori_loop(0, 4, block, 0, unroll=True)
     emit([(32 + at, 2, 44 + at) for at in range(4)], 0, 4)
     edges_ref[:, 64:72, :] = stage_ref[...].reshape(CHANNELS, 16, LANES)[:, :8].astype(BF16)
 
@@ -92,7 +93,10 @@
 def edges(pair, pair_gain, weight):
     return pl.pallas_call(
         edges_kernel,
-        out_shape=jax.ShapeDtypeStruct((CHANNELS, EDGE_ROWS, LANES), BF16),
+        out_shape=(
+            jax.ShapeDtypeStruct((CHANNELS, EDGE_ROWS, LANES), BF16),
+            jax.ShapeDtypeStruct((1, CHANNELS), F32),
+        ),
         scratch_shapes=[
             pltpu.VMEM((ROWS * COLS, CHANNELS), F32),
             pltpu.VMEM((CHANNELS * 16, LANES), F32),
@@ -136,7 +140,7 @@
                 ref[at_rows, row * LANES : (row + 1) * LANES] = whole.astype(BF16)
             return carry
 
-        lax.fori_loop(0, 16, gather, 0)
+        lax.fori_loop(0, 16, gather, 0, unroll=True)
         flip_ref[row * LANES : (row + 1) * LANES, :] = right_ref[
             :, row * LANES : (row + 1) * LANES
         ].T
@@ -165,7 +169,7 @@
                     sums_ref[row * 16 + col_pair * 2 + side] = whole.astype(BF16)
                 return carry
 
-            lax.fori_loop(0, 8, pack, 0)
+            lax.fori_loop(0, 8, pack, 0, unroll=True)
 
 
 def triangle(chunks):
@@ -187,7 +191,7 @@
 
 
 def update_kernel(sums_ref, pair_ref, gate_ref, gain_ref, weight_ref, out_ref, normed_ref, update_ref):
-    gain = gain_ref[...]
+    gain = jnp.broadcast_to(gain_ref[...], (CHANNELS, LANES)).T
     weight = weight_ref[...]
 
     def norm_step(step, carry):
@@ -210,7 +214,7 @@
 
         return carry
 
-    lax.fori_loop(0, SUM_ROWS // 8, norm_step, 0)
+    lax.fori_loop(0, SUM_ROWS // 8, norm_step, 0, unroll=True)
 
     def out_step(step, carry):
         rows = pl.ds(step * 8, 8)
@@ -219,7 +223,7 @@
         out_ref[rows] = (pair_ref[rows].astype(F32) + gate_ref[rows] * update).astype(BF16)
         return carry
 
-    lax.fori_loop(0, ROWS // 8, out_step, 0)
+    lax.fori_loop(0, ROWS // 8, out_step, 0, unroll=4)
 
 
 def update_pair(sums, pair, gate, out_gain, tri_out):
@@ -250,7 +254,7 @@
     first_ref, place_ref, pair_ref, gain_ref, weight_ref, bias_ref, gate_ref, band_ref, table_ref
 ):
     gain = gain_ref[...]
-    weight = weight_ref[...]
+    weight = weight_ref[:, 512:]
     bias = jnp.concatenate([part.astype(F32) for part in split3(bias_ref[...])], 0).astype(BF16)
     table_ref[...] = jnp.zeros_like(table_ref)
 
@@ -274,7 +278,7 @@
                 table_ref[head, pl.ds(8 + step * 8 + at, 1), 0:COLS] = found[head : head + 1]
         return carry
 
-    lax.fori_loop(0, ROWS // 8, norm_step, 0)
+    lax.fori_loop(0, ROWS // 8, norm_step, 0, unroll=4)
 
     lane = lax.broadcasted_iota(jnp.int32, (BAND_ROWS, LANES), 1)
     row_base = place_ref[0]
@@ -294,7 +298,7 @@
         band_ref[target] = total
         return carry
 
-    lax.fori_loop(0, 16, band_step, 0)
+    lax.fori_loop(0, 16, band_step, 0, unroll=4)
 
 
 def side(first, place, pair, pair_gain, gate_weight, bias_wide):
@@ -432,8 +436,7 @@
     col_id = lax.axis_index("col")
     device = row_id * 16 + col_id
 
-    weight = tri_proj[:, :512].T
-    chunks = edges(pair, pair_gain[None], weight)
+    chunks, later_gain = edges(pair, pair_gain[None], tri_proj)
     arrived = lax.all_to_all(chunks, BOTH, 0, 0, tiled=True)
 
     ends = jnp.cumsum(token_atoms)
@@ -451,7 +454,7 @@
 
     bias_wide = jnp.pad(bias_weight.T, ((0, 4), (0, 0)))
     place = jnp.stack([row_id * ROWS, col_id * COLS]).astype(jnp.int32)
-    gate, bands = side(firsts, place, pair, pair_gain[None], tri_proj[:, 512:], bias_wide)
+    gate, bands = side(firsts, place, pair, later_gain, tri_proj, bias_wide)
     band = lax.all_to_all(bands, "col", 0, 0, tiled=True)
 
     ring = list(range(127))
@@ -477,7 +480,7 @@
 
     sums = triangle(arrived)
     returned = lax.all_to_all(sums, BOTH, 0, 0, tiled=True)
-    pair_out = update_pair(returned, pair, gate, out_gain[:, None], tri_out)
+    pair_out = update_pair(returned, pair, gate, out_gain[None], tri_out)
     return (pair_out, atoms_out)
 
 

time: 129 us -> 99.3 us (0.77)
  Pallas kernels: 59.7 us -> 20.7 us
  waiting for transfers between devices: 24.2 us -> 33.7 us
  local copies, waits for them, and re-layouts: 9.19 us -> 11.3 us
    pallas_call x1, Pallas kernels: 22.1 us -> 3.31 us  [triangle(): pl.pallas_call(triangle_kernel, out_shape=jax.ShapeDtypeStruct((CHANNELS,...]
    pallas_call x1, Pallas kernels: 13.6 us -> 3.49 us  [update_pair(): pl.pallas_call(update_kernel, out_shape=jax.ShapeDtypeStruct((ROWS, COLS,...]
    unnamed x19 -> x44, local copies, waits for them, and re-layouts: 3.09 us -> 10 us
    pallas_call x1, Pallas kernels: 10.2 us -> 4.31 us  [side(): pl.pallas_call(side_kernel, out_shape=(jax.ShapeDtypeStruct((ROWS, COLS,...]
    all_to_all x1, waiting for transfers between devices: 19.4 us -> 23.9 us  [on_device(): arrived = lax.all_to_all(chunks, BOTH, 0, 0, tiled=True)]
    pallas_call x1, Pallas kernels: 8.9 us -> 4.9 us  [edges(): pl.pallas_call(edges_kernel, out_shape=(jax.ShapeDtypeStruct((CHANNELS, E...]
    slice x3 -> x1, local copies, waits for them, and re-layouts: 2.37 us -> 0.07 us  [the longest x1 1.38 us: on_device(): tri_proj[:, 512:]]
    ppermute x1, waiting for transfers between devices: 0.01 us -> 1.96 us  [on_device(): after = lax.ppermute(atoms[:HALO], BOTH, [(at + 1, at) for at in ring])]
  transfers between devices with their start and end apart: 5 -> 5, of which waited for: 2 -> 4; matrix products, arithmetic and copies ran while one was open for 6% -> 3% of each run, Pallas kernels for 30% -> 13%
where the time goes in v2:
time: 99.3 us; the launch traced here: 97.7 us
  waiting for transfers between devices  33.7 us (34%)
  starting transfers between devices  26.3 us (26%)
  Pallas kernels  20.7 us (21%)
  local copies, waits for them, and re-layouts  11.3 us (11%)
  between operations  3.53 us (4%)
  other arithmetic  2.04 us (2%)
    all_to_all x1, waiting for transfers between devices, on_device(): arrived = lax.all_to_all(chunks, BOTH, 0, 0, tiled=True)  23.9 us
    all_to_all x1, starting transfers between devices, on_device(): arrived = lax.all_to_all(chunks, BOTH, 0, 0, tiled=True)  11.5 us
    unnamed x44, local copies, waits for them, and re-layouts  10 us
    all_to_all x1, waiting for transfers between devices, on_device(): returned = lax.all_to_all(sums, BOTH, 0, 0, tiled=True)  5.98 us
    pallas_call x1, Pallas kernels, edges(): pl.pallas_call(edges_kernel, out_shape=(jax.ShapeDtypeStruct((CHANNELS, E...  4.9 us
    pallas_call x1, Pallas kernels, atoms_block(): pl.pallas_call(atoms_kernel, out_shape=jax.ShapeDtypeStruct((ATOM_ROWS, L...  4.73 us
    all_to_all x1, starting transfers between devices, on_device(): returned = lax.all_to_all(sums, BOTH, 0, 0, tiled=True)  4.53 us
    all_to_all x1, starting transfers between devices, on_device(): band = lax.all_to_all(bands, 'col', 0, 0, tiled=True)  4.5 us
  transfers between devices with their start and end apart: 5, of which 4 were waited for; matrix products, arithmetic and copies ran while one was open for 3% of the time, Pallas kernels for 13%

profile of v2, /device:TPU:1, one launch (start us, length us, event | category | flops | bytes accessed | tf_op | source)
XLA Modules:
  0.0 97.7 jit_solution(7505881565402658876)
XLA Ops:
  0.6 1.3 %copy-done.4 = bf16[96,48,128]{2,1,0:T(8,128)(2,1)S(1)} copy-done((bf16[96,48,128]{2,1,0:T(8,128)(2,1)S(1)}, bf16[96,48,128]{2,1,0:T(8,128)(2,1)}, u32[]{:S(2)}) %copy-start.4) | copy-done | bytes 1179672
  1.9 0.9 copy-done.10
  2.8 0.7 copy-done.16
  3.5 4.9 %edges.1 = (bf16[128,72,128]{2,1,0:T(8,128)(2,1)S(1)}, f32[1,128]{1,0:T(1,128)S(1)}) custom-call(bf16[96,48,128]{2,1,0:T(8,128)(2,1)S(1)} %copy-done.4, f32[1,128]{1,0:T(1,128)S(1)} %bitcast.17, bf16[128,640]{1,0:T(8,128)(2,1)S(1)} %copy-done.10), custom_call_target="tpu_custom_call" | custom-call | flops 603979776 | bytes 4000000 | tf_op jit(solution)/shard_map/edges/pallas_call | solution.py:94
  8.4 1.4 %copy-done.2 = bf16[128,72,128]{2,1,0:T(8,128)(2,1)} copy-done((bf16[128,72,128]{2,1,0:T(8,128)(2,1)}, bf16[128,72,128]{2,1,0:T(8,128)(2,1)S(1)}, u32[]{:S(2)}) %copy-start.2) | copy-done | bytes 2359320
  9.8 11.5 %all-to-all-start = ((bf16[128,72,128]{2,1,0:T(8,128)(2,1)}), bf16[128,72,128]{2,1,0:T(8,128)(2,1)S(1)}, u32[]{:S(2)}, u32[]{:S(2)}) async-start(bf16[128,72,128]{2,1,0:T(8,128)(2,1)} %copy-done.2), calls=%async_computation | async-start | bytes 4718592 | tf_op jit(solution)/shard_map/all_to_all | solution.py:440
  21.3 0.3 reduce-window.9
  21.7 0.7 pad.4.bias_ref
  22.5 0.1 slice_reduce_fusion
  22.6 0.8 fusion
  23.4 0.2 convert_reduce_fusion.first_ref
  23.6 0.9 copy-done.11
  24.5 4.3 %side.1 = (f32[96,48,128]{2,1,0:T(8,128)S(1)}, f32[16,16,128]{2,1,0:T(8,128)S(1)}) custom-call(s32[16]{0:T(128)S(1)} %convert_reduce_fusion.first_ref, s32[2]{0:T(128)S(1)} %pad_add_fusion.4.place_ref, bf16[96,48,128]{2,1,0:T(8,128)(2,1)S(1)} %copy-done.5, f32[1,128]{1,0:T(1,128)S(1)} %get-tuple-element.7.gain_ref, bf16[128,640]{1,0:T(8,128)(2,1)S(1)} %copy-done.11, ...), custom_call_target="tpu_custom_call" | custom-call | flops 603979776 | bytes 5000000 | tf_op jit(solution)/shard_map/side/pallas_call | solution.py:307
  28.8 1.4 %copy-done = f32[96,48,128]{2,1,0:T(8,128)} copy-done((f32[96,48,128]{2,1,0:T(8,128)}, f32[96,48,128]{2,1,0:T(8,128)S(1)}, u32[]{:S(2)}) %copy-start) | copy-done | bytes 2359320
  30.2 0.7 copy-done.6
  30.9 23.9 %all-to-all-done.chunks_ref = bf16[128,72,128]{2,1,0:T(8,128)(2,1)S(1)} async-done(((bf16[128,72,128]{2,1,0:T(8,128)(2,1)}), bf16[128,72,128]{2,1,0:T(8,128)(2,1)S(1)}, u32[]{:S(2)}, u32[]{:S(2)}) %all-to-all-start) | async-done | bytes 2359328 | tf_op jit(solution)/shard_map/all_to_all | solution.py:440
  54.8 4.5 %all-to-all-start.2 = ((f32[16,16,128]{2,1,0:T(8,128)}), f32[16,16,128]{2,1,0:T(8,128)}, u32[]{:S(2)}, u32[]{:S(2)}) async-start(f32[16,16,128]{2,1,0:T(8,128)} %copy-done.6), calls=%async_computation.2 | async-start | bytes 262144 | tf_op jit(solution)/shard_map/all_to_all | solution.py:458
  59.3 3.3 %triangle.1 = bf16[128,40,128]{2,1,0:T(8,128)(2,1)S(1)} custom-call(bf16[128,72,128]{2,1,0:T(8,128)(2,1)S(1)} %all-to-all-done.chunks_ref), custom_call_target="tpu_custom_call" | custom-call | flops 1610612736 | bytes 4000000 | tf_op jit(solution)/shard_map/triangle/pallas_call | solution.py:176
  62.6 1.0 %copy-done.3 = bf16[128,40,128]{2,1,0:T(8,128)(2,1)} copy-done((bf16[128,40,128]{2,1,0:T(8,128)(2,1)}, bf16[128,40,128]{2,1,0:T(8,128)(2,1)S(1)}, u32[]{:S(2)}) %copy-start.3) | copy-done | bytes 1310744
  63.7 1.9 %all-to-all-done.2.band_ref = f32[16,16,128]{2,1,0:T(8,128)} async-done(((f32[16,16,128]{2,1,0:T(8,128)}), f32[16,16,128]{2,1,0:T(8,128)}, u32[]{:S(2)}, u32[]{:S(2)}) %all-to-all-start.2) | async-done | bytes 131104 | tf_op jit(solution)/shard_map/all_to_all | solution.py:458
  65.6 4.5 %all-to-all-start.1 = ((bf16[128,40,128]{2,1,0:T(8,128)(2,1)}), bf16[128,40,128]{2,1,0:T(8,128)(2,1)S(1)}, u32[]{:S(2)}, u32[]{:S(2)}) async-start(bf16[128,40,128]{2,1,0:T(8,128)(2,1)} %copy-done.3), calls=%async_computation.1 | async-start | bytes 2621440 | tf_op jit(solution)/shard_map/all_to_all | solution.py:482
  70.2 3.7 %collective-permute-start = (bf16[48,128]{1,0:T(8,128)(2,1)S(1)}, bf16[48,128]{1,0:T(8,128)(2,1)S(1)}, u32[]{:S(2)}, u32[]{:S(2)}) collective-permute-start(bf16[48,128]{1,0:T(8,128)(2,1)S(1)} %get-tuple-element.13), channel_id=1, source_target_pairs={{0,1},{1,2},{2,3},{3,4},{4,5},{5,6},{6,7},{7,8},{8,9},{9,10},{10,1... | collective-permute-start | bytes 36872 | tf_op jit(solution)/shard_map/ppermute | solution.py:461
  73.9 2.1 %collective-permute-start.1 = (bf16[48,128]{1,0:T(8,128)(2,1)S(1)}, bf16[48,128]{1,0:T(8,128)(2,1)S(1)}, u32[]{:S(2)}, u32[]{:S(2)}) collective-permute-start(bf16[48,128]{1,0:T(8,128)(2,1)S(1)} %get-tuple-element.12), channel_id=1, source_target_pairs={{1,0},{2,1},{3,2},{4,3},{5,4},{6,5},{7,6},{8,7},{9,8},{10,9},{11,1... | collective-permute-start | bytes 36872 | tf_op jit(solution)/shard_map/ppermute | solution.py:462
  76.0 0.7 convert_reduce_fusion.1
  78.0 0.1 dynamic-slice_bitcast_fusion
  79.5 0.1 broadcast_in_dim_tile.8.sub_start_ref
  79.7 0.1 broadcast_in_dim_tile.9.sub_end_ref
  79.8 2.0 %collective-permute-done.1.after_ref = bf16[48,128]{1,0:T(8,128)(2,1)S(1)} collective-permute-done((bf16[48,128]{1,0:T(8,128)(2,1)S(1)}, bf16[48,128]{1,0:T(8,128)(2,1)S(1)}, u32[]{:S(2)}, u32[]{:S(2)}) %collective-permute-start.1) | collective-permute-done | bytes 12320 | tf_op jit(solution)/shard_map/ppermute | solution.py:462
  81.8 4.7 %atoms_block.1 = bf16[192,128]{1,0:T(8,128)(2,1)} custom-call(s32[1]{0:T(128)} %bitcast.7.base_ref, bf16[192,128]{1,0:T(8,128)(2,1)S(1)} %copy-done.8, bf16[48,128]{1,0:T(8,128)(2,1)S(1)} %collective-permute-done.before_ref, bf16[48,128]{1,0:T(8,128)(2,1)S(1)} %collective-permute-done.1.after_ref, f32[16,16,128]{2,1,0:T(8,128)} %all-to-all-done.2.band_ref, ...), custom_call_target="tpu_custom_call" | custom-call | flops 800000000 | bytes 2000000 | tf_op jit(solution)/shard_map/atoms_block/pallas_call | solution.py:406
  86.5 6.0 %all-to-all-done.1.sums_ref = bf16[128,40,128]{2,1,0:T(8,128)(2,1)S(1)} async-done(((bf16[128,40,128]{2,1,0:T(8,128)(2,1)}), bf16[128,40,128]{2,1,0:T(8,128)(2,1)S(1)}, u32[]{:S(2)}, u32[]{:S(2)}) %all-to-all-start.1) | async-done | bytes 1310752 | tf_op jit(solution)/shard_map/all_to_all | solution.py:482
  92.5 1.7 %copy-done.1 = f32[96,48,128]{2,1,0:T(8,128)S(1)} copy-done((f32[96,48,128]{2,1,0:T(8,128)S(1)}, f32[96,48,128]{2,1,0:T(8,128)}, u32[]{:S(2)}) %copy-start.1) | copy-done | bytes 2359320
  94.2 3.5 %update_pair.1 = bf16[96,48,128]{2,1,0:T(8,128)(2,1)} custom-call(bf16[128,40,128]{2,1,0:T(8,128)(2,1)S(1)} %all-to-all-done.1.sums_ref, bf16[96,48,128]{2,1,0:T(8,128)(2,1)S(1)} %copy-done.5, f32[96,48,128]{2,1,0:T(8,128)S(1)} %copy-done.1, f32[1,128]{1,0:T(1,128)S(1)} %bitcast.16, bf16[128,128]{1,0:T(8,128)(2,1)S(1)} %copy-done.7), custom_call_target="tpu_custom_call" | custom-call | flops 150994944 | bytes 6000000 | tf_op jit(solution)/shard_map/update_pair/pallas_call | solution.py:230
  (47 shorter events, 0.4 us)
Async XLA Ops:
  0.6 1.3 %copy-start.4 = (bf16[96,48,128]{2,1,0:T(8,128)(2,1)S(1)}, bf16[96,48,128]{2,1,0:T(8,128)(2,1)}, u32[]{:S(2)}) copy-start(bf16[96,48,128]{2,1,0:T(8,128)(2,1)} %pair_ref.5) | copy-start | bytes 3538948
  1.9 0.9 copy-start.10
  2.8 0.7 copy-start.16
  8.4 1.4 %copy-start.2 = (bf16[128,72,128]{2,1,0:T(8,128)(2,1)}, bf16[128,72,128]{2,1,0:T(8,128)(2,1)S(1)}, u32[]{:S(2)}) copy-start(bf16[128,72,128]{2,1,0:T(8,128)(2,1)S(1)} %get-tuple-element.6) | copy-start | bytes 7077892
  9.8 11.5 %copy-start.19 = (s32[768]{0:T(1024)S(1)}, s32[768]{0:T(1024)}, u32[]{:S(2)}) copy-start(s32[768]{0:T(1024)} %param.16) | copy-start | bytes 9220
  9.8 13.7 %copy-start.5 = (bf16[96,48,128]{2,1,0:T(8,128)(2,1)S(1)}, bf16[96,48,128]{2,1,0:T(8,128)(2,1)}, u32[]{:S(2)}) copy-start(bf16[96,48,128]{2,1,0:T(8,128)(2,1)} %pair_ref.5) | copy-start | bytes 3538948
  9.8 45.0 %all-to-all-start = ((bf16[128,72,128]{2,1,0:T(8,128)(2,1)}), bf16[128,72,128]{2,1,0:T(8,128)(2,1)S(1)}, u32[]{:S(2)}, u32[]{:S(2)}) async-start(bf16[128,72,128]{2,1,0:T(8,128)(2,1)} %copy-done.2), calls=%async_computation | async-start | bytes 4718592 | tf_op jit(solution)/shard_map/all_to_all | solution.py:440
  22.6 1.0 copy-start.20
  23.6 0.9 copy-start.11
  28.8 1.4 %copy-start = (f32[96,48,128]{2,1,0:T(8,128)}, f32[96,48,128]{2,1,0:T(8,128)S(1)}, u32[]{:S(2)}) copy-start(f32[96,48,128]{2,1,0:T(8,128)S(1)} %get-tuple-element.8.gate_ref) | copy-start | bytes 7077892
  30.2 0.7 copy-start.6
  54.8 10.8 %all-to-all-start.2 = ((f32[16,16,128]{2,1,0:T(8,128)}), f32[16,16,128]{2,1,0:T(8,128)}, u32[]{:S(2)}, u32[]{:S(2)}) async-start(f32[16,16,128]{2,1,0:T(8,128)} %copy-done.6), calls=%async_computation.2 | async-start | bytes 262144 | tf_op jit(solution)/shard_map/all_to_all | solution.py:458
  62.6 1.1 %copy-start.3 = (bf16[128,40,128]{2,1,0:T(8,128)(2,1)}, bf16[128,40,128]{2,1,0:T(8,128)(2,1)S(1)}, u32[]{:S(2)}) copy-start(bf16[128,40,128]{2,1,0:T(8,128)(2,1)S(1)} %triangle.1) | copy-start | bytes 3932164
  63.7 6.5 %copy-start.8 = (bf16[192,128]{1,0:T(8,128)(2,1)S(1)}, bf16[192,128]{1,0:T(8,128)(2,1)}, u32[]{:S(2)}) copy-start(bf16[192,128]{1,0:T(8,128)(2,1)} %atoms_ref.1) | copy-start | bytes 147460
  63.7 12.3 %copy-start.21 = (s32[6]{0:T(128)S(1)}, s32[6]{0:T(128)}, u32[]{:S(2)}) copy-start(s32[6]{0:T(128)} %copy-done.20) | copy-start | bytes 76
  63.7 18.1 %copy-start.12 = (bf16[128,512]{1,0:T(8,128)(2,1)S(1)}, bf16[128,512]{1,0:T(8,128)(2,1)}, u32[]{:S(2)}) copy-start(bf16[128,512]{1,0:T(8,128)(2,1)} %project_ref.1) | copy-start | bytes 393220
  63.7 18.1 %copy-start.13 = (bf16[128,512]{1,0:T(8,128)(2,1)S(1)}, bf16[128,512]{1,0:T(8,128)(2,1)}, u32[]{:S(2)}) copy-start(bf16[128,512]{1,0:T(8,128)(2,1)} %up_ref.1) | copy-start | bytes 393220
  63.7 18.1 %copy-start.14 = (bf16[256,128]{1,0:T(8,128)(2,1)S(1)}, bf16[256,128]{1,0:T(8,128)(2,1)}, u32[]{:S(2)}) copy-start(bf16[256,128]{1,0:T(8,128)(2,1)} %down_ref.1) | copy-start | bytes 196612
  63.7 18.1 %copy-start.15 = (bf16[128,128]{1,0:T(8,128)(2,1)S(1)}, bf16[128,128]{1,0:T(8,128)(2,1)}, u32[]{:S(2)}) copy-start(bf16[128,128]{1,0:T(8,128)(2,1)} %output_ref.1) | copy-start | bytes 98308
  63.7 18.1 %copy-start.17 = (f32[128]{0:T(128)S(1)}, f32[128]{0:T(128)}, u32[]{:S(2)}) copy-start(f32[128]{0:T(128)} %param.22) | copy-start | bytes 1540
  63.7 18.1 %copy-start.18 = (f32[128]{0:T(128)S(1)}, f32[128]{0:T(128)}, u32[]{:S(2)}) copy-start(f32[128]{0:T(128)} %param.25) | copy-start | bytes 1540
  65.6 26.9 %all-to-all-start.1 = ((bf16[128,40,128]{2,1,0:T(8,128)(2,1)}), bf16[128,40,128]{2,1,0:T(8,128)(2,1)S(1)}, u32[]{:S(2)}, u32[]{:S(2)}) async-start(bf16[128,40,128]{2,1,0:T(8,128)(2,1)} %copy-done.3), calls=%async_computation.1 | async-start | bytes 2621440 | tf_op jit(solution)/shard_map/all_to_all | solution.py:482
  70.2 9.6 %collective-permute-start = (bf16[48,128]{1,0:T(8,128)(2,1)S(1)}, bf16[48,128]{1,0:T(8,128)(2,1)S(1)}, u32[]{:S(2)}, u32[]{:S(2)}) collective-permute-start(bf16[48,128]{1,0:T(8,128)(2,1)S(1)} %get-tuple-element.13), channel_id=1, source_target_pairs={{0,1},{1,2},{2,3},{3,4},{4,5},{5,6},{6,7},{7,8},{8,9},{9,10},{10,1... | collective-permute-start | bytes 36872 | tf_op jit(solution)/shard_map/ppermute | solution.py:461
  73.9 7.9 %collective-permute-start.1 = (bf16[48,128]{1,0:T(8,128)(2,1)S(1)}, bf16[48,128]{1,0:T(8,128)(2,1)S(1)}, u32[]{:S(2)}, u32[]{:S(2)}) collective-permute-start(bf16[48,128]{1,0:T(8,128)(2,1)S(1)} %get-tuple-element.12), channel_id=1, source_target_pairs={{1,0},{2,1},{3,2},{4,3},{5,4},{6,5},{7,6},{8,7},{9,8},{10,9},{11,1... | collective-permute-start | bytes 36872 | tf_op jit(solution)/shard_map/ppermute | solution.py:462
  81.8 10.7 %copy-start.7 = (bf16[128,128]{1,0:T(8,128)(2,1)S(1)}, bf16[128,128]{1,0:T(8,128)(2,1)}, u32[]{:S(2)}) copy-start(bf16[128,128]{1,0:T(8,128)(2,1)} %weight_ref.5) | copy-start | bytes 98308
  81.8 10.7 %copy-start.9 = (f32[128]{0:T(128)S(1)}, f32[128]{0:T(128)}, u32[]{:S(2)}) copy-start(f32[128]{0:T(128)} %param.20) | copy-start | bytes 1540
  92.5 1.7 %copy-start.1 = (f32[96,48,128]{2,1,0:T(8,128)S(1)}, f32[96,48,128]{2,1,0:T(8,128)}, u32[]{:S(2)}) copy-start(f32[96,48,128]{2,1,0:T(8,128)} %copy-done) | copy-start | bytes 7077892

commit v3 on v2

--- a/solution.py
+++ b/solution.py
@@ -41,37 +41,81 @@
     return 0.5 * jnp.tanh(0.5 * values) + 0.5
 
 
-def edges_kernel(pair_ref, gain_ref, weight_ref, edges_ref, gain_out_ref, normed_ref, stage_ref):
-    gain = gain_ref[...]
-    gain_out_ref[...] = gain
-    weight = weight_ref[:, :512].T
+def edges_kernel(
+    pair_ref,
+    gain_ref,
+    weight_ref,
+    edges_ref,
+    gain_out_ref,
+    tile_ref,
+    gain_in_ref,
+    weight_in_ref,
+    wide_ref,
+    stage_ref,
+    ready_ref,
+    in_sems,
+    param_sems,
+    out_sems,
+):
+    steps = ROWS // 8
+    gain_copy = pltpu.make_async_copy(gain_ref, gain_in_ref, param_sems.at[0])
+    weight_copy = pltpu.make_async_copy(weight_ref, weight_in_ref, param_sems.at[1])
+    tile_copies = [
+        pltpu.make_async_copy(
+            pair_ref.at[pl.ds(step * 8, 8)], tile_ref.at[pl.ds(step * 8, 8)], in_sems.at[step]
+        )
+        for step in range(steps)
+    ]
+    gain_copy.start()
+    for copy in tile_copies:
+        copy.start()
+    weight_copy.start()
+    gain_copy.wait()
+    gain_out_ref[...] = gain_in_ref[...]
+    gain = jnp.broadcast_to(gain_in_ref[...], (2 * LANES, CHANNELS)).T
+    eye = (
+        lax.broadcasted_iota(jnp.int32, (CHANNELS, CHANNELS), 0)
+        == lax.broadcasted_iota(jnp.int32, (CHANNELS, CHANNELS), 1)
+    ).astype(F32).astype(BF16)
 
     def norm_step(step, carry):
-        tile = pair_ref[pl.ds(step * 8, 8)].astype(F32).reshape(8 * COLS, CHANNELS)
-        normed_ref[pl.ds(pl.multiple_of(step * 8 * COLS, 8 * COLS), 8 * COLS), :] = (
-            layer_norm(tile) * gain
-        )
+        rows = pl.ds(step * 8, 8)
+        pltpu.make_async_copy(pair_ref.at[rows], tile_ref.at[rows], in_sems.at[step]).wait()
+        tile = tile_ref[rows].astype(F32).reshape(8 * COLS, CHANNELS)
+        wide_ref[pl.ds(pl.multiple_of(step * 8 * COLS, 8 * COLS), 8 * COLS), :] = tile
         return carry
 
-    lax.fori_loop(0, ROWS // 8, norm_step, 0, unroll=4)
+    lax.fori_loop(0, steps, norm_step, 0, unroll=3)
+    weight_copy.wait()
+    weight = weight_in_ref[:, :512].T
 
     def packed(col, third, extra):
-        main = normed_ref[pl.ds(col, ROWS, stride=COLS), :]
-        rest = normed_ref[pl.ds(third * 32 * COLS + extra, 32, stride=COLS), :]
+        main = wide_ref[pl.ds(col, ROWS, stride=COLS), :]
+        rest = wide_ref[pl.ds(third * 32 * COLS + extra, 32, stride=COLS), :]
         return jnp.concatenate([main, rest], 0).astype(BF16)
 
-    def emit(sources, left_at, right_at):
-        for at in range(0, len(sources), 2):
+    def emit(sources, count):
+        for at in range(0, count, 2):
             rows = jnp.concatenate([packed(*source) for source in sources[at : at + 2]], 0)
-            project = lax.dot_general(
-                weight, rows, (((1,), (1,)), ((), ())), preferred_element_type=F32
+            flipped = lax.dot_general(
+                eye, rows, (((1,), (1,)), ((), ())), preferred_element_type=F32
             )
+            center = flipped - jnp.mean(flipped, 0, keepdims=True)
+            scale = lax.rsqrt(jnp.mean(center * center, 0, keepdims=True) + EPSILON)
+            inputs = (center * scale * gain).astype(BF16)
+            project = jnp.dot(weight, inputs, preferred_element_type=F32)
             left = sigmoid(project[:128]) * project[128:256]
             right = sigmoid(project[256:384]) * project[384:]
             for half in range(2):
                 lanes = slice(half * LANES, (half + 1) * LANES)
-                stage_ref[pl.ds(left_at + at + half, CHANNELS, stride=16), :] = left[:, lanes]
-                stage_ref[pl.ds(right_at + at + half, CHANNELS, stride=16), :] = right[:, lanes]
+                stage_ref[pl.ds(at + half, CHANNELS, stride=24), :] = left[:, lanes]
+                stage_ref[pl.ds(count + at + half, CHANNELS, stride=24), :] = right[:, lanes]
+
+    def block_copy(group):
+        rows = pl.ds(pl.multiple_of(group * 16, 16), 16)
+        return pltpu.make_async_copy(
+            ready_ref.at[group], edges_ref.at[:, rows, :], out_sems.at[group]
+        )
 
     def block(group, carry):
         sources = []
@@ -79,29 +123,45 @@
             third = jnp.where(group < 3, group, at // 4)
             extra = jnp.where(group < 3, 36 + at, 44 + at % 4)
             sources.append((group * 8 + at, third, extra))
-        emit(sources, 0, 8)
-        edges_ref[:, pl.ds(pl.multiple_of(group * 16, 16), 16), :] = (
-            stage_ref[...].reshape(CHANNELS, 16, LANES).astype(BF16)
-        )
+        emit(sources, 8)
+        ready_ref[group] = stage_ref[...].reshape(CHANNELS, 24, LANES)[:, :16].astype(BF16)
+        block_copy(group).start()
         return carry
 
-    lax.fori_loop(0, 4, block, 0, unroll=True)
-    emit([(32 + at, 2, 44 + at) for at in range(4)], 0, 4)
-    edges_ref[:, 64:72, :] = stage_ref[...].reshape(CHANNELS, 16, LANES)[:, :8].astype(BF16)
+    lax.fori_loop(0, 4, block, 0, unroll=4)
+    emit([(32 + at, 2, 44 + at) for at in range(4)], 4)
+    ready_ref[4, :, 0:8, :] = stage_ref[...].reshape(CHANNELS, 24, LANES)[:, :8].astype(BF16)
+    last = pltpu.make_async_copy(
+        ready_ref.at[4, :, pl.ds(0, 8), :], edges_ref.at[:, pl.ds(64, 8), :], out_sems.at[4]
+    )
+    last.start()
+    for group in range(4):
+        block_copy(group).wait()
+    last.wait()
 
 
 def edges(pair, pair_gain, weight):
+    far = pl.BlockSpec(memory_space=pltpu.HBM)
     return pl.pallas_call(
         edges_kernel,
         out_shape=(
             jax.ShapeDtypeStruct((CHANNELS, EDGE_ROWS, LANES), BF16),
             jax.ShapeDtypeStruct((1, CHANNELS), F32),
         ),
+        in_specs=[far] * 3,
+        out_specs=(far, pl.BlockSpec(memory_space=pltpu.VMEM)),
         scratch_shapes=[
+            pltpu.VMEM((ROWS, COLS, CHANNELS), BF16),
+            pltpu.VMEM((1, CHANNELS), F32),
+            pltpu.VMEM((CHANNELS, 640), BF16),
             pltpu.VMEM((ROWS * COLS, CHANNELS), F32),
-            pltpu.VMEM((CHANNELS * 16, LANES), F32),
+            pltpu.VMEM((CHANNELS * 24, LANES), F32),
+            pltpu.VMEM((5, CHANNELS, 16, LANES), BF16),
+            pltpu.SemaphoreType.DMA((ROWS // 8,)),
+            pltpu.SemaphoreType.DMA((2,)),
+            pltpu.SemaphoreType.DMA((5,)),
         ],
-        compiler_params=pltpu.CompilerParams(vmem_limit_bytes=VMEM_LIMIT),
+        compiler_params=pltpu.CompilerParams(vmem_limit_bytes=56 * 1024 * 1024),
         cost_estimate=pl.CostEstimate(
             flops=2 * ROWS * COLS * 128 * 512, bytes_accessed=4000000, transcendentals=1200000
         ),
@@ -109,7 +169,25 @@
     )(pair, pair_gain, weight)
 
 
-def triangle_kernel(chunks_ref, sums_ref, left_ref, right_ref, flip_ref, out_ref):
+def triangle_kernel(
+    arrived_ref,
+    sums_ref,
+    chunks_ref,
+    left_ref,
+    right_ref,
+    flip_ref,
+    out_ref,
+    ready_ref,
+    in_sems,
+    sems,
+):
+    def row_load(row):
+        part = pl.ds(pl.multiple_of(row * 16, 16), 16)
+        return pltpu.make_async_copy(arrived_ref.at[part], chunks_ref.at[part], in_sems.at[row])
+
+    for row in range(8):
+        row_load(row).start()
+
     lane = lax.broadcasted_iota(jnp.int32, (8, LANES), 1)
     low = lax.broadcasted_iota(jnp.int32, (8, LANES), 0) < 4
 
@@ -120,7 +198,9 @@
             jnp.where(lane < 64, pltpu.roll(second, 64, 1), pltpu.roll(third, 96, 1)),
         )
 
-    for row in range(8):
+    def gather_row(row, carry):
+        row_load(row).wait()
+        lanes = pl.ds(pl.multiple_of(row * LANES, LANES), LANES)
 
         def gather(col, carry):
             chunk = chunks_ref[row * 16 + col].astype(F32)
@@ -137,19 +217,23 @@
                 whole = jnp.concatenate(
                     main + [thirds(main[0], main[1], main[2]), jnp.where(low, last, fine)], 0
                 )
-                ref[at_rows, row * LANES : (row + 1) * LANES] = whole.astype(BF16)
+                ref[at_rows, lanes] = whole.astype(BF16)
             return carry
 
-        lax.fori_loop(0, 16, gather, 0, unroll=True)
-        flip_ref[row * LANES : (row + 1) * LANES, :] = right_ref[
-            :, row * LANES : (row + 1) * LANES
-        ].T
-
-    for pair_at in range(4):
+        lax.fori_loop(0, 16, gather, 0, unroll=16)
+        flip_ref[lanes, :] = right_ref[:, lanes].T
+        return carry
+
+    lax.fori_loop(0, 8, gather_row, 0, unroll=True)
+
+    def row_copy(row):
+        part = pl.ds(pl.multiple_of(row * 16, 16), 16)
+        return pltpu.make_async_copy(ready_ref.at[part], sums_ref.at[part], sems.at[row])
+
+    def product(pair_at, carry):
+        lanes = pl.ds(pl.multiple_of(pair_at * 256, 256), 256)
         out_ref[...] = jnp.dot(
-            flip_ref[...],
-            left_ref[:, pair_at * 256 : (pair_at + 1) * 256],
-            preferred_element_type=F32,
+            flip_ref[...], left_ref[:, lanes], preferred_element_type=F32
         )
         for half in range(2):
             row = pair_at * 2 + half
@@ -166,23 +250,35 @@
                         for at in range(3)
                     ]
                     whole = jnp.concatenate(head + [block[24:40]], 0)
-                    sums_ref[row * 16 + col_pair * 2 + side] = whole.astype(BF16)
+                    ready_ref[row * 16 + col_pair * 2 + side] = whole.astype(BF16)
                 return carry
 
-            lax.fori_loop(0, 8, pack, 0, unroll=True)
+            lax.fori_loop(0, 8, pack, 0, unroll=8)
+            row_copy(row).start()
+        return carry
+
+    lax.fori_loop(0, 4, product, 0, unroll=True)
+    for row in range(8):
+        row_copy(row).wait()
 
 
 def triangle(chunks):
     return pl.pallas_call(
         triangle_kernel,
         out_shape=jax.ShapeDtypeStruct((CHANNELS, SUM_ROWS, LANES), BF16),
+        in_specs=[pl.BlockSpec(memory_space=pltpu.HBM)],
+        out_specs=pl.BlockSpec(memory_space=pltpu.HBM),
         scratch_shapes=[
+            pltpu.VMEM((CHANNELS, EDGE_ROWS, LANES), BF16),
             pltpu.VMEM((TOKENS, 1024), BF16),
             pltpu.VMEM((TOKENS, 1024), BF16),
             pltpu.VMEM((1024, TOKENS), BF16),
             pltpu.VMEM((1024, 256), F32),
+            pltpu.VMEM((CHANNELS, SUM_ROWS, LANES), BF16),
+            pltpu.SemaphoreType.DMA((8,)),
+            pltpu.SemaphoreType.DMA((8,)),
         ],
-        compiler_params=pltpu.CompilerParams(vmem_limit_bytes=VMEM_LIMIT),
+        compiler_params=pltpu.CompilerParams(vmem_limit_bytes=52 * 1024 * 1024),
         cost_estimate=pl.CostEstimate(
             flops=2 * 1024 * 1024 * 768, bytes_accessed=4000000, transcendentals=0
         ),
@@ -190,13 +286,38 @@
     )(chunks)
 
 
-def update_kernel(sums_ref, pair_ref, gate_ref, gain_ref, weight_ref, out_ref, normed_ref, update_ref):
+def update_kernel(
+    sums_ref,
+    pair_ref,
+    gate_ref,
+    gain_ref,
+    weight_ref,
+    out_ref,
+    pair_in_ref,
+    gate_in_ref,
+    ready_ref,
+    normed_ref,
+    update_ref,
+    pair_sems,
+    gate_sems,
+    out_sems,
+):
+    parts = [pl.ds(at * 24, 24) for at in range(4)]
+    loads = []
+    for at, part in enumerate(parts):
+        loads.append(
+            (
+                pltpu.make_async_copy(pair_ref.at[part], pair_in_ref.at[part], pair_sems.at[at]),
+                pltpu.make_async_copy(gate_ref.at[part], gate_in_ref.at[part], gate_sems.at[at]),
+            )
+        )
+        for copy in loads[-1]:
+            copy.start()
     gain = jnp.broadcast_to(gain_ref[...], (CHANNELS, LANES)).T
     weight = weight_ref[...]
 
-    def norm_step(step, carry):
-        rows = pl.ds(pl.multiple_of(step * 8, 8), 8)
-        tile = sums_ref[:, rows, :].astype(F32)
+    for step in range(SUM_ROWS // 8):
+        tile = sums_ref[:, step * 8 : step * 8 + 8, :].astype(F32)
         center = tile - jnp.mean(tile, 0, keepdims=True)
         scale = lax.rsqrt(jnp.mean(center * center, 0, keepdims=True) + EPSILON)
         normed_ref[...] = (center * scale).reshape(CHANNELS * 8, LANES)
@@ -206,35 +327,46 @@
                 block, weight, (((0,), (0,)), ((), ())), preferred_element_type=F32
             )
             update_ref[pl.ds(step * 8 + at, ROWS, stride=COLS), :] = update[:ROWS]
-
-            @pl.when(step < 3)
-            def _():
+            if step < 3:
                 start = step * 32 * COLS + 40 + at
                 update_ref[pl.ds(start, 32, stride=COLS), :] = update[ROWS:]
 
-        return carry
-
-    lax.fori_loop(0, SUM_ROWS // 8, norm_step, 0, unroll=True)
-
-    def out_step(step, carry):
-        rows = pl.ds(step * 8, 8)
-        update = update_ref[pl.ds(pl.multiple_of(step * 8 * COLS, 8 * COLS), 8 * COLS), :]
-        update = update.reshape(8, COLS, CHANNELS)
-        out_ref[rows] = (pair_ref[rows].astype(F32) + gate_ref[rows] * update).astype(BF16)
-        return carry
-
-    lax.fori_loop(0, ROWS // 8, out_step, 0, unroll=4)
+    stores = []
+    for at, part in enumerate(parts):
+        for copy in loads[at]:
+            copy.wait()
+        for step in range(at * 3, at * 3 + 3):
+            rows = pl.ds(step * 8, 8)
+            update = update_ref[pl.ds(step * 8 * COLS, 8 * COLS), :].reshape(8, COLS, CHANNELS)
+            ready_ref[rows] = (
+                pair_in_ref[rows].astype(F32) + gate_in_ref[rows] * update
+            ).astype(BF16)
+        copy = pltpu.make_async_copy(ready_ref.at[part], out_ref.at[part], out_sems.at[at])
+        copy.start()
+        stores.append(copy)
+    for copy in stores:
+        copy.wait()
 
 
 def update_pair(sums, pair, gate, out_gain, tri_out):
+    far = pl.BlockSpec(memory_space=pltpu.HBM)
+    near = pl.BlockSpec(memory_space=pltpu.VMEM)
     return pl.pallas_call(
         update_kernel,
         out_shape=jax.ShapeDtypeStruct((ROWS, COLS, CHANNELS), BF16),
+        in_specs=[near, far, far, near, near],
+        out_specs=far,
         scratch_shapes=[
+            pltpu.VMEM((ROWS, COLS, CHANNELS), BF16),
+            pltpu.VMEM((ROWS, COLS, CHANNELS), F32),
+            pltpu.VMEM((ROWS, COLS, CHANNELS), BF16),
             pltpu.VMEM((CHANNELS * 8, LANES), F32),
             pltpu.VMEM((ROWS * COLS, CHANNELS), F32),
+            pltpu.SemaphoreType.DMA((4,)),
+            pltpu.SemaphoreType.DMA((4,)),
+            pltpu.SemaphoreType.DMA((4,)),
         ],
-        compiler_params=pltpu.CompilerParams(vmem_limit_bytes=VMEM_LIMIT),
+        compiler_params=pltpu.CompilerParams(vmem_limit_bytes=50 * 1024 * 1024),
         cost_estimate=pl.CostEstimate(
             flops=2 * ROWS * COLS * 128 * 128, bytes_accessed=6000000, transcendentals=5000
         ),
@@ -284,8 +416,8 @@
     row_base = place_ref[0]
     col_base = place_ref[1]
 
-    def band_step(target, carry):
-        first = first_ref[target]
+    def band_step(slot, carry):
+        first = first_ref[jnp.bitwise_xor(slot, place_ref[2])]
         start = first - row_base + 8
         total = jnp.zeros((BAND_ROWS, LANES), F32)
         shift = col_base - (first - NEAR)
@@ -295,7 +427,7 @@
             col = lane - head * BAND_COLS - shift
             keep = (lane // BAND_COLS == head) & (col >= 0) & (col < COLS)
             total = total + jnp.where(keep, moved, 0.0)
-        band_ref[target] = total
+        band_ref[slot] = total
         return carry
 
     lax.fori_loop(0, 16, band_step, 0, unroll=4)
@@ -326,7 +458,10 @@
     atoms_ref,
     before_ref,
     after_ref,
-    band_ref,
+    band0_ref,
+    band1_ref,
+    band2_ref,
+    band3_ref,
     lane_start_ref,
     lane_end_ref,
     sub_start_ref,
@@ -363,7 +498,7 @@
     )
     token_head = lax.broadcasted_iota(jnp.int32, (LANES, KEY_ROWS), 0) // BAND_COLS
 
-    band = jnp.sum(band_ref[...], 0)
+    band = band0_ref[0] + band1_ref[0] + band2_ref[0] + band3_ref[0]
     band = jnp.concatenate([band, jnp.zeros((LANES - BAND_ROWS, LANES), F32)], 0)
     picked = [
         jnp.dot(query_hot, part, preferred_element_type=F32).astype(BF16) for part in split3(band)
@@ -453,10 +588,18 @@
     sub_end = lax.dynamic_slice(all_ends, (first + LANES - NEAR,), (BAND_COLS,))
 
     bias_wide = jnp.pad(bias_weight.T, ((0, 4), (0, 0)))
-    place = jnp.stack([row_id * ROWS, col_id * COLS]).astype(jnp.int32)
+    place = jnp.stack([row_id * ROWS, col_id * COLS, col_id]).astype(jnp.int32)
     gate, bands = side(firsts, place, pair, later_gain, tri_proj, bias_wide)
-    band = lax.all_to_all(bands, "col", 0, 0, tiled=True)
-
+    def exchange(values, size):
+        parts = [values[:size]]
+        for at in range(1, 4):
+            pairs = [(device, device ^ (at * size)) for device in range(16)]
+            parts.append(lax.ppermute(values[at * size : (at + 1) * size], "col", pairs))
+        return parts
+
+    halves = exchange(bands, 4)
+    arrived, *halves = lax.optimization_barrier((arrived, *halves))
+    parts = exchange(sum(halves), 1)
     ring = list(range(127))
     before = lax.ppermute(atoms[ATOM_ROWS - HALO :], BOTH, [(at, at + 1) for at in ring])
     after = lax.ppermute(atoms[:HALO], BOTH, [(at + 1, at) for at in ring])
@@ -465,7 +608,7 @@
         atoms,
         before,
         after,
-        band,
+        *parts,
         lane_start[None],
         lane_end[None],
         jnp.tile(sub_start, HEADS)[:, None],

time: 99.3 us -> 90.5 us (0.911); the launches traced: 97.7 us -> 89.9 us
  local copies, waits for them, and re-layouts: 11.3 us -> 2.19 us
  waiting for transfers between devices: 33.7 us -> 28.6 us
  starting transfers between devices: 26.3 us -> 30.1 us
  Pallas kernels: 20.7 us -> 23.9 us
    ppermute x0 -> x6, waiting for transfers between devices: none -> 22.2 us  [exchange(): parts.append(lax.ppermute(values[at * size:(at + 1) * size], 'col', pairs))]
    all_to_all x1, waiting for transfers between devices: 23.9 us -> 4.1 us  [on_device(): arrived = lax.all_to_all(chunks, BOTH, 0, 0, tiled=True)]
    unnamed x44 -> x30, local copies, waits for them, and re-layouts: 10 us -> 1.54 us
    ppermute x0 -> x6, starting transfers between devices: none -> 6.85 us  [exchange(): parts.append(lax.ppermute(values[at * size:(at + 1) * size], 'col', pairs))]
    all_to_all x1 -> x0, starting transfers between devices: 4.5 us -> none  [on_device(): band = lax.all_to_all(bands, 'col', 0, 0, tiled=True)]
    all_to_all x1, waiting for transfers between devices: 5.98 us -> 2.36 us  [on_device(): returned = lax.all_to_all(sums, BOTH, 0, 0, tiled=True)]
    pallas_call x1, Pallas kernels: 3.31 us -> 5.75 us  [triangle(): pl.pallas_call(triangle_kernel, out_shape=jax.ShapeDtypeStruct((CHANNELS,...]
    ppermute x1, waiting for transfers between devices: 1.96 us -> 0.01 us  [on_device(): after = lax.ppermute(atoms[:HALO], BOTH, [(at + 1, at) for at in ring])]
  transfers between devices with their start and end apart: 5 -> 10, of which waited for: 4 -> 6; matrix products, arithmetic and copies ran while one was open for 3% -> 2% of each run, Pallas kernels for 13% -> 9%
where the time goes in v3:
time: 90.5 us; the launch traced here: 89.9 us
  starting transfers between devices  30.1 us (33%)
  waiting for transfers between devices  28.6 us (32%)
  Pallas kernels  23.9 us (26%)
  between operations  3.76 us (4%)
  local copies, waits for them, and re-layouts  2.19 us (2%)
  other arithmetic  1.37 us (2%)
    ppermute x6, waiting for transfers between devices, exchange(): parts.append(lax.ppermute(values[at * size:(at + 1) * size], 'col', pairs))  22.2 us
    all_to_all x1, starting transfers between devices, on_device(): arrived = lax.all_to_all(chunks, BOTH, 0, 0, tiled=True)  11.9 us
    ppermute x6, starting transfers between devices, exchange(): parts.append(lax.ppermute(values[at * size:(at + 1) * size], 'col', pairs))  6.85 us
    pallas_call x1, Pallas kernels, edges(): pl.pallas_call(edges_kernel, out_shape=(jax.ShapeDtypeStruct((CHANNELS, E...  6.41 us
    pallas_call x1, Pallas kernels, triangle(): pl.pallas_call(triangle_kernel, out_shape=jax.ShapeDtypeStruct((CHANNELS,...  5.75 us
    all_to_all x1, starting transfers between devices, on_device(): returned = lax.all_to_all(sums, BOTH, 0, 0, tiled=True)  5.74 us
    pallas_call x1, Pallas kernels, side(): pl.pallas_call(side_kernel, out_shape=(jax.ShapeDtypeStruct((ROWS, COLS,...  4.31 us
    all_to_all x1, waiting for transfers between devices, on_device(): arrived = lax.all_to_all(chunks, BOTH, 0, 0, tiled=True)  4.1 us
  transfers between devices with their start and end apart: 10, of which 6 were waited for; matrix products, arithmetic and copies ran while one was open for 2% of the time, Pallas kernels for 9%

profile of v3, /device:TPU:1, one launch (start us, length us, event | category | flops | bytes accessed | tf_op | source)
XLA Modules:
  0.0 89.9 jit_solution(15456382161635444777)
XLA Ops:
  0.6 6.4 %edges.1 = (bf16[128,72,128]{2,1,0:T(8,128)(2,1)}, f32[1,128]{1,0:T(1,128)}) custom-call(bf16[96,48,128]{2,1,0:T(8,128)(2,1)} %pair_ref.5, f32[1,128]{1,0:T(1,128)} %bitcast.22, bf16[128,640]{1,0:T(8,128)(2,1)} %weight_ref.4), custom_call_target="tpu_custom_call" | custom-call | flops 603979776 | bytes 4000000 | tf_op jit(solution)/shard_map/edges/pallas_call | solution.py:145
  7.1 11.9 %all-to-all-start = ((bf16[128,72,128]{2,1,0:T(8,128)(2,1)}), bf16[128,72,128]{2,1,0:T(8,128)(2,1)}, u32[]{:S(2)}, u32[]{:S(2)}) async-start(bf16[128,72,128]{2,1,0:T(8,128)(2,1)} %get-tuple-element.11), calls=%async_computation | async-start | bytes 4718592 | tf_op jit(solution)/shard_map/all_to_all | solution.py:575
  19.0 0.3 reduce-window.9
  19.3 0.1 slice.37
  19.4 0.1 pad_add_fusion.4.place_ref
  19.5 0.1 slice_reduce_fusion
  19.6 0.1 fusion
  19.7 0.2 convert_reduce_fusion.first_ref
  19.9 4.3 %side.1 = (f32[96,48,128]{2,1,0:T(8,128)S(1)}, f32[16,16,128]{2,1,0:T(8,128)S(1)}) custom-call(s32[16]{0:T(128)S(1)} %convert_reduce_fusion.first_ref, s32[3]{0:T(128)S(1)} %pad_add_fusion.4.place_ref, bf16[96,48,128]{2,1,0:T(8,128)(2,1)S(1)} %copy-done.1, f32[1,128]{1,0:T(1,128)S(1)} %copy-done.12, bf16[128,640]{1,0:T(8,128)(2,1)S(1)} %copy-done.5, ...), custom_call_target="tpu_custom_call" | custom-call | flops 603979776 | bytes 5000000 | tf_op jit(solution)/shard_map/side/pallas_call | solution.py:439
  24.2 1.4 %copy-done = f32[96,48,128]{2,1,0:T(8,128)} copy-done((f32[96,48,128]{2,1,0:T(8,128)}, f32[96,48,128]{2,1,0:T(8,128)S(1)}, u32[]{:S(2)}) %copy-start) | copy-done | bytes 2359320
  25.7 3.4 %collective-permute-start = (f32[4,16,128]{2,1,0:T(8,128)S(1)}, f32[4,16,128]{2,1,0:T(8,128)S(1)}, u32[]{:S(2)}, u32[]{:S(2)}) collective-permute-start(f32[4,16,128]{2,1,0:T(8,128)S(1)} %get-tuple-element.24), channel_id=1, source_target_pairs={{0,4},{1,5},{2,6},{3,7},{4,0},{5,1},{6,2},{7,3},{8,12},{9,13},{10,... | collective-permute-start | bytes 98312 | tf_op jit(solution)/shard_map/ppermute | solution.py:597
  29.1 1.2 %collective-permute-start.1 = (f32[4,16,128]{2,1,0:T(8,128)S(1)}, f32[4,16,128]{2,1,0:T(8,128)S(1)}, u32[]{:S(2)}, u32[]{:S(2)}) collective-permute-start(f32[4,16,128]{2,1,0:T(8,128)S(1)} %get-tuple-element.23), channel_id=1, source_target_pairs={{0,8},{1,9},{2,10},{3,11},{4,12},{5,13},{6,14},{7,15},{8,0},{9,1},... | collective-permute-start | bytes 98312 | tf_op jit(solution)/shard_map/ppermute | solution.py:597
  30.3 17.1 %collective-permute-done = f32[4,16,128]{2,1,0:T(8,128)S(1)} collective-permute-done((f32[4,16,128]{2,1,0:T(8,128)S(1)}, f32[4,16,128]{2,1,0:T(8,128)S(1)}, u32[]{:S(2)}, u32[]{:S(2)}) %collective-permute-start) | collective-permute-done | bytes 32800 | tf_op jit(solution)/shard_map/ppermute | solution.py:597
  47.4 0.7 collective-permute-done.2
  48.1 4.1 %all-to-all-done.arrived_ref = bf16[128,72,128]{2,1,0:T(8,128)(2,1)} async-done(((bf16[128,72,128]{2,1,0:T(8,128)(2,1)}), bf16[128,72,128]{2,1,0:T(8,128)(2,1)}, u32[]{:S(2)}, u32[]{:S(2)}) %all-to-all-start) | async-done | bytes 2359328 | tf_op jit(solution)/shard_map/all_to_all | solution.py:575
  52.2 5.7 %triangle.1 = bf16[128,40,128]{2,1,0:T(8,128)(2,1)} custom-call(bf16[128,72,128]{2,1,0:T(8,128)(2,1)} %all-to-all-done.arrived_ref), custom_call_target="tpu_custom_call" | custom-call | flops 1610612736 | bytes 4000000 | tf_op jit(solution)/shard_map/triangle/pallas_call | solution.py:266
  58.0 5.7 %all-to-all-start.1 = ((bf16[128,40,128]{2,1,0:T(8,128)(2,1)}), bf16[128,40,128]{2,1,0:T(8,128)(2,1)S(1)}, u32[]{:S(2)}, u32[]{:S(2)}) async-start(bf16[128,40,128]{2,1,0:T(8,128)(2,1)} %triangle.1), calls=%async_computation.1 | async-start | bytes 2621440 | tf_op jit(solution)/shard_map/all_to_all | solution.py:625
  63.8 3.7 %collective-permute-start.3 = (bf16[48,128]{1,0:T(8,128)(2,1)S(1)}, bf16[48,128]{1,0:T(8,128)(2,1)S(1)}, u32[]{:S(2)}, u32[]{:S(2)}) collective-permute-start(bf16[48,128]{1,0:T(8,128)(2,1)S(1)} %get-tuple-element.27), channel_id=1, source_target_pairs={{0,1},{1,2},{2,3},{3,4},{4,5},{5,6},{6,7},{7,8},{8,9},{9,10},{10,1... | collective-permute-start | bytes 36872 | tf_op jit(solution)/shard_map/ppermute | solution.py:604
  67.5 1.9 %collective-permute-start.4 = (bf16[48,128]{1,0:T(8,128)(2,1)S(1)}, bf16[48,128]{1,0:T(8,128)(2,1)S(1)}, u32[]{:S(2)}, u32[]{:S(2)}) collective-permute-start(bf16[48,128]{1,0:T(8,128)(2,1)S(1)} %get-tuple-element.26), channel_id=1, source_target_pairs={{1,0},{2,1},{3,2},{4,3},{5,4},{6,5},{7,6},{8,7},{9,8},{10,9},{11,1... | collective-permute-start | bytes 36872 | tf_op jit(solution)/shard_map/ppermute | solution.py:605
  69.4 0.7 convert_reduce_fusion.1
  71.5 0.1 collective-permute-start.5
  71.6 1.9 %collective-permute-start.6 = (f32[1,16,128]{2,1,0:T(8,128)S(1)}, f32[1,16,128]{2,1,0:T(8,128)S(1)}, u32[]{:S(2)}, u32[]{:S(2)}) collective-permute-start(f32[1,16,128]{2,1,0:T(8,128)S(1)} %get-tuple-element.29), channel_id=1, source_target_pairs={{0,2},{1,3},{2,0},{3,1},{4,6},{5,7},{6,4},{7,5},{8,10},{9,11},{10,... | collective-permute-start | bytes 24584 | tf_op jit(solution)/shard_map/ppermute | solution.py:597
  73.4 0.3 collective-permute-start.7
  73.7 0.1 dynamic-slice_bitcast_fusion
  75.1 0.1 dynamic_slice.14
  75.1 0.1 dynamic_slice.15
  75.2 0.1 broadcast_in_dim_tile.8.sub_start_ref
  75.3 0.1 broadcast_in_dim_tile.9.sub_end_ref
  75.6 4.3 %collective-permute-done.7.band3_ref = f32[1,16,128]{2,1,0:T(8,128)S(1)} collective-permute-done((f32[1,16,128]{2,1,0:T(8,128)S(1)}, f32[1,16,128]{2,1,0:T(8,128)S(1)}, u32[]{:S(2)}, u32[]{:S(2)}) %collective-permute-start.7) | collective-permute-done | bytes 8224 | tf_op jit(solution)/shard_map/ppermute | solution.py:597
  79.9 3.8 %atoms_block.1 = bf16[192,128]{1,0:T(8,128)(2,1)} custom-call(s32[1]{0:T(128)} %bitcast.8.base_ref, bf16[192,128]{1,0:T(8,128)(2,1)S(1)} %copy-done.3, bf16[48,128]{1,0:T(8,128)(2,1)S(1)} %collective-permute-done.3.before_ref, bf16[48,128]{1,0:T(8,128)(2,1)S(1)} %collective-permute-done.4.after_ref, f32[1,16,128]{2,1,0:T(8,128)S(1)} %get-tuple-element.31.band0_ref, ...), custom_call_target="tpu_custom_call" | custom-call | flops 800000000 | bytes 2000000 | tf_op jit(solution)/shard_map/atoms_block/pallas_call | solution.py:541
  83.8 2.4 %all-to-all-done.1.sums_ref = bf16[128,40,128]{2,1,0:T(8,128)(2,1)S(1)} async-done(((bf16[128,40,128]{2,1,0:T(8,128)(2,1)}), bf16[128,40,128]{2,1,0:T(8,128)(2,1)S(1)}, u32[]{:S(2)}, u32[]{:S(2)}) %all-to-all-start.1) | async-done | bytes 1310752 | tf_op jit(solution)/shard_map/all_to_all | solution.py:625
  86.1 3.6 %update_pair.1 = bf16[96,48,128]{2,1,0:T(8,128)(2,1)} custom-call(bf16[128,40,128]{2,1,0:T(8,128)(2,1)S(1)} %all-to-all-done.1.sums_ref, bf16[96,48,128]{2,1,0:T(8,128)(2,1)S(1)} %copy-done.1, f32[96,48,128]{2,1,0:T(8,128)} %copy-done, f32[1,128]{1,0:T(1,128)S(1)} %bitcast.17, bf16[128,128]{1,0:T(8,128)(2,1)S(1)} %copy-done.2), custom_call_target="tpu_custom_call" | custom-call | flops 150994944 | bytes 6000000 | tf_op jit(solution)/shard_map/update_pair/pallas_call | solution.py:354
  (46 shorter events, 0.3 us)
Async XLA Ops:
  7.0 12.0 %copy-start.13 = (s32[768]{0:T(1024)S(1)}, s32[768]{0:T(1024)}, u32[]{:S(2)}) copy-start(s32[768]{0:T(1024)} %param.16) | copy-start | bytes 9220
  7.1 12.4 %copy-start.14 = (f32[128,4]{0,1:T(4,128)S(1)}, f32[128,4]{0,1:T(4,128)}, u32[]{:S(2)}) copy-start(f32[128,4]{0,1:T(4,128)} %param.21) | copy-start | bytes 6148
  7.1 12.8 %copy-start.1 = (bf16[96,48,128]{2,1,0:T(8,128)(2,1)S(1)}, bf16[96,48,128]{2,1,0:T(8,128)(2,1)}, u32[]{:S(2)}) copy-start(bf16[96,48,128]{2,1,0:T(8,128)(2,1)} %pair_ref.5) | copy-start | bytes 3538948
  7.1 12.8 %copy-start.5 = (bf16[128,640]{1,0:T(8,128)(2,1)S(1)}, bf16[128,640]{1,0:T(8,128)(2,1)}, u32[]{:S(2)}) copy-start(bf16[128,640]{1,0:T(8,128)(2,1)} %weight_ref.4) | copy-start | bytes 491524
  7.1 12.8 %copy-start.12 = (f32[1,128]{1,0:T(1,128)S(1)}, f32[1,128]{1,0:T(1,128)}, u32[]{:S(2)}) copy-start(f32[1,128]{1,0:T(1,128)} %get-tuple-element.12.gain_ref) | copy-start | bytes 1540
  7.1 45.1 %all-to-all-start = ((bf16[128,72,128]{2,1,0:T(8,128)(2,1)}), bf16[128,72,128]{2,1,0:T(8,128)(2,1)}, u32[]{:S(2)}, u32[]{:S(2)}) async-start(bf16[128,72,128]{2,1,0:T(8,128)(2,1)} %get-tuple-element.11), calls=%async_computation | async-start | bytes 4718592 | tf_op jit(solution)/shard_map/all_to_all | solution.py:575
  24.2 1.5 %copy-start = (f32[96,48,128]{2,1,0:T(8,128)}, f32[96,48,128]{2,1,0:T(8,128)S(1)}, u32[]{:S(2)}) copy-start(f32[96,48,128]{2,1,0:T(8,128)S(1)} %get-tuple-element.15.gate_ref) | copy-start | bytes 7077892
  25.7 21.7 %collective-permute-start = (f32[4,16,128]{2,1,0:T(8,128)S(1)}, f32[4,16,128]{2,1,0:T(8,128)S(1)}, u32[]{:S(2)}, u32[]{:S(2)}) collective-permute-start(f32[4,16,128]{2,1,0:T(8,128)S(1)} %get-tuple-element.24), channel_id=1, source_target_pairs={{0,4},{1,5},{2,6},{3,7},{4,0},{5,1},{6,2},{7,3},{8,12},{9,13},{10,... | collective-permute-start | bytes 98312 | tf_op jit(solution)/shard_map/ppermute | solution.py:597
  29.1 18.3 %collective-permute-start.1 = (f32[4,16,128]{2,1,0:T(8,128)S(1)}, f32[4,16,128]{2,1,0:T(8,128)S(1)}, u32[]{:S(2)}, u32[]{:S(2)}) collective-permute-start(f32[4,16,128]{2,1,0:T(8,128)S(1)} %get-tuple-element.23), channel_id=1, source_target_pairs={{0,8},{1,9},{2,10},{3,11},{4,12},{5,13},{6,14},{7,15},{8,0},{9,1},... | collective-permute-start | bytes 98312 | tf_op jit(solution)/shard_map/ppermute | solution.py:597
  30.3 17.8 %collective-permute-start.2 = (f32[4,16,128]{2,1,0:T(8,128)S(1)}, f32[4,16,128]{2,1,0:T(8,128)S(1)}, u32[]{:S(2)}, u32[]{:S(2)}) collective-permute-start(f32[4,16,128]{2,1,0:T(8,128)S(1)} %get-tuple-element.22), channel_id=1, source_target_pairs={{0,12},{1,13},{2,14},{3,15},{4,8},{5,9},{6,10},{7,11},{8,4},{9,5},... | collective-permute-start | bytes 98312 | tf_op jit(solution)/shard_map/ppermute | solution.py:597
  57.9 5.8 %copy-start.3 = (bf16[192,128]{1,0:T(8,128)(2,1)S(1)}, bf16[192,128]{1,0:T(8,128)(2,1)}, u32[]{:S(2)}) copy-start(bf16[192,128]{1,0:T(8,128)(2,1)} %atoms_ref.1) | copy-start | bytes 147460
  58.0 21.9 %copy-start.6 = (bf16[128,512]{1,0:T(8,128)(2,1)S(1)}, bf16[128,512]{1,0:T(8,128)(2,1)}, u32[]{:S(2)}) copy-start(bf16[128,512]{1,0:T(8,128)(2,1)} %project_ref.1) | copy-start | bytes 393220
  58.0 21.9 %copy-start.7 = (bf16[128,512]{1,0:T(8,128)(2,1)S(1)}, bf16[128,512]{1,0:T(8,128)(2,1)}, u32[]{:S(2)}) copy-start(bf16[128,512]{1,0:T(8,128)(2,1)} %up_ref.1) | copy-start | bytes 393220
  58.0 21.9 %copy-start.8 = (bf16[256,128]{1,0:T(8,128)(2,1)S(1)}, bf16[256,128]{1,0:T(8,128)(2,1)}, u32[]{:S(2)}) copy-start(bf16[256,128]{1,0:T(8,128)(2,1)} %down_ref.1) | copy-start | bytes 196612
  58.0 21.9 %copy-start.9 = (bf16[128,128]{1,0:T(8,128)(2,1)S(1)}, bf16[128,128]{1,0:T(8,128)(2,1)}, u32[]{:S(2)}) copy-start(bf16[128,128]{1,0:T(8,128)(2,1)} %output_ref.1) | copy-start | bytes 98308
  58.0 21.9 %copy-start.10 = (f32[128]{0:T(128)S(1)}, f32[128]{0:T(128)}, u32[]{:S(2)}) copy-start(f32[128]{0:T(128)} %param.22) | copy-start | bytes 1540
  58.0 21.9 %copy-start.11 = (f32[128]{0:T(128)S(1)}, f32[128]{0:T(128)}, u32[]{:S(2)}) copy-start(f32[128]{0:T(128)} %param.25) | copy-start | bytes 1540
  58.0 28.1 %all-to-all-start.1 = ((bf16[128,40,128]{2,1,0:T(8,128)(2,1)}), bf16[128,40,128]{2,1,0:T(8,128)(2,1)S(1)}, u32[]{:S(2)}, u32[]{:S(2)}) async-start(bf16[128,40,128]{2,1,0:T(8,128)(2,1)} %triangle.1), calls=%async_computation.1 | async-start | bytes 2621440 | tf_op jit(solution)/shard_map/all_to_all | solution.py:625
  63.8 11.7 %collective-permute-start.3 = (bf16[48,128]{1,0:T(8,128)(2,1)S(1)}, bf16[48,128]{1,0:T(8,128)(2,1)S(1)}, u32[]{:S(2)}, u32[]{:S(2)}) collective-permute-start(bf16[48,128]{1,0:T(8,128)(2,1)S(1)} %get-tuple-element.27), channel_id=1, source_target_pairs={{0,1},{1,2},{2,3},{3,4},{4,5},{5,6},{6,7},{7,8},{8,9},{9,10},{10,1... | collective-permute-start | bytes 36872 | tf_op jit(solution)/shard_map/ppermute | solution.py:604
  67.5 8.0 %collective-permute-start.4 = (bf16[48,128]{1,0:T(8,128)(2,1)S(1)}, bf16[48,128]{1,0:T(8,128)(2,1)S(1)}, u32[]{:S(2)}, u32[]{:S(2)}) collective-permute-start(bf16[48,128]{1,0:T(8,128)(2,1)S(1)} %get-tuple-element.26), channel_id=1, source_target_pairs={{1,0},{2,1},{3,2},{4,3},{5,4},{6,5},{7,6},{8,7},{9,8},{10,9},{11,1... | collective-permute-start | bytes 36872 | tf_op jit(solution)/shard_map/ppermute | solution.py:605
  71.5 4.0 %collective-permute-start.5 = (f32[1,16,128]{2,1,0:T(8,128)S(1)}, f32[1,16,128]{2,1,0:T(8,128)S(1)}, u32[]{:S(2)}, u32[]{:S(2)}) collective-permute-start(f32[1,16,128]{2,1,0:T(8,128)S(1)} %get-tuple-element.30), channel_id=1, source_target_pairs={{0,1},{1,0},{2,3},{3,2},{4,5},{5,4},{6,7},{7,6},{8,9},{9,8},{10,11... | collective-permute-start | bytes 24584 | tf_op jit(solution)/shard_map/ppermute | solution.py:597
  71.6 4.0 %collective-permute-start.6 = (f32[1,16,128]{2,1,0:T(8,128)S(1)}, f32[1,16,128]{2,1,0:T(8,128)S(1)}, u32[]{:S(2)}, u32[]{:S(2)}) collective-permute-start(f32[1,16,128]{2,1,0:T(8,128)S(1)} %get-tuple-element.29), channel_id=1, source_target_pairs={{0,2},{1,3},{2,0},{3,1},{4,6},{5,7},{6,4},{7,5},{8,10},{9,11},{10,... | collective-permute-start | bytes 24584 | tf_op jit(solution)/shard_map/ppermute | solution.py:597
  73.4 6.5 %collective-permute-start.7 = (f32[1,16,128]{2,1,0:T(8,128)S(1)}, f32[1,16,128]{2,1,0:T(8,128)S(1)}, u32[]{:S(2)}, u32[]{:S(2)}) collective-permute-start(f32[1,16,128]{2,1,0:T(8,128)S(1)} %get-tuple-element.28), channel_id=1, source_target_pairs={{0,3},{1,2},{2,1},{3,0},{4,7},{5,6},{6,5},{7,4},{8,11},{9,10},{10,... | collective-permute-start | bytes 24584 | tf_op jit(solution)/shard_map/ppermute | solution.py:597
  79.9 6.2 %copy-start.2 = (bf16[128,128]{1,0:T(8,128)(2,1)S(1)}, bf16[128,128]{1,0:T(8,128)(2,1)}, u32[]{:S(2)}) copy-start(bf16[128,128]{1,0:T(8,128)(2,1)} %weight_ref.5) | copy-start | bytes 98308
  79.9 6.2 %copy-start.4 = (f32[128]{0:T(128)S(1)}, f32[128]{0:T(128)}, u32[]{:S(2)}) copy-start(f32[128]{0:T(128)} %param.20) | copy-start | bytes 1540

commit v4 on v3

--- a/solution.py
+++ b/solution.py
@@ -23,6 +23,7 @@
 BAND_ROWS = 16
 BAND_COLS = 32
 EDGE_ROWS = 72
+WIDE = 56
 SUM_ROWS = 40
 EPSILON = 1e-05
 BOTH = ("row", "col")
@@ -81,8 +82,10 @@
     def norm_step(step, carry):
         rows = pl.ds(step * 8, 8)
         pltpu.make_async_copy(pair_ref.at[rows], tile_ref.at[rows], in_sems.at[step]).wait()
-        tile = tile_ref[rows].astype(F32).reshape(8 * COLS, CHANNELS)
-        wide_ref[pl.ds(pl.multiple_of(step * 8 * COLS, 8 * COLS), 8 * COLS), :] = tile
+        tile = tile_ref[rows].astype(F32)
+        for at in range(8):
+            start = pl.multiple_of((step * 8 + at) * WIDE, 8)
+            wide_ref[pl.ds(start, COLS), :] = tile[at]
         return carry
 
     lax.fori_loop(0, steps, norm_step, 0, unroll=3)
@@ -90,8 +93,8 @@
     weight = weight_in_ref[:, :512].T
 
     def packed(col, third, extra):
-        main = wide_ref[pl.ds(col, ROWS, stride=COLS), :]
-        rest = wide_ref[pl.ds(third * 32 * COLS + extra, 32, stride=COLS), :]
+        main = wide_ref[pl.ds(col, ROWS, stride=WIDE), :]
+        rest = wide_ref[pl.ds(third * 32 * WIDE + extra, 32, stride=WIDE), :]
         return jnp.concatenate([main, rest], 0).astype(BF16)
 
     def emit(sources, count):
@@ -154,7 +157,7 @@
             pltpu.VMEM((ROWS, COLS, CHANNELS), BF16),
             pltpu.VMEM((1, CHANNELS), F32),
             pltpu.VMEM((CHANNELS, 640), BF16),
-            pltpu.VMEM((ROWS * COLS, CHANNELS), F32),
+            pltpu.VMEM((ROWS * WIDE, CHANNELS), F32),
             pltpu.VMEM((CHANNELS * 24, LANES), F32),
             pltpu.VMEM((5, CHANNELS, 16, LANES), BF16),
             pltpu.SemaphoreType.DMA((ROWS // 8,)),
@@ -221,7 +224,7 @@
             return carry
 
         lax.fori_loop(0, 16, gather, 0, unroll=16)
-        flip_ref[lanes, :] = right_ref[:, lanes].T
+        flip_ref[pl.ds(pl.multiple_of(row * ROWS, ROWS), ROWS), :] = right_ref[:, lanes].T[:ROWS]
         return carry
 
     lax.fori_loop(0, 8, gather_row, 0, unroll=True)
@@ -230,9 +233,9 @@
         part = pl.ds(pl.multiple_of(row * 16, 16), 16)
         return pltpu.make_async_copy(ready_ref.at[part], sums_ref.at[part], sems.at[row])
 
-    def product(pair_at, carry):
+    for pair_at in range(4):
         lanes = pl.ds(pl.multiple_of(pair_at * 256, 256), 256)
-        out_ref[...] = jnp.dot(
+        out_ref[pair_at % 2] = jnp.dot(
             flip_ref[...], left_ref[:, lanes], preferred_element_type=F32
         )
         for half in range(2):
@@ -240,8 +243,8 @@
 
             def pack(col_pair, carry):
                 for side in range(2):
-                    start = pl.multiple_of(col_pair * LANES + side * COLS, 16)
-                    block = out_ref[pl.ds(start, COLS), half * LANES : (half + 1) * LANES]
+                    start = pl.multiple_of(col_pair * ROWS + side * COLS, 16)
+                    block = out_ref[pair_at % 2, pl.ds(start, COLS), half * LANES : (half + 1) * LANES]
                     rest = block[40:48]
                     head = [
                         jnp.where(
@@ -255,9 +258,7 @@
 
             lax.fori_loop(0, 8, pack, 0, unroll=8)
             row_copy(row).start()
-        return carry
-
-    lax.fori_loop(0, 4, product, 0, unroll=True)
+
     for row in range(8):
         row_copy(row).wait()
 
@@ -272,8 +273,8 @@
             pltpu.VMEM((CHANNELS, EDGE_ROWS, LANES), BF16),
             pltpu.VMEM((TOKENS, 1024), BF16),
             pltpu.VMEM((TOKENS, 1024), BF16),
-            pltpu.VMEM((1024, TOKENS), BF16),
-            pltpu.VMEM((1024, 256), F32),
+            pltpu.VMEM((TOKENS, TOKENS), BF16),
+            pltpu.VMEM((2, TOKENS, 256), F32),
             pltpu.VMEM((CHANNELS, SUM_ROWS, LANES), BF16),
             pltpu.SemaphoreType.DMA((8,)),
             pltpu.SemaphoreType.DMA((8,)),
@@ -326,10 +327,10 @@
             update = lax.dot_general(
                 block, weight, (((0,), (0,)), ((), ())), preferred_element_type=F32
             )
-            update_ref[pl.ds(step * 8 + at, ROWS, stride=COLS), :] = update[:ROWS]
+            update_ref[pl.ds(step * 8 + at, ROWS, stride=WIDE), :] = update[:ROWS]
             if step < 3:
-                start = step * 32 * COLS + 40 + at
-                update_ref[pl.ds(start, 32, stride=COLS), :] = update[ROWS:]
+                start = step * 32 * WIDE + 40 + at
+                update_ref[pl.ds(start, 32, stride=WIDE), :] = update[ROWS:]
 
     stores = []
     for at, part in enumerate(parts):
@@ -337,7 +338,7 @@
             copy.wait()
         for step in range(at * 3, at * 3 + 3):
             rows = pl.ds(step * 8, 8)
-            update = update_ref[pl.ds(step * 8 * COLS, 8 * COLS), :].reshape(8, COLS, CHANNELS)
+            update = update_ref[pl.ds(step * 8 * WIDE, 8 * WIDE), :].reshape(8, WIDE, CHANNELS)[:, :COLS]
             ready_ref[rows] = (
                 pair_in_ref[rows].astype(F32) + gate_in_ref[rows] * update
             ).astype(BF16)
@@ -361,7 +362,7 @@
             pltpu.VMEM((ROWS, COLS, CHANNELS), F32),
             pltpu.VMEM((ROWS, COLS, CHANNELS), BF16),
             pltpu.VMEM((CHANNELS * 8, LANES), F32),
-            pltpu.VMEM((ROWS * COLS, CHANNELS), F32),
+            pltpu.VMEM((ROWS * WIDE, CHANNELS), F32),
             pltpu.SemaphoreType.DMA((4,)),
             pltpu.SemaphoreType.DMA((4,)),
             pltpu.SemaphoreType.DMA((4,)),
@@ -598,11 +599,13 @@
         return parts
 
     halves = exchange(bands, 4)
-    arrived, *halves = lax.optimization_barrier((arrived, *halves))
-    parts = exchange(sum(halves), 1)
     ring = list(range(127))
     before = lax.ppermute(atoms[ATOM_ROWS - HALO :], BOTH, [(at, at + 1) for at in ring])
     after = lax.ppermute(atoms[:HALO], BOTH, [(at + 1, at) for at in ring])
+    arrived, before, after, *halves = lax.optimization_barrier(
+        (arrived, before, after, *halves)
+    )
+    parts = exchange(sum(halves), 1)
     atoms_out = atoms_block(
         (device * ATOM_ROWS).astype(jnp.int32)[None],
         atoms,

time: 90.5 us -> 89.6 us (0.990)
  starting transfers between devices: 30.1 us -> 31.3 us
  waiting for transfers between devices: 28.6 us -> 27.6 us
    ppermute x6, waiting for transfers between devices: 22.2 us -> 6.62 us  [exchange(): parts.append(lax.ppermute(values[at * size:(at + 1) * size], 'col', pairs))]
    ppermute x1, waiting for transfers between devices: 0.01 us -> 10.3 us  [on_device(): after = lax.ppermute(atoms[:HALO], BOTH, [(at + 1, at) for at in ring])]
    all_to_all x1, waiting for transfers between devices: 2.36 us -> 6.55 us  [on_device(): returned = lax.all_to_all(sums, BOTH, 0, 0, tiled=True)]
  transfers between devices with their start and end apart: 10 -> 10, of which waited for: 6 -> 7; matrix products, arithmetic and copies ran while one was open for 2% -> 2% of each run, Pallas kernels for 9% -> 9%
where the time goes in v4:
time: 89.6 us; the launch traced here: 89.2 us
  starting transfers between devices  31.3 us (35%)
  waiting for transfers between devices  27.6 us (31%)
  Pallas kernels  23.1 us (26%)
  between operations  3.73 us (4%)
  local copies, waits for them, and re-layouts  2.19 us (2%)
  other arithmetic  1.37 us (2%)
    all_to_all x1, starting transfers between devices, on_device(): arrived = lax.all_to_all(chunks, BOTH, 0, 0, tiled=True)  11.9 us
    ppermute x1, waiting for transfers between devices, on_device(): after = lax.ppermute(atoms[:HALO], BOTH, [(at + 1, at) for at in ring])  10.3 us
    ppermute x6, starting transfers between devices, exchange(): parts.append(lax.ppermute(values[at * size:(at + 1) * size], 'col', pairs))  7.51 us
    ppermute x6, waiting for transfers between devices, exchange(): parts.append(lax.ppermute(values[at * size:(at + 1) * size], 'col', pairs))  6.62 us
    all_to_all x1, waiting for transfers between devices, on_device(): returned = lax.all_to_all(sums, BOTH, 0, 0, tiled=True)  6.55 us
    pallas_call x1, Pallas kernels, edges(): pl.pallas_call(edges_kernel, out_shape=(jax.ShapeDtypeStruct((CHANNELS, E...  6.38 us
    all_to_all x1, starting transfers between devices, on_device(): returned = lax.all_to_all(sums, BOTH, 0, 0, tiled=True)  5.88 us
    pallas_call x1, Pallas kernels, triangle(): pl.pallas_call(triangle_kernel, out_shape=jax.ShapeDtypeStruct((CHANNELS,...  5.32 us
  transfers between devices with their start and end apart: 10, of which 7 were waited for; matrix products, arithmetic and copies ran while one was open for 2% of the time, Pallas kernels for 9%

profile of v4, /device:TPU:1, one launch (start us, length us, event | category | flops | bytes accessed | tf_op | source)
XLA Modules:
  0.0 89.2 jit_solution(12039676878586449675)
XLA Ops:
  0.6 6.4 %edges.1 = (bf16[128,72,128]{2,1,0:T(8,128)(2,1)}, f32[1,128]{1,0:T(1,128)}) custom-call(bf16[96,48,128]{2,1,0:T(8,128)(2,1)} %pair_ref.5, f32[1,128]{1,0:T(1,128)} %bitcast.22, bf16[128,640]{1,0:T(8,128)(2,1)} %weight_ref.4), custom_call_target="tpu_custom_call" | custom-call | flops 603979776 | bytes 4000000 | tf_op jit(solution)/shard_map/edges/pallas_call | solution.py:148
  7.1 11.9 %all-to-all-start = ((bf16[128,72,128]{2,1,0:T(8,128)(2,1)}), bf16[128,72,128]{2,1,0:T(8,128)(2,1)}, u32[]{:S(2)}, u32[]{:S(2)}) async-start(bf16[128,72,128]{2,1,0:T(8,128)(2,1)} %get-tuple-element.13), calls=%async_computation | async-start | bytes 4718592 | tf_op jit(solution)/shard_map/all_to_all | solution.py:576
  19.0 0.3 reduce-window.9
  19.3 0.1 slice.39
  19.4 0.1 pad_add_fusion.4.place_ref
  19.5 0.1 slice_reduce_fusion
  19.6 0.1 fusion
  19.7 0.2 convert_reduce_fusion.first_ref
  19.9 4.3 %side.1 = (f32[96,48,128]{2,1,0:T(8,128)S(1)}, f32[16,16,128]{2,1,0:T(8,128)S(1)}) custom-call(s32[16]{0:T(128)S(1)} %convert_reduce_fusion.first_ref, s32[3]{0:T(128)S(1)} %pad_add_fusion.4.place_ref, bf16[96,48,128]{2,1,0:T(8,128)(2,1)S(1)} %copy-done.1, f32[1,128]{1,0:T(1,128)S(1)} %copy-done.12, bf16[128,640]{1,0:T(8,128)(2,1)S(1)} %copy-done.5, ...), custom_call_target="tpu_custom_call" | custom-call | flops 603979776 | bytes 5000000 | tf_op jit(solution)/shard_map/side/pallas_call | solution.py:440
  24.2 1.4 %copy-done = f32[96,48,128]{2,1,0:T(8,128)} copy-done((f32[96,48,128]{2,1,0:T(8,128)}, f32[96,48,128]{2,1,0:T(8,128)S(1)}, u32[]{:S(2)}) %copy-start) | copy-done | bytes 2359320
  25.7 3.4 %collective-permute-start.2 = (f32[4,16,128]{2,1,0:T(8,128)S(1)}, f32[4,16,128]{2,1,0:T(8,128)S(1)}, u32[]{:S(2)}, u32[]{:S(2)}) collective-permute-start(f32[4,16,128]{2,1,0:T(8,128)S(1)} %get-tuple-element.28), channel_id=1, source_target_pairs={{0,4},{1,5},{2,6},{3,7},{4,0},{5,1},{6,2},{7,3},{8,12},{9,13},{10,... | collective-permute-start | bytes 98312 | tf_op jit(solution)/shard_map/ppermute | solution.py:598
  29.1 1.2 %collective-permute-start.3 = (f32[4,16,128]{2,1,0:T(8,128)S(1)}, f32[4,16,128]{2,1,0:T(8,128)S(1)}, u32[]{:S(2)}, u32[]{:S(2)}) collective-permute-start(f32[4,16,128]{2,1,0:T(8,128)S(1)} %get-tuple-element.27), channel_id=1, source_target_pairs={{0,8},{1,9},{2,10},{3,11},{4,12},{5,13},{6,14},{7,15},{8,0},{9,1},... | collective-permute-start | bytes 98312 | tf_op jit(solution)/shard_map/ppermute | solution.py:598
  30.3 4.1 %collective-permute-start = (bf16[48,128]{1,0:T(8,128)(2,1)S(1)}, bf16[48,128]{1,0:T(8,128)(2,1)S(1)}, u32[]{:S(2)}, u32[]{:S(2)}) collective-permute-start(bf16[48,128]{1,0:T(8,128)(2,1)S(1)} %get-tuple-element.31), channel_id=1, source_target_pairs={{0,1},{1,2},{2,3},{3,4},{4,5},{5,6},{6,7},{7,8},{8,9},{9,10},{10,1... | collective-permute-start | bytes 36872 | tf_op jit(solution)/shard_map/ppermute | solution.py:603
  34.4 1.9 %collective-permute-start.1 = (bf16[48,128]{1,0:T(8,128)(2,1)S(1)}, bf16[48,128]{1,0:T(8,128)(2,1)S(1)}, u32[]{:S(2)}, u32[]{:S(2)}) collective-permute-start(bf16[48,128]{1,0:T(8,128)(2,1)S(1)} %get-tuple-element.30), channel_id=1, source_target_pairs={{1,0},{2,1},{3,2},{4,3},{5,4},{6,5},{7,6},{8,7},{9,8},{10,9},{11,1... | collective-permute-start | bytes 36872 | tf_op jit(solution)/shard_map/ppermute | solution.py:604
  36.4 10.3 %collective-permute-done.1.after_ref = bf16[48,128]{1,0:T(8,128)(2,1)S(1)} collective-permute-done((bf16[48,128]{1,0:T(8,128)(2,1)S(1)}, bf16[48,128]{1,0:T(8,128)(2,1)S(1)}, u32[]{:S(2)}, u32[]{:S(2)}) %collective-permute-start.1) | collective-permute-done | bytes 12320 | tf_op jit(solution)/shard_map/ppermute | solution.py:604
  46.6 0.7 collective-permute-done.2
  47.4 0.7 collective-permute-done.4
  48.1 4.1 %all-to-all-done.arrived_ref = bf16[128,72,128]{2,1,0:T(8,128)(2,1)} async-done(((bf16[128,72,128]{2,1,0:T(8,128)(2,1)}), bf16[128,72,128]{2,1,0:T(8,128)(2,1)}, u32[]{:S(2)}, u32[]{:S(2)}) %all-to-all-start) | async-done | bytes 2359328 | tf_op jit(solution)/shard_map/all_to_all | solution.py:576
  52.2 5.3 %triangle.1 = bf16[128,40,128]{2,1,0:T(8,128)(2,1)} custom-call(bf16[128,72,128]{2,1,0:T(8,128)(2,1)} %all-to-all-done.arrived_ref), custom_call_target="tpu_custom_call" | custom-call | flops 1610612736 | bytes 4000000 | tf_op jit(solution)/shard_map/triangle/pallas_call | solution.py:267
  57.6 5.9 %all-to-all-start.1 = ((bf16[128,40,128]{2,1,0:T(8,128)(2,1)}), bf16[128,40,128]{2,1,0:T(8,128)(2,1)S(1)}, u32[]{:S(2)}, u32[]{:S(2)}) async-start(bf16[128,40,128]{2,1,0:T(8,128)(2,1)} %triangle.1), calls=%async_computation.1 | async-start | bytes 2621440 | tf_op jit(solution)/shard_map/all_to_all | solution.py:628
  63.5 0.7 convert_reduce_fusion.1
  65.5 1.1 %collective-permute-start.5 = (f32[1,16,128]{2,1,0:T(8,128)S(1)}, f32[1,16,128]{2,1,0:T(8,128)S(1)}, u32[]{:S(2)}, u32[]{:S(2)}) collective-permute-start(f32[1,16,128]{2,1,0:T(8,128)S(1)} %get-tuple-element.34), channel_id=1, source_target_pairs={{0,1},{1,0},{2,3},{3,2},{4,5},{5,4},{6,7},{7,6},{8,9},{9,8},{10,11... | collective-permute-start | bytes 24584 | tf_op jit(solution)/shard_map/ppermute | solution.py:598
  66.7 0.8 collective-permute-start.6
  67.5 0.9 %collective-permute-start.7 = (f32[1,16,128]{2,1,0:T(8,128)S(1)}, f32[1,16,128]{2,1,0:T(8,128)S(1)}, u32[]{:S(2)}, u32[]{:S(2)}) collective-permute-start(f32[1,16,128]{2,1,0:T(8,128)S(1)} %get-tuple-element.32), channel_id=1, source_target_pairs={{0,3},{1,2},{2,1},{3,0},{4,7},{5,6},{6,5},{7,4},{8,11},{9,10},{10,... | collective-permute-start | bytes 24584 | tf_op jit(solution)/shard_map/ppermute | solution.py:598
  69.8 0.1 dynamic_slice.14
  69.9 0.1 broadcast_in_dim_tile.8.sub_start_ref
  70.0 0.1 broadcast_in_dim_tile.9.sub_end_ref
  70.2 4.8 %collective-permute-done.6.band2_ref = f32[1,16,128]{2,1,0:T(8,128)S(1)} collective-permute-done((f32[1,16,128]{2,1,0:T(8,128)S(1)}, f32[1,16,128]{2,1,0:T(8,128)S(1)}, u32[]{:S(2)}, u32[]{:S(2)}) %collective-permute-start.6) | collective-permute-done | bytes 8224 | tf_op jit(solution)/shard_map/ppermute | solution.py:598
  75.0 0.4 collective-permute-done.7.band3_ref
  75.4 3.8 %atoms_block.1 = bf16[192,128]{1,0:T(8,128)(2,1)} custom-call(s32[1]{0:T(128)} %bitcast.8.base_ref, bf16[192,128]{1,0:T(8,128)(2,1)S(1)} %copy-done.3, bf16[48,128]{1,0:T(8,128)(2,1)S(1)} %collective-permute-done.before_ref, bf16[48,128]{1,0:T(8,128)(2,1)S(1)} %collective-permute-done.1.after_ref, f32[1,16,128]{2,1,0:T(8,128)S(1)} %get-tuple-element.35.band0_ref, ...), custom_call_target="tpu_custom_call" | custom-call | flops 800000000 | bytes 2000000 | tf_op jit(solution)/shard_map/atoms_block/pallas_call | solution.py:542
  79.3 6.6 %all-to-all-done.1.sums_ref = bf16[128,40,128]{2,1,0:T(8,128)(2,1)S(1)} async-done(((bf16[128,40,128]{2,1,0:T(8,128)(2,1)}), bf16[128,40,128]{2,1,0:T(8,128)(2,1)S(1)}, u32[]{:S(2)}, u32[]{:S(2)}) %all-to-all-start.1) | async-done | bytes 1310752 | tf_op jit(solution)/shard_map/all_to_all | solution.py:628
  85.8 3.2 %update_pair.1 = bf16[96,48,128]{2,1,0:T(8,128)(2,1)} custom-call(bf16[128,40,128]{2,1,0:T(8,128)(2,1)S(1)} %all-to-all-done.1.sums_ref, bf16[96,48,128]{2,1,0:T(8,128)(2,1)S(1)} %copy-done.1, f32[96,48,128]{2,1,0:T(8,128)} %copy-done, f32[1,128]{1,0:T(1,128)S(1)} %bitcast.17, bf16[128,128]{1,0:T(8,128)(2,1)S(1)} %copy-done.2), custom_call_target="tpu_custom_call" | custom-call | flops 150994944 | bytes 6000000 | tf_op jit(solution)/shard_map/update_pair/pallas_call | solution.py:355
  (46 shorter events, 0.4 us)
Async XLA Ops:
  7.0 12.0 %copy-start.13 = (s32[768]{0:T(1024)S(1)}, s32[768]{0:T(1024)}, u32[]{:S(2)}) copy-start(s32[768]{0:T(1024)} %param.16) | copy-start | bytes 9220
  7.0 12.4 %copy-start.14 = (f32[128,4]{0,1:T(4,128)S(1)}, f32[128,4]{0,1:T(4,128)}, u32[]{:S(2)}) copy-start(f32[128,4]{0,1:T(4,128)} %param.21) | copy-start | bytes 6148
  7.0 12.8 %copy-start.1 = (bf16[96,48,128]{2,1,0:T(8,128)(2,1)S(1)}, bf16[96,48,128]{2,1,0:T(8,128)(2,1)}, u32[]{:S(2)}) copy-start(bf16[96,48,128]{2,1,0:T(8,128)(2,1)} %pair_ref.5) | copy-start | bytes 3538948
  7.1 12.8 %copy-start.5 = (bf16[128,640]{1,0:T(8,128)(2,1)S(1)}, bf16[128,640]{1,0:T(8,128)(2,1)}, u32[]{:S(2)}) copy-start(bf16[128,640]{1,0:T(8,128)(2,1)} %weight_ref.4) | copy-start | bytes 491524
  7.1 12.8 %copy-start.12 = (f32[1,128]{1,0:T(1,128)S(1)}, f32[1,128]{1,0:T(1,128)}, u32[]{:S(2)}) copy-start(f32[1,128]{1,0:T(1,128)} %get-tuple-element.14.gain_ref) | copy-start | bytes 1540
  7.1 45.1 %all-to-all-start = ((bf16[128,72,128]{2,1,0:T(8,128)(2,1)}), bf16[128,72,128]{2,1,0:T(8,128)(2,1)}, u32[]{:S(2)}, u32[]{:S(2)}) async-start(bf16[128,72,128]{2,1,0:T(8,128)(2,1)} %get-tuple-element.13), calls=%async_computation | async-start | bytes 4718592 | tf_op jit(solution)/shard_map/all_to_all | solution.py:576
  19.0 11.3 %copy-start.3 = (bf16[192,128]{1,0:T(8,128)(2,1)S(1)}, bf16[192,128]{1,0:T(8,128)(2,1)}, u32[]{:S(2)}) copy-start(bf16[192,128]{1,0:T(8,128)(2,1)} %atoms_ref.1) | copy-start | bytes 147460
  24.2 1.5 %copy-start = (f32[96,48,128]{2,1,0:T(8,128)}, f32[96,48,128]{2,1,0:T(8,128)S(1)}, u32[]{:S(2)}) copy-start(f32[96,48,128]{2,1,0:T(8,128)S(1)} %get-tuple-element.17.gate_ref) | copy-start | bytes 7077892
  25.7 21.7 %collective-permute-start.2 = (f32[4,16,128]{2,1,0:T(8,128)S(1)}, f32[4,16,128]{2,1,0:T(8,128)S(1)}, u32[]{:S(2)}, u32[]{:S(2)}) collective-permute-start(f32[4,16,128]{2,1,0:T(8,128)S(1)} %get-tuple-element.28), channel_id=1, source_target_pairs={{0,4},{1,5},{2,6},{3,7},{4,0},{5,1},{6,2},{7,3},{8,12},{9,13},{10,... | collective-permute-start | bytes 98312 | tf_op jit(solution)/shard_map/ppermute | solution.py:598
  29.1 18.3 %collective-permute-start.3 = (f32[4,16,128]{2,1,0:T(8,128)S(1)}, f32[4,16,128]{2,1,0:T(8,128)S(1)}, u32[]{:S(2)}, u32[]{:S(2)}) collective-permute-start(f32[4,16,128]{2,1,0:T(8,128)S(1)} %get-tuple-element.27), channel_id=1, source_target_pairs={{0,8},{1,9},{2,10},{3,11},{4,12},{5,13},{6,14},{7,15},{8,0},{9,1},... | collective-permute-start | bytes 98312 | tf_op jit(solution)/shard_map/ppermute | solution.py:598
  30.3 17.8 %collective-permute-start.4 = (f32[4,16,128]{2,1,0:T(8,128)S(1)}, f32[4,16,128]{2,1,0:T(8,128)S(1)}, u32[]{:S(2)}, u32[]{:S(2)}) collective-permute-start(f32[4,16,128]{2,1,0:T(8,128)S(1)} %get-tuple-element.26), channel_id=1, source_target_pairs={{0,12},{1,13},{2,14},{3,15},{4,8},{5,9},{6,10},{7,11},{8,4},{9,5},... | collective-permute-start | bytes 98312 | tf_op jit(solution)/shard_map/ppermute | solution.py:598
  30.3 6.0 %collective-permute-start = (bf16[48,128]{1,0:T(8,128)(2,1)S(1)}, bf16[48,128]{1,0:T(8,128)(2,1)S(1)}, u32[]{:S(2)}, u32[]{:S(2)}) collective-permute-start(bf16[48,128]{1,0:T(8,128)(2,1)S(1)} %get-tuple-element.31), channel_id=1, source_target_pairs={{0,1},{1,2},{2,3},{3,4},{4,5},{5,6},{6,7},{7,8},{8,9},{9,10},{10,1... | collective-permute-start | bytes 36872 | tf_op jit(solution)/shard_map/ppermute | solution.py:603
  34.4 12.2 %collective-permute-start.1 = (bf16[48,128]{1,0:T(8,128)(2,1)S(1)}, bf16[48,128]{1,0:T(8,128)(2,1)S(1)}, u32[]{:S(2)}, u32[]{:S(2)}) collective-permute-start(bf16[48,128]{1,0:T(8,128)(2,1)S(1)} %get-tuple-element.30), channel_id=1, source_target_pairs={{1,0},{2,1},{3,2},{4,3},{5,4},{6,5},{7,6},{8,7},{9,8},{10,9},{11,1... | collective-permute-start | bytes 36872 | tf_op jit(solution)/shard_map/ppermute | solution.py:604
  57.5 17.9 %copy-start.6 = (bf16[128,512]{1,0:T(8,128)(2,1)S(1)}, bf16[128,512]{1,0:T(8,128)(2,1)}, u32[]{:S(2)}) copy-start(bf16[128,512]{1,0:T(8,128)(2,1)} %project_ref.1) | copy-start | bytes 393220
  57.5 17.9 %copy-start.7 = (bf16[128,512]{1,0:T(8,128)(2,1)S(1)}, bf16[128,512]{1,0:T(8,128)(2,1)}, u32[]{:S(2)}) copy-start(bf16[128,512]{1,0:T(8,128)(2,1)} %up_ref.1) | copy-start | bytes 393220
  57.5 17.9 %copy-start.8 = (bf16[256,128]{1,0:T(8,128)(2,1)S(1)}, bf16[256,128]{1,0:T(8,128)(2,1)}, u32[]{:S(2)}) copy-start(bf16[256,128]{1,0:T(8,128)(2,1)} %down_ref.1) | copy-start | bytes 196612
  57.5 17.9 %copy-start.9 = (bf16[128,128]{1,0:T(8,128)(2,1)S(1)}, bf16[128,128]{1,0:T(8,128)(2,1)}, u32[]{:S(2)}) copy-start(bf16[128,128]{1,0:T(8,128)(2,1)} %output_ref.1) | copy-start | bytes 98308
  57.5 17.9 %copy-start.10 = (f32[128]{0:T(128)S(1)}, f32[128]{0:T(128)}, u32[]{:S(2)}) copy-start(f32[128]{0:T(128)} %param.22) | copy-start | bytes 1540
  57.6 17.9 %copy-start.11 = (f32[128]{0:T(128)S(1)}, f32[128]{0:T(128)}, u32[]{:S(2)}) copy-start(f32[128]{0:T(128)} %param.25) | copy-start | bytes 1540
  57.6 28.3 %all-to-all-start.1 = ((bf16[128,40,128]{2,1,0:T(8,128)(2,1)}), bf16[128,40,128]{2,1,0:T(8,128)(2,1)S(1)}, u32[]{:S(2)}, u32[]{:S(2)}) async-start(bf16[128,40,128]{2,1,0:T(8,128)(2,1)} %triangle.1), calls=%async_computation.1 | async-start | bytes 2621440 | tf_op jit(solution)/shard_map/all_to_all | solution.py:628
  65.5 4.6 %collective-permute-start.5 = (f32[1,16,128]{2,1,0:T(8,128)S(1)}, f32[1,16,128]{2,1,0:T(8,128)S(1)}, u32[]{:S(2)}, u32[]{:S(2)}) collective-permute-start(f32[1,16,128]{2,1,0:T(8,128)S(1)} %get-tuple-element.34), channel_id=1, source_target_pairs={{0,1},{1,0},{2,3},{3,2},{4,5},{5,4},{6,7},{7,6},{8,9},{9,8},{10,11... | collective-permute-start | bytes 24584 | tf_op jit(solution)/shard_map/ppermute | solution.py:598
  66.7 8.3 %collective-permute-start.6 = (f32[1,16,128]{2,1,0:T(8,128)S(1)}, f32[1,16,128]{2,1,0:T(8,128)S(1)}, u32[]{:S(2)}, u32[]{:S(2)}) collective-permute-start(f32[1,16,128]{2,1,0:T(8,128)S(1)} %get-tuple-element.33), channel_id=1, source_target_pairs={{0,2},{1,3},{2,0},{3,1},{4,6},{5,7},{6,4},{7,5},{8,10},{9,11},{10,... | collective-permute-start | bytes 24584 | tf_op jit(solution)/shard_map/ppermute | solution.py:598
  67.5 7.9 %collective-permute-start.7 = (f32[1,16,128]{2,1,0:T(8,128)S(1)}, f32[1,16,128]{2,1,0:T(8,128)S(1)}, u32[]{:S(2)}, u32[]{:S(2)}) collective-permute-start(f32[1,16,128]{2,1,0:T(8,128)S(1)} %get-tuple-element.32), channel_id=1, source_target_pairs={{0,3},{1,2},{2,1},{3,0},{4,7},{5,6},{6,5},{7,4},{8,11},{9,10},{10,... | collective-permute-start | bytes 24584 | tf_op jit(solution)/shard_map/ppermute | solution.py:598
  75.4 10.4 %copy-start.2 = (bf16[128,128]{1,0:T(8,128)(2,1)S(1)}, bf16[128,128]{1,0:T(8,128)(2,1)}, u32[]{:S(2)}) copy-start(bf16[128,128]{1,0:T(8,128)(2,1)} %weight_ref.5) | copy-start | bytes 98308
  75.4 10.4 %copy-start.4 = (f32[128]{0:T(128)S(1)}, f32[128]{0:T(128)}, u32[]{:S(2)}) copy-start(f32[128]{0:T(128)} %param.20) | copy-start | bytes 1540

commit v5 on v4

--- a/solution.py
+++ b/solution.py
@@ -24,7 +24,8 @@
 BAND_COLS = 32
 EDGE_ROWS = 72
 WIDE = 56
-SUM_ROWS = 40
+SUM_ROWS = 36
+SUM_TILES = CHANNELS * SUM_ROWS // 8
 EPSILON = 1e-05
 BOTH = ("row", "col")
 VMEM_LIMIT = 20 * 1024 * 1024
@@ -230,7 +231,7 @@
     lax.fori_loop(0, 8, gather_row, 0, unroll=True)
 
     def row_copy(row):
-        part = pl.ds(pl.multiple_of(row * 16, 16), 16)
+        part = pl.ds(row * 72, 72)
         return pltpu.make_async_copy(ready_ref.at[part], sums_ref.at[part], sems.at[row])
 
     for pair_at in range(4):
@@ -242,18 +243,25 @@
             row = pair_at * 2 + half
 
             def pack(col_pair, carry):
+                tiles = []
                 for side in range(2):
                     start = pl.multiple_of(col_pair * ROWS + side * COLS, 16)
-                    block = out_ref[pair_at % 2, pl.ds(start, COLS), half * LANES : (half + 1) * LANES]
-                    rest = block[40:48]
-                    head = [
-                        jnp.where(
-                            lane < 96, block[at * 8 : at * 8 + 8], pltpu.roll(rest, 96 - 32 * at, 1)
-                        )
-                        for at in range(3)
+                    block = out_ref[
+                        pair_at % 2, pl.ds(start, COLS), half * LANES : (half + 1) * LANES
                     ]
-                    whole = jnp.concatenate(head + [block[24:40]], 0)
-                    ready_ref[row * 16 + col_pair * 2 + side] = whole.astype(BF16)
+                    part = [block[at * 8 : at * 8 + 8] for at in range(6)]
+                    turned = pltpu.roll(part[4], 4, 0)
+                    fine = jnp.where(low, pltpu.roll(turned, 96, 1), pltpu.roll(part[4], 64, 1))
+                    rest = [pltpu.roll(part[5], 96 - 32 * at, 1) for at in range(3)] + [fine]
+                    whole = [jnp.where(lane < 96, part[at], rest[at]) for at in range(4)]
+                    if side == 0:
+                        last = jnp.where(lane < 96, part[4], pltpu.roll(turned, 32, 1))
+                        tiles = whole
+                    else:
+                        other = jnp.where(lane < 96, turned, pltpu.roll(part[4], 32, 1))
+                        tiles = tiles + [jnp.where(low, last, other)] + whole
+                packed = jnp.concatenate(tiles, 0).reshape(9, 8, LANES).astype(BF16)
+                ready_ref[pl.ds((row * 8 + col_pair) * 9, 9)] = packed
                 return carry
 
             lax.fori_loop(0, 8, pack, 0, unroll=8)
@@ -266,7 +274,7 @@
 def triangle(chunks):
     return pl.pallas_call(
         triangle_kernel,
-        out_shape=jax.ShapeDtypeStruct((CHANNELS, SUM_ROWS, LANES), BF16),
+        out_shape=jax.ShapeDtypeStruct((SUM_TILES, 8, LANES), BF16),
         in_specs=[pl.BlockSpec(memory_space=pltpu.HBM)],
         out_specs=pl.BlockSpec(memory_space=pltpu.HBM),
         scratch_shapes=[
@@ -275,7 +283,7 @@
             pltpu.VMEM((TOKENS, 1024), BF16),
             pltpu.VMEM((TOKENS, TOKENS), BF16),
             pltpu.VMEM((2, TOKENS, 256), F32),
-            pltpu.VMEM((CHANNELS, SUM_ROWS, LANES), BF16),
+            pltpu.VMEM((SUM_TILES, 8, LANES), BF16),
             pltpu.SemaphoreType.DMA((8,)),
             pltpu.SemaphoreType.DMA((8,)),
         ],
@@ -288,6 +296,7 @@
 
 
 def update_kernel(
+    odd_ref,
     sums_ref,
     pair_ref,
     gate_ref,
@@ -298,6 +307,7 @@
     gate_in_ref,
     ready_ref,
     normed_ref,
+    fold_ref,
     update_ref,
     pair_sems,
     gate_sems,
@@ -317,20 +327,39 @@
     gain = jnp.broadcast_to(gain_ref[...], (CHANNELS, LANES)).T
     weight = weight_ref[...]
 
-    for step in range(SUM_ROWS // 8):
-        tile = sums_ref[:, step * 8 : step * 8 + 8, :].astype(F32)
-        center = tile - jnp.mean(tile, 0, keepdims=True)
-        scale = lax.rsqrt(jnp.mean(center * center, 0, keepdims=True) + EPSILON)
-        normed_ref[...] = (center * scale).reshape(CHANNELS * 8, LANES)
-        for at in range(8):
-            block = (normed_ref[pl.ds(at, CHANNELS, stride=8), :] * gain).astype(BF16)
-            update = lax.dot_general(
-                block, weight, (((0,), (0,)), ((), ())), preferred_element_type=F32
-            )
-            update_ref[pl.ds(step * 8 + at, ROWS, stride=WIDE), :] = update[:ROWS]
-            if step < 3:
-                start = step * 32 * WIDE + 40 + at
-                update_ref[pl.ds(start, 32, stride=WIDE), :] = update[ROWS:]
+    def tiles(step):
+        return sums_ref[step * 72 : step * 72 + 72].astype(F32).reshape(8, 9, 8, LANES)
+
+    def channel_mean(total):
+        fold_ref[...] = total.reshape(2 * SUM_ROWS, LANES)
+        mean = (fold_ref[0:SUM_ROWS] + fold_ref[SUM_ROWS:]) * (1.0 / CHANNELS)
+        fold_ref[0:SUM_ROWS] = mean
+        fold_ref[SUM_ROWS:] = mean
+        return fold_ref[...].reshape(1, 9, 8, LANES)
+
+    total = jnp.zeros((9, 8, LANES), F32)
+    for step in range(8):
+        total = total + jnp.sum(tiles(step), 0)
+    mean = channel_mean(total)
+    total = jnp.zeros((9, 8, LANES), F32)
+    for step in range(8):
+        center = tiles(step) - mean
+        total = total + jnp.sum(center * center, 0)
+    scale = lax.rsqrt(channel_mean(total) + EPSILON)
+    for step in range(8):
+        normed = (tiles(step) - mean) * scale
+        normed_ref[step * 576 : step * 576 + 576, :] = normed.reshape(576, LANES)
+
+    turn = odd_ref[0] * 4
+    for at in range(SUM_ROWS):
+        row = lax.rem(turn + at, SUM_ROWS)
+        block = (normed_ref[pl.ds(row, CHANNELS, stride=SUM_ROWS), :] * gain).astype(BF16)
+        update = lax.dot_general(
+            block, weight, (((0,), (0,)), ((), ())), preferred_element_type=F32
+        )
+        update_ref[pl.ds(at, ROWS, stride=WIDE), :] = update[:ROWS]
+        third, col = (at // 8, 40 + at % 8) if at < 24 else (at // 4 - 6, 36 + at % 4)
+        update_ref[pl.ds(third * 32 * WIDE + col, 32, stride=WIDE), :] = update[ROWS:]
 
     stores = []
     for at, part in enumerate(parts):
@@ -349,19 +378,20 @@
         copy.wait()
 
 
-def update_pair(sums, pair, gate, out_gain, tri_out):
+def update_pair(odd, sums, pair, gate, out_gain, tri_out):
     far = pl.BlockSpec(memory_space=pltpu.HBM)
     near = pl.BlockSpec(memory_space=pltpu.VMEM)
     return pl.pallas_call(
         update_kernel,
         out_shape=jax.ShapeDtypeStruct((ROWS, COLS, CHANNELS), BF16),
-        in_specs=[near, far, far, near, near],
+        in_specs=[pl.BlockSpec(memory_space=pltpu.SMEM), near, far, far, near, near],
         out_specs=far,
         scratch_shapes=[
             pltpu.VMEM((ROWS, COLS, CHANNELS), BF16),
             pltpu.VMEM((ROWS, COLS, CHANNELS), F32),
             pltpu.VMEM((ROWS, COLS, CHANNELS), BF16),
-            pltpu.VMEM((CHANNELS * 8, LANES), F32),
+            pltpu.VMEM((CHANNELS * SUM_ROWS, LANES), F32),
+            pltpu.VMEM((2 * SUM_ROWS, LANES), F32),
             pltpu.VMEM((ROWS * WIDE, CHANNELS), F32),
             pltpu.SemaphoreType.DMA((4,)),
             pltpu.SemaphoreType.DMA((4,)),
@@ -372,7 +402,7 @@
             flops=2 * ROWS * COLS * 128 * 128, bytes_accessed=6000000, transcendentals=5000
         ),
         name="update_pair",
-    )(sums, pair, gate, out_gain, tri_out)
+    )(odd, sums, pair, gate, out_gain, tri_out)
 
 
 def split3(values):
@@ -625,8 +655,10 @@
     )
 
     sums = triangle(arrived)
-    returned = lax.all_to_all(sums, BOTH, 0, 0, tiled=True)
-    pair_out = update_pair(returned, pair, gate, out_gain[None], tri_out)
+    chunks = sums.reshape(CHANNELS, SUM_ROWS // 4, 4, LANES)
+    returned = lax.all_to_all(chunks, BOTH, 0, 0, tiled=True).reshape(sums.shape)
+    odd = lax.rem(col_id, 2).astype(jnp.int32)[None]
+    pair_out = update_pair(odd, returned, pair, gate, out_gain[None], tri_out)
     return (pair_out, atoms_out)
 
 

time: 89.6 us -> 88.4 us (0.987)
  waiting for transfers between devices: 27.6 us -> 26.2 us
where the time goes in v5:
time: 88.4 us; the launch traced here: 88.1 us
  starting transfers between devices  31.3 us (35%)
  waiting for transfers between devices  26.2 us (30%)
  Pallas kernels  23.3 us (26%)
  between operations  3.67 us (4%)
  local copies, waits for them, and re-layouts  2.15 us (2%)
  other arithmetic  1.44 us (2%)
    all_to_all x1, starting transfers between devices, on_device(): arrived = lax.all_to_all(chunks, BOTH, 0, 0, tiled=True)  11.9 us
    ppermute x1, waiting for transfers between devices, on_device(): after = lax.ppermute(atoms[:HALO], BOTH, [(at + 1, at) for at in ring])  10.3 us
    ppermute x6, starting transfers between devices, exchange(): parts.append(lax.ppermute(values[at * size:(at + 1) * size], 'col', pairs))  7.51 us
    pallas_call x1, Pallas kernels, edges(): pl.pallas_call(edges_kernel, out_shape=(jax.ShapeDtypeStruct((CHANNELS, E...  6.4 us
    all_to_all x1, waiting for transfers between devices, on_device(): lax.all_to_all(chunks, BOTH, 0, 0, tiled=True).reshape(sums.shape)  6 us
    all_to_all x1, starting transfers between devices, on_device(): lax.all_to_all(chunks, BOTH, 0, 0, tiled=True).reshape(sums.shape)  5.88 us
    ppermute x6, waiting for transfers between devices, exchange(): parts.append(lax.ppermute(values[at * size:(at + 1) * size], 'col', pairs))  5.79 us
    pallas_call x1, Pallas kernels, triangle(): pl.pallas_call(triangle_kernel, out_shape=jax.ShapeDtypeStruct((SUM_TILES...  5.3 us
  transfers between devices with their start and end apart: 10, of which 7 were waited for; matrix products, arithmetic and copies ran while one was open for 2% of the time, Pallas kernels for 9%

profile of v5, /device:TPU:1, one launch (start us, length us, event | category | flops | bytes accessed | tf_op | source)
XLA Modules:
  0.0 88.1 jit_solution(13004320197864793396)
XLA Ops:
  0.6 6.4 %edges.1 = (bf16[128,72,128]{2,1,0:T(8,128)(2,1)}, f32[1,128]{1,0:T(1,128)}) custom-call(bf16[96,48,128]{2,1,0:T(8,128)(2,1)} %pair_ref.5, f32[1,128]{1,0:T(1,128)} %bitcast.26, bf16[128,640]{1,0:T(8,128)(2,1)} %weight_ref.4), custom_call_target="tpu_custom_call" | custom-call | flops 603979776 | bytes 4000000 | tf_op jit(solution)/shard_map/edges/pallas_call | solution.py:149
  7.1 11.9 %all-to-all-start = ((bf16[128,72,128]{2,1,0:T(8,128)(2,1)}), bf16[128,72,128]{2,1,0:T(8,128)(2,1)}, u32[]{:S(2)}, u32[]{:S(2)}) async-start(bf16[128,72,128]{2,1,0:T(8,128)(2,1)} %get-tuple-element.13), calls=%async_computation | async-start | bytes 4718592 | tf_op jit(solution)/shard_map/all_to_all | solution.py:606
  19.0 0.3 reduce-window.9
  19.3 0.1 slice.39
  19.4 0.1 pad_add_fusion.4.place_ref
  19.5 0.1 slice_reduce_fusion
  19.6 0.1 fusion
  19.7 0.2 convert_reduce_fusion.first_ref
  19.9 4.3 %side.1 = (f32[96,48,128]{2,1,0:T(8,128)S(1)}, f32[16,16,128]{2,1,0:T(8,128)S(1)}) custom-call(s32[16]{0:T(128)S(1)} %convert_reduce_fusion.first_ref, s32[3]{0:T(128)S(1)} %pad_add_fusion.4.place_ref, bf16[96,48,128]{2,1,0:T(8,128)(2,1)S(1)} %copy-done.1, f32[1,128]{1,0:T(1,128)S(1)} %copy-done.12, bf16[128,640]{1,0:T(8,128)(2,1)S(1)} %copy-done.5, ...), custom_call_target="tpu_custom_call" | custom-call | flops 603979776 | bytes 5000000 | tf_op jit(solution)/shard_map/side/pallas_call | solution.py:470
  24.2 1.4 %copy-done = f32[96,48,128]{2,1,0:T(8,128)} copy-done((f32[96,48,128]{2,1,0:T(8,128)}, f32[96,48,128]{2,1,0:T(8,128)S(1)}, u32[]{:S(2)}) %copy-start) | copy-done | bytes 2359320
  25.7 3.4 %collective-permute-start.2 = (f32[4,16,128]{2,1,0:T(8,128)S(1)}, f32[4,16,128]{2,1,0:T(8,128)S(1)}, u32[]{:S(2)}, u32[]{:S(2)}) collective-permute-start(f32[4,16,128]{2,1,0:T(8,128)S(1)} %get-tuple-element.28), channel_id=1, source_target_pairs={{0,4},{1,5},{2,6},{3,7},{4,0},{5,1},{6,2},{7,3},{8,12},{9,13},{10,... | collective-permute-start | bytes 98312 | tf_op jit(solution)/shard_map/ppermute | solution.py:628
  29.0 1.2 %collective-permute-start.3 = (f32[4,16,128]{2,1,0:T(8,128)S(1)}, f32[4,16,128]{2,1,0:T(8,128)S(1)}, u32[]{:S(2)}, u32[]{:S(2)}) collective-permute-start(f32[4,16,128]{2,1,0:T(8,128)S(1)} %get-tuple-element.27), channel_id=1, source_target_pairs={{0,8},{1,9},{2,10},{3,11},{4,12},{5,13},{6,14},{7,15},{8,0},{9,1},... | collective-permute-start | bytes 98312 | tf_op jit(solution)/shard_map/ppermute | solution.py:628
  30.3 4.1 %collective-permute-start = (bf16[48,128]{1,0:T(8,128)(2,1)S(1)}, bf16[48,128]{1,0:T(8,128)(2,1)S(1)}, u32[]{:S(2)}, u32[]{:S(2)}) collective-permute-start(bf16[48,128]{1,0:T(8,128)(2,1)S(1)} %get-tuple-element.31), channel_id=1, source_target_pairs={{0,1},{1,2},{2,3},{3,4},{4,5},{5,6},{6,7},{7,8},{8,9},{9,10},{10,1... | collective-permute-start | bytes 36872 | tf_op jit(solution)/shard_map/ppermute | solution.py:633
  34.4 1.9 %collective-permute-start.1 = (bf16[48,128]{1,0:T(8,128)(2,1)S(1)}, bf16[48,128]{1,0:T(8,128)(2,1)S(1)}, u32[]{:S(2)}, u32[]{:S(2)}) collective-permute-start(bf16[48,128]{1,0:T(8,128)(2,1)S(1)} %get-tuple-element.30), channel_id=1, source_target_pairs={{1,0},{2,1},{3,2},{4,3},{5,4},{6,5},{7,6},{8,7},{9,8},{10,9},{11,1... | collective-permute-start | bytes 36872 | tf_op jit(solution)/shard_map/ppermute | solution.py:634
  36.3 10.3 %collective-permute-done.1.after_ref = bf16[48,128]{1,0:T(8,128)(2,1)S(1)} collective-permute-done((bf16[48,128]{1,0:T(8,128)(2,1)S(1)}, bf16[48,128]{1,0:T(8,128)(2,1)S(1)}, u32[]{:S(2)}, u32[]{:S(2)}) %collective-permute-start.1) | collective-permute-done | bytes 12320 | tf_op jit(solution)/shard_map/ppermute | solution.py:634
  46.7 0.7 collective-permute-done.2
  47.4 0.7 collective-permute-done.4
  48.1 4.1 %all-to-all-done.arrived_ref = bf16[128,72,128]{2,1,0:T(8,128)(2,1)} async-done(((bf16[128,72,128]{2,1,0:T(8,128)(2,1)}), bf16[128,72,128]{2,1,0:T(8,128)(2,1)}, u32[]{:S(2)}, u32[]{:S(2)}) %all-to-all-start) | async-done | bytes 2359328 | tf_op jit(solution)/shard_map/all_to_all | solution.py:606
  52.2 5.3 %triangle.1 = bf16[576,8,128]{2,1,0:T(8,128)(2,1)} custom-call(bf16[128,72,128]{2,1,0:T(8,128)(2,1)} %all-to-all-done.arrived_ref), custom_call_target="tpu_custom_call" | custom-call | flops 1610612736 | bytes 4000000 | tf_op jit(solution)/shard_map/triangle/pallas_call | solution.py:275
  57.6 5.9 %all-to-all-start.1 = ((bf16[128,9,4,128]{3,2,1,0:T(4,128)(2,1)}), bf16[128,9,4,128]{3,2,1,0:T(4,128)(2,1)S(1)}, u32[]{:S(2)}, u32[]{:S(2)}) async-start(bf16[128,9,4,128]{3,2,1,0:T(4,128)(2,1)} %bitcast.8), calls=%async_computation.1 | async-start | bytes 2359296 | tf_op jit(solution)/shard_map/all_to_all | solution.py:659
  63.5 0.8 convert_reduce_fusion.1
  65.5 1.1 %collective-permute-start.5 = (f32[1,16,128]{2,1,0:T(8,128)S(1)}, f32[1,16,128]{2,1,0:T(8,128)S(1)}, u32[]{:S(2)}, u32[]{:S(2)}) collective-permute-start(f32[1,16,128]{2,1,0:T(8,128)S(1)} %get-tuple-element.34), channel_id=1, source_target_pairs={{0,1},{1,0},{2,3},{3,2},{4,5},{5,4},{6,7},{7,6},{8,9},{9,8},{10,11... | collective-permute-start | bytes 24584 | tf_op jit(solution)/shard_map/ppermute | solution.py:628
  66.7 0.8 collective-permute-start.6
  67.5 0.9 %collective-permute-start.7 = (f32[1,16,128]{2,1,0:T(8,128)S(1)}, f32[1,16,128]{2,1,0:T(8,128)S(1)}, u32[]{:S(2)}, u32[]{:S(2)}) collective-permute-start(f32[1,16,128]{2,1,0:T(8,128)S(1)} %get-tuple-element.32), channel_id=1, source_target_pairs={{0,3},{1,2},{2,1},{3,0},{4,7},{5,6},{6,5},{7,4},{8,11},{9,10},{10,... | collective-permute-start | bytes 24584 | tf_op jit(solution)/shard_map/ppermute | solution.py:628
  69.8 0.1 dynamic_slice.14
  69.9 0.1 broadcast_in_dim_tile.8.sub_start_ref
  70.0 0.1 broadcast_in_dim_tile.9.sub_end_ref
  70.2 4.1 %collective-permute-done.6.band2_ref = f32[1,16,128]{2,1,0:T(8,128)S(1)} collective-permute-done((f32[1,16,128]{2,1,0:T(8,128)S(1)}, f32[1,16,128]{2,1,0:T(8,128)S(1)}, u32[]{:S(2)}, u32[]{:S(2)}) %collective-permute-start.6) | collective-permute-done | bytes 8224 | tf_op jit(solution)/shard_map/ppermute | solution.py:628
  74.2 0.3 collective-permute-done.7.band3_ref
  74.6 3.8 %atoms_block.1 = bf16[192,128]{1,0:T(8,128)(2,1)} custom-call(s32[1]{0:T(128)} %bitcast.11.base_ref, bf16[192,128]{1,0:T(8,128)(2,1)S(1)} %copy-done.3, bf16[48,128]{1,0:T(8,128)(2,1)S(1)} %collective-permute-done.before_ref, bf16[48,128]{1,0:T(8,128)(2,1)S(1)} %collective-permute-done.1.after_ref, f32[1,16,128]{2,1,0:T(8,128)S(1)} %get-tuple-element.35.band0_ref, ...), custom_call_target="tpu_custom_call" | custom-call | flops 800000000 | bytes 2000000 | tf_op jit(solution)/shard_map/atoms_block/pallas_call | solution.py:572
  78.4 6.0 %all-to-all-done.1 = bf16[128,9,4,128]{3,2,1,0:T(4,128)(2,1)S(1)} async-done(((bf16[128,9,4,128]{3,2,1,0:T(4,128)(2,1)}), bf16[128,9,4,128]{3,2,1,0:T(4,128)(2,1)S(1)}, u32[]{:S(2)}, u32[]{:S(2)}) %all-to-all-start.1) | async-done | bytes 1179680 | tf_op jit(solution)/shard_map/all_to_all | solution.py:659
  84.4 3.5 %update_pair.1 = bf16[96,48,128]{2,1,0:T(8,128)(2,1)} custom-call(s32[1]{0:T(128)} %bitcast.odd_ref, bf16[576,8,128]{2,1,0:T(8,128)(2,1)S(1)} %bitcast.20, bf16[96,48,128]{2,1,0:T(8,128)(2,1)S(1)} %copy-done.1, f32[96,48,128]{2,1,0:T(8,128)} %copy-done, f32[1,128]{1,0:T(1,128)S(1)} %bitcast.21, bf16[128,128]{1,0:T(8,128)(2,1)S(1)} %copy-done.2), custom_call_target="tpu_custom_call" | custom-call | flops 150994944 | bytes 6000000 | tf_op jit(solution)/shard_map/update_pair/pallas_call | solution.py:384
  (46 shorter events, 0.4 us)
Async XLA Ops:
  7.0 12.0 %copy-start.13 = (s32[768]{0:T(1024)S(1)}, s32[768]{0:T(1024)}, u32[]{:S(2)}) copy-start(s32[768]{0:T(1024)} %param.16) | copy-start | bytes 9220
  7.0 12.4 %copy-start.14 = (f32[128,4]{0,1:T(4,128)S(1)}, f32[128,4]{0,1:T(4,128)}, u32[]{:S(2)}) copy-start(f32[128,4]{0,1:T(4,128)} %param.21) | copy-start | bytes 6148
  7.1 12.8 %copy-start.1 = (bf16[96,48,128]{2,1,0:T(8,128)(2,1)S(1)}, bf16[96,48,128]{2,1,0:T(8,128)(2,1)}, u32[]{:S(2)}) copy-start(bf16[96,48,128]{2,1,0:T(8,128)(2,1)} %pair_ref.5) | copy-start | bytes 3538948
  7.1 12.8 %copy-start.5 = (bf16[128,640]{1,0:T(8,128)(2,1)S(1)}, bf16[128,640]{1,0:T(8,128)(2,1)}, u32[]{:S(2)}) copy-start(bf16[128,640]{1,0:T(8,128)(2,1)} %weight_ref.4) | copy-start | bytes 491524
  7.1 12.8 %copy-start.12 = (f32[1,128]{1,0:T(1,128)S(1)}, f32[1,128]{1,0:T(1,128)}, u32[]{:S(2)}) copy-start(f32[1,128]{1,0:T(1,128)} %get-tuple-element.14.gain_ref) | copy-start | bytes 1540
  7.1 45.1 %all-to-all-start = ((bf16[128,72,128]{2,1,0:T(8,128)(2,1)}), bf16[128,72,128]{2,1,0:T(8,128)(2,1)}, u32[]{:S(2)}, u32[]{:S(2)}) async-start(bf16[128,72,128]{2,1,0:T(8,128)(2,1)} %get-tuple-element.13), calls=%async_computation | async-start | bytes 4718592 | tf_op jit(solution)/shard_map/all_to_all | solution.py:606
  19.9 10.4 %copy-start.3 = (bf16[192,128]{1,0:T(8,128)(2,1)S(1)}, bf16[192,128]{1,0:T(8,128)(2,1)}, u32[]{:S(2)}) copy-start(bf16[192,128]{1,0:T(8,128)(2,1)} %atoms_ref.1) | copy-start | bytes 147460
  24.2 1.4 %copy-start = (f32[96,48,128]{2,1,0:T(8,128)}, f32[96,48,128]{2,1,0:T(8,128)S(1)}, u32[]{:S(2)}) copy-start(f32[96,48,128]{2,1,0:T(8,128)S(1)} %get-tuple-element.17.gate_ref) | copy-start | bytes 7077892
  25.7 21.7 %collective-permute-start.2 = (f32[4,16,128]{2,1,0:T(8,128)S(1)}, f32[4,16,128]{2,1,0:T(8,128)S(1)}, u32[]{:S(2)}, u32[]{:S(2)}) collective-permute-start(f32[4,16,128]{2,1,0:T(8,128)S(1)} %get-tuple-element.28), channel_id=1, source_target_pairs={{0,4},{1,5},{2,6},{3,7},{4,0},{5,1},{6,2},{7,3},{8,12},{9,13},{10,... | collective-permute-start | bytes 98312 | tf_op jit(solution)/shard_map/ppermute | solution.py:628
  29.0 18.4 %collective-permute-start.3 = (f32[4,16,128]{2,1,0:T(8,128)S(1)}, f32[4,16,128]{2,1,0:T(8,128)S(1)}, u32[]{:S(2)}, u32[]{:S(2)}) collective-permute-start(f32[4,16,128]{2,1,0:T(8,128)S(1)} %get-tuple-element.27), channel_id=1, source_target_pairs={{0,8},{1,9},{2,10},{3,11},{4,12},{5,13},{6,14},{7,15},{8,0},{9,1},... | collective-permute-start | bytes 98312 | tf_op jit(solution)/shard_map/ppermute | solution.py:628
  30.3 17.8 %collective-permute-start.4 = (f32[4,16,128]{2,1,0:T(8,128)S(1)}, f32[4,16,128]{2,1,0:T(8,128)S(1)}, u32[]{:S(2)}, u32[]{:S(2)}) collective-permute-start(f32[4,16,128]{2,1,0:T(8,128)S(1)} %get-tuple-element.26), channel_id=1, source_target_pairs={{0,12},{1,13},{2,14},{3,15},{4,8},{5,9},{6,10},{7,11},{8,4},{9,5},... | collective-permute-start | bytes 98312 | tf_op jit(solution)/shard_map/ppermute | solution.py:628
  30.3 6.0 %collective-permute-start = (bf16[48,128]{1,0:T(8,128)(2,1)S(1)}, bf16[48,128]{1,0:T(8,128)(2,1)S(1)}, u32[]{:S(2)}, u32[]{:S(2)}) collective-permute-start(bf16[48,128]{1,0:T(8,128)(2,1)S(1)} %get-tuple-element.31), channel_id=1, source_target_pairs={{0,1},{1,2},{2,3},{3,4},{4,5},{5,6},{6,7},{7,8},{8,9},{9,10},{10,1... | collective-permute-start | bytes 36872 | tf_op jit(solution)/shard_map/ppermute | solution.py:633
  34.4 12.2 %collective-permute-start.1 = (bf16[48,128]{1,0:T(8,128)(2,1)S(1)}, bf16[48,128]{1,0:T(8,128)(2,1)S(1)}, u32[]{:S(2)}, u32[]{:S(2)}) collective-permute-start(bf16[48,128]{1,0:T(8,128)(2,1)S(1)} %get-tuple-element.30), channel_id=1, source_target_pairs={{1,0},{2,1},{3,2},{4,3},{5,4},{6,5},{7,6},{8,7},{9,8},{10,9},{11,1... | collective-permute-start | bytes 36872 | tf_op jit(solution)/shard_map/ppermute | solution.py:634
  57.5 17.1 %copy-start.6 = (bf16[128,512]{1,0:T(8,128)(2,1)S(1)}, bf16[128,512]{1,0:T(8,128)(2,1)}, u32[]{:S(2)}) copy-start(bf16[128,512]{1,0:T(8,128)(2,1)} %project_ref.1) | copy-start | bytes 393220
  57.5 17.0 %copy-start.7 = (bf16[128,512]{1,0:T(8,128)(2,1)S(1)}, bf16[128,512]{1,0:T(8,128)(2,1)}, u32[]{:S(2)}) copy-start(bf16[128,512]{1,0:T(8,128)(2,1)} %up_ref.1) | copy-start | bytes 393220
  57.5 17.0 %copy-start.8 = (bf16[256,128]{1,0:T(8,128)(2,1)S(1)}, bf16[256,128]{1,0:T(8,128)(2,1)}, u32[]{:S(2)}) copy-start(bf16[256,128]{1,0:T(8,128)(2,1)} %down_ref.1) | copy-start | bytes 196612
  57.5 17.0 %copy-start.9 = (bf16[128,128]{1,0:T(8,128)(2,1)S(1)}, bf16[128,128]{1,0:T(8,128)(2,1)}, u32[]{:S(2)}) copy-start(bf16[128,128]{1,0:T(8,128)(2,1)} %output_ref.1) | copy-start | bytes 98308
  57.5 17.0 %copy-start.10 = (f32[128]{0:T(128)S(1)}, f32[128]{0:T(128)}, u32[]{:S(2)}) copy-start(f32[128]{0:T(128)} %param.22) | copy-start | bytes 1540
  57.5 17.0 %copy-start.11 = (f32[128]{0:T(128)S(1)}, f32[128]{0:T(128)}, u32[]{:S(2)}) copy-start(f32[128]{0:T(128)} %param.25) | copy-start | bytes 1540
  57.6 26.9 %all-to-all-start.1 = ((bf16[128,9,4,128]{3,2,1,0:T(4,128)(2,1)}), bf16[128,9,4,128]{3,2,1,0:T(4,128)(2,1)S(1)}, u32[]{:S(2)}, u32[]{:S(2)}) async-start(bf16[128,9,4,128]{3,2,1,0:T(4,128)(2,1)} %bitcast.8), calls=%async_computation.1 | async-start | bytes 2359296 | tf_op jit(solution)/shard_map/all_to_all | solution.py:659
  65.5 4.6 %collective-permute-start.5 = (f32[1,16,128]{2,1,0:T(8,128)S(1)}, f32[1,16,128]{2,1,0:T(8,128)S(1)}, u32[]{:S(2)}, u32[]{:S(2)}) collective-permute-start(f32[1,16,128]{2,1,0:T(8,128)S(1)} %get-tuple-element.34), channel_id=1, source_target_pairs={{0,1},{1,0},{2,3},{3,2},{4,5},{5,4},{6,7},{7,6},{8,9},{9,8},{10,11... | collective-permute-start | bytes 24584 | tf_op jit(solution)/shard_map/ppermute | solution.py:628
  66.7 7.6 %collective-permute-start.6 = (f32[1,16,128]{2,1,0:T(8,128)S(1)}, f32[1,16,128]{2,1,0:T(8,128)S(1)}, u32[]{:S(2)}, u32[]{:S(2)}) collective-permute-start(f32[1,16,128]{2,1,0:T(8,128)S(1)} %get-tuple-element.33), channel_id=1, source_target_pairs={{0,2},{1,3},{2,0},{3,1},{4,6},{5,7},{6,4},{7,5},{8,10},{9,11},{10,... | collective-permute-start | bytes 24584 | tf_op jit(solution)/shard_map/ppermute | solution.py:628
  67.5 7.0 %collective-permute-start.7 = (f32[1,16,128]{2,1,0:T(8,128)S(1)}, f32[1,16,128]{2,1,0:T(8,128)S(1)}, u32[]{:S(2)}, u32[]{:S(2)}) collective-permute-start(f32[1,16,128]{2,1,0:T(8,128)S(1)} %get-tuple-element.32), channel_id=1, source_target_pairs={{0,3},{1,2},{2,1},{3,0},{4,7},{5,6},{6,5},{7,4},{8,11},{9,10},{10,... | collective-permute-start | bytes 24584 | tf_op jit(solution)/shard_map/ppermute | solution.py:628
  74.6 9.9 %copy-start.2 = (bf16[128,128]{1,0:T(8,128)(2,1)S(1)}, bf16[128,128]{1,0:T(8,128)(2,1)}, u32[]{:S(2)}) copy-start(bf16[128,128]{1,0:T(8,128)(2,1)} %weight_ref.5) | copy-start | bytes 98308
  74.6 9.8 %copy-start.4 = (f32[128]{0:T(128)S(1)}, f32[128]{0:T(128)}, u32[]{:S(2)}) copy-start(f32[128]{0:T(128)} %param.20) | copy-start | bytes 1540

commit v6 on v5

--- a/solution.py
+++ b/solution.py
@@ -75,10 +75,10 @@
     gain_copy.wait()
     gain_out_ref[...] = gain_in_ref[...]
     gain = jnp.broadcast_to(gain_in_ref[...], (2 * LANES, CHANNELS)).T
-    eye = (
-        lax.broadcasted_iota(jnp.int32, (CHANNELS, CHANNELS), 0)
-        == lax.broadcasted_iota(jnp.int32, (CHANNELS, CHANNELS), 1)
-    ).astype(F32).astype(BF16)
+    same = lax.broadcasted_iota(jnp.int32, (CHANNELS, CHANNELS), 0) == lax.broadcasted_iota(
+        jnp.int32, (CHANNELS, CHANNELS), 1
+    )
+    centering = (same.astype(F32) - 1.0 / CHANNELS).astype(BF16)
 
     def norm_step(step, carry):
         rows = pl.ds(step * 8, 8)
@@ -101,10 +101,9 @@
     def emit(sources, count):
         for at in range(0, count, 2):
             rows = jnp.concatenate([packed(*source) for source in sources[at : at + 2]], 0)
-            flipped = lax.dot_general(
-                eye, rows, (((1,), (1,)), ((), ())), preferred_element_type=F32
+            center = lax.dot_general(
+                centering, rows, (((1,), (1,)), ((), ())), preferred_element_type=F32
             )
-            center = flipped - jnp.mean(flipped, 0, keepdims=True)
             scale = lax.rsqrt(jnp.mean(center * center, 0, keepdims=True) + EPSILON)
             inputs = (center * scale * gain).astype(BF16)
             project = jnp.dot(weight, inputs, preferred_element_type=F32)
@@ -128,13 +127,13 @@
             extra = jnp.where(group < 3, 36 + at, 44 + at % 4)
             sources.append((group * 8 + at, third, extra))
         emit(sources, 8)
-        ready_ref[group] = stage_ref[...].reshape(CHANNELS, 24, LANES)[:, :16].astype(BF16)
+        ready_ref[group] = stage_ref[: CHANNELS * 24].reshape(CHANNELS, 24, LANES)[:, :16].astype(BF16)
         block_copy(group).start()
         return carry
 
     lax.fori_loop(0, 4, block, 0, unroll=4)
     emit([(32 + at, 2, 44 + at) for at in range(4)], 4)
-    ready_ref[4, :, 0:8, :] = stage_ref[...].reshape(CHANNELS, 24, LANES)[:, :8].astype(BF16)
+    ready_ref[4, :, 0:8, :] = stage_ref[: CHANNELS * 24].reshape(CHANNELS, 24, LANES)[:, :8].astype(BF16)
     last = pltpu.make_async_copy(
         ready_ref.at[4, :, pl.ds(0, 8), :], edges_ref.at[:, pl.ds(64, 8), :], out_sems.at[4]
     )
@@ -158,8 +157,8 @@
             pltpu.VMEM((ROWS, COLS, CHANNELS), BF16),
             pltpu.VMEM((1, CHANNELS), F32),
             pltpu.VMEM((CHANNELS, 640), BF16),
-            pltpu.VMEM((ROWS * WIDE, CHANNELS), F32),
-            pltpu.VMEM((CHANNELS * 24, LANES), F32),
+            pltpu.VMEM(((ROWS + 1) * WIDE, CHANNELS), F32),
+            pltpu.VMEM(((CHANNELS + 1) * 24, LANES), F32),
             pltpu.VMEM((5, CHANNELS, 16, LANES), BF16),
             pltpu.SemaphoreType.DMA((ROWS // 8,)),
             pltpu.SemaphoreType.DMA((2,)),
@@ -390,9 +389,9 @@
             pltpu.VMEM((ROWS, COLS, CHANNELS), BF16),
             pltpu.VMEM((ROWS, COLS, CHANNELS), F32),
             pltpu.VMEM((ROWS, COLS, CHANNELS), BF16),
-            pltpu.VMEM((CHANNELS * SUM_ROWS, LANES), F32),
+            pltpu.VMEM(((CHANNELS + 1) * SUM_ROWS, LANES), F32),
             pltpu.VMEM((2 * SUM_ROWS, LANES), F32),
-            pltpu.VMEM((ROWS * WIDE, CHANNELS), F32),
+            pltpu.VMEM(((ROWS + 1) * WIDE, CHANNELS), F32),
             pltpu.SemaphoreType.DMA((4,)),
             pltpu.SemaphoreType.DMA((4,)),
             pltpu.SemaphoreType.DMA((4,)),

time: 88.4 us -> 88.1 us (level)
  no operation moved by 1% of the time
where the time goes in v6:
time: 88.1 us; the launch traced here: 87.7 us
  starting transfers between devices  31.3 us (36%)
  waiting for transfers between devices  26.2 us (30%)
  Pallas kernels  23 us (26%)
  between operations  3.67 us (4%)
  local copies, waits for them, and re-layouts  2.15 us (2%)
  other arithmetic  1.44 us (2%)
    all_to_all x1, starting transfers between devices, on_device(): arrived = lax.all_to_all(chunks, BOTH, 0, 0, tiled=True)  11.9 us
    ppermute x1, waiting for transfers between devices, on_device(): after = lax.ppermute(atoms[:HALO], BOTH, [(at + 1, at) for at in ring])  10.3 us
    ppermute x6, starting transfers between devices, exchange(): parts.append(lax.ppermute(values[at * size:(at + 1) * size], 'col', pairs))  7.51 us
    pallas_call x1, Pallas kernels, edges(): pl.pallas_call(edges_kernel, out_shape=(jax.ShapeDtypeStruct((CHANNELS, E...  6.08 us
    all_to_all x1, waiting for transfers between devices, on_device(): lax.all_to_all(chunks, BOTH, 0, 0, tiled=True).reshape(sums.shape)  6 us
    all_to_all x1, starting transfers between devices, on_device(): lax.all_to_all(chunks, BOTH, 0, 0, tiled=True).reshape(sums.shape)  5.88 us
    ppermute x6, waiting for transfers between devices, exchange(): parts.append(lax.ppermute(values[at * size:(at + 1) * size], 'col', pairs))  5.79 us
    pallas_call x1, Pallas kernels, triangle(): pl.pallas_call(triangle_kernel, out_shape=jax.ShapeDtypeStruct((SUM_TILES...  5.3 us
  transfers between devices with their start and end apart: 10, of which 7 were waited for; matrix products, arithmetic and copies ran while one was open for 2% of the time, Pallas kernels for 9%

profile of v6, /device:TPU:1, one launch (start us, length us, event | category | flops | bytes accessed | tf_op | source)
XLA Modules:
  0.0 87.7 jit_solution(9438880280358626296)
XLA Ops:
  0.6 6.1 %edges.1 = (bf16[128,72,128]{2,1,0:T(8,128)(2,1)}, f32[1,128]{1,0:T(1,128)}) custom-call(bf16[96,48,128]{2,1,0:T(8,128)(2,1)} %pair_ref.5, f32[1,128]{1,0:T(1,128)} %bitcast.26, bf16[128,640]{1,0:T(8,128)(2,1)} %weight_ref.4), custom_call_target="tpu_custom_call" | custom-call | flops 603979776 | bytes 4000000 | tf_op jit(solution)/shard_map/edges/pallas_call | solution.py:148
  6.8 11.9 %all-to-all-start = ((bf16[128,72,128]{2,1,0:T(8,128)(2,1)}), bf16[128,72,128]{2,1,0:T(8,128)(2,1)}, u32[]{:S(2)}, u32[]{:S(2)}) async-start(bf16[128,72,128]{2,1,0:T(8,128)(2,1)} %get-tuple-element.13), calls=%async_computation | async-start | bytes 4718592 | tf_op jit(solution)/shard_map/all_to_all | solution.py:605
  18.7 0.3 reduce-window.9
  19.0 0.1 slice.39
  19.1 0.1 pad_add_fusion.4.place_ref
  19.2 0.1 slice_reduce_fusion
  19.3 0.1 fusion
  19.4 0.2 convert_reduce_fusion.first_ref
  19.6 4.3 %side.1 = (f32[96,48,128]{2,1,0:T(8,128)S(1)}, f32[16,16,128]{2,1,0:T(8,128)S(1)}) custom-call(s32[16]{0:T(128)S(1)} %convert_reduce_fusion.first_ref, s32[3]{0:T(128)S(1)} %pad_add_fusion.4.place_ref, bf16[96,48,128]{2,1,0:T(8,128)(2,1)S(1)} %copy-done.1, f32[1,128]{1,0:T(1,128)S(1)} %copy-done.12, bf16[128,640]{1,0:T(8,128)(2,1)S(1)} %copy-done.5, ...), custom_call_target="tpu_custom_call" | custom-call | flops 603979776 | bytes 5000000 | tf_op jit(solution)/shard_map/side/pallas_call | solution.py:469
  23.9 1.4 %copy-done = f32[96,48,128]{2,1,0:T(8,128)} copy-done((f32[96,48,128]{2,1,0:T(8,128)}, f32[96,48,128]{2,1,0:T(8,128)S(1)}, u32[]{:S(2)}) %copy-start) | copy-done | bytes 2359320
  25.4 3.4 %collective-permute-start.2 = (f32[4,16,128]{2,1,0:T(8,128)S(1)}, f32[4,16,128]{2,1,0:T(8,128)S(1)}, u32[]{:S(2)}, u32[]{:S(2)}) collective-permute-start(f32[4,16,128]{2,1,0:T(8,128)S(1)} %get-tuple-element.28), channel_id=1, source_target_pairs={{0,4},{1,5},{2,6},{3,7},{4,0},{5,1},{6,2},{7,3},{8,12},{9,13},{10,... | collective-permute-start | bytes 98312 | tf_op jit(solution)/shard_map/ppermute | solution.py:627
  28.7 1.2 %collective-permute-start.3 = (f32[4,16,128]{2,1,0:T(8,128)S(1)}, f32[4,16,128]{2,1,0:T(8,128)S(1)}, u32[]{:S(2)}, u32[]{:S(2)}) collective-permute-start(f32[4,16,128]{2,1,0:T(8,128)S(1)} %get-tuple-element.27), channel_id=1, source_target_pairs={{0,8},{1,9},{2,10},{3,11},{4,12},{5,13},{6,14},{7,15},{8,0},{9,1},... | collective-permute-start | bytes 98312 | tf_op jit(solution)/shard_map/ppermute | solution.py:627
  30.0 4.1 %collective-permute-start = (bf16[48,128]{1,0:T(8,128)(2,1)S(1)}, bf16[48,128]{1,0:T(8,128)(2,1)S(1)}, u32[]{:S(2)}, u32[]{:S(2)}) collective-permute-start(bf16[48,128]{1,0:T(8,128)(2,1)S(1)} %get-tuple-element.31), channel_id=1, source_target_pairs={{0,1},{1,2},{2,3},{3,4},{4,5},{5,6},{6,7},{7,8},{8,9},{9,10},{10,1... | collective-permute-start | bytes 36872 | tf_op jit(solution)/shard_map/ppermute | solution.py:632
  34.1 1.9 %collective-permute-start.1 = (bf16[48,128]{1,0:T(8,128)(2,1)S(1)}, bf16[48,128]{1,0:T(8,128)(2,1)S(1)}, u32[]{:S(2)}, u32[]{:S(2)}) collective-permute-start(bf16[48,128]{1,0:T(8,128)(2,1)S(1)} %get-tuple-element.30), channel_id=1, source_target_pairs={{1,0},{2,1},{3,2},{4,3},{5,4},{6,5},{7,6},{8,7},{9,8},{10,9},{11,1... | collective-permute-start | bytes 36872 | tf_op jit(solution)/shard_map/ppermute | solution.py:633
  36.0 10.3 %collective-permute-done.1.after_ref = bf16[48,128]{1,0:T(8,128)(2,1)S(1)} collective-permute-done((bf16[48,128]{1,0:T(8,128)(2,1)S(1)}, bf16[48,128]{1,0:T(8,128)(2,1)S(1)}, u32[]{:S(2)}, u32[]{:S(2)}) %collective-permute-start.1) | collective-permute-done | bytes 12320 | tf_op jit(solution)/shard_map/ppermute | solution.py:633
  46.3 0.7 collective-permute-done.2
  47.1 0.7 collective-permute-done.4
  47.8 4.1 %all-to-all-done.arrived_ref = bf16[128,72,128]{2,1,0:T(8,128)(2,1)} async-done(((bf16[128,72,128]{2,1,0:T(8,128)(2,1)}), bf16[128,72,128]{2,1,0:T(8,128)(2,1)}, u32[]{:S(2)}, u32[]{:S(2)}) %all-to-all-start) | async-done | bytes 2359328 | tf_op jit(solution)/shard_map/all_to_all | solution.py:605
  51.9 5.3 %triangle.1 = bf16[576,8,128]{2,1,0:T(8,128)(2,1)} custom-call(bf16[128,72,128]{2,1,0:T(8,128)(2,1)} %all-to-all-done.arrived_ref), custom_call_target="tpu_custom_call" | custom-call | flops 1610612736 | bytes 4000000 | tf_op jit(solution)/shard_map/triangle/pallas_call | solution.py:274
  57.2 5.9 %all-to-all-start.1 = ((bf16[128,9,4,128]{3,2,1,0:T(4,128)(2,1)}), bf16[128,9,4,128]{3,2,1,0:T(4,128)(2,1)S(1)}, u32[]{:S(2)}, u32[]{:S(2)}) async-start(bf16[128,9,4,128]{3,2,1,0:T(4,128)(2,1)} %bitcast.8), calls=%async_computation.1 | async-start | bytes 2359296 | tf_op jit(solution)/shard_map/all_to_all | solution.py:658
  63.1 0.8 convert_reduce_fusion.1
  65.2 1.1 %collective-permute-start.5 = (f32[1,16,128]{2,1,0:T(8,128)S(1)}, f32[1,16,128]{2,1,0:T(8,128)S(1)}, u32[]{:S(2)}, u32[]{:S(2)}) collective-permute-start(f32[1,16,128]{2,1,0:T(8,128)S(1)} %get-tuple-element.34), channel_id=1, source_target_pairs={{0,1},{1,0},{2,3},{3,2},{4,5},{5,4},{6,7},{7,6},{8,9},{9,8},{10,11... | collective-permute-start | bytes 24584 | tf_op jit(solution)/shard_map/ppermute | solution.py:627
  66.4 0.8 collective-permute-start.6
  67.2 0.9 %collective-permute-start.7 = (f32[1,16,128]{2,1,0:T(8,128)S(1)}, f32[1,16,128]{2,1,0:T(8,128)S(1)}, u32[]{:S(2)}, u32[]{:S(2)}) collective-permute-start(f32[1,16,128]{2,1,0:T(8,128)S(1)} %get-tuple-element.32), channel_id=1, source_target_pairs={{0,3},{1,2},{2,1},{3,0},{4,7},{5,6},{6,5},{7,4},{8,11},{9,10},{10,... | collective-permute-start | bytes 24584 | tf_op jit(solution)/shard_map/ppermute | solution.py:627
  69.4 0.1 dynamic_slice.14
  69.6 0.1 broadcast_in_dim_tile.8.sub_start_ref
  69.7 0.1 broadcast_in_dim_tile.9.sub_end_ref
  69.8 4.1 %collective-permute-done.6.band2_ref = f32[1,16,128]{2,1,0:T(8,128)S(1)} collective-permute-done((f32[1,16,128]{2,1,0:T(8,128)S(1)}, f32[1,16,128]{2,1,0:T(8,128)S(1)}, u32[]{:S(2)}, u32[]{:S(2)}) %collective-permute-start.6) | collective-permute-done | bytes 8224 | tf_op jit(solution)/shard_map/ppermute | solution.py:627
  73.9 0.3 collective-permute-done.7.band3_ref
  74.3 3.8 %atoms_block.1 = bf16[192,128]{1,0:T(8,128)(2,1)} custom-call(s32[1]{0:T(128)} %bitcast.11.base_ref, bf16[192,128]{1,0:T(8,128)(2,1)S(1)} %copy-done.3, bf16[48,128]{1,0:T(8,128)(2,1)S(1)} %collective-permute-done.before_ref, bf16[48,128]{1,0:T(8,128)(2,1)S(1)} %collective-permute-done.1.after_ref, f32[1,16,128]{2,1,0:T(8,128)S(1)} %get-tuple-element.35.band0_ref, ...), custom_call_target="tpu_custom_call" | custom-call | flops 800000000 | bytes 2000000 | tf_op jit(solution)/shard_map/atoms_block/pallas_call | solution.py:571
  78.1 6.0 %all-to-all-done.1 = bf16[128,9,4,128]{3,2,1,0:T(4,128)(2,1)S(1)} async-done(((bf16[128,9,4,128]{3,2,1,0:T(4,128)(2,1)}), bf16[128,9,4,128]{3,2,1,0:T(4,128)(2,1)S(1)}, u32[]{:S(2)}, u32[]{:S(2)}) %all-to-all-start.1) | async-done | bytes 1179680 | tf_op jit(solution)/shard_map/all_to_all | solution.py:658
  84.1 3.5 %update_pair.1 = bf16[96,48,128]{2,1,0:T(8,128)(2,1)} custom-call(s32[1]{0:T(128)} %bitcast.odd_ref, bf16[576,8,128]{2,1,0:T(8,128)(2,1)S(1)} %bitcast.20, bf16[96,48,128]{2,1,0:T(8,128)(2,1)S(1)} %copy-done.1, f32[96,48,128]{2,1,0:T(8,128)} %copy-done, f32[1,128]{1,0:T(1,128)S(1)} %bitcast.21, bf16[128,128]{1,0:T(8,128)(2,1)S(1)} %copy-done.2), custom_call_target="tpu_custom_call" | custom-call | flops 150994944 | bytes 6000000 | tf_op jit(solution)/shard_map/update_pair/pallas_call | solution.py:383
  (46 shorter events, 0.4 us)
Async XLA Ops:
  6.7 12.0 %copy-start.13 = (s32[768]{0:T(1024)S(1)}, s32[768]{0:T(1024)}, u32[]{:S(2)}) copy-start(s32[768]{0:T(1024)} %param.16) | copy-start | bytes 9220
  6.7 12.4 %copy-start.14 = (f32[128,4]{0,1:T(4,128)S(1)}, f32[128,4]{0,1:T(4,128)}, u32[]{:S(2)}) copy-start(f32[128,4]{0,1:T(4,128)} %param.21) | copy-start | bytes 6148
  6.7 12.8 %copy-start.1 = (bf16[96,48,128]{2,1,0:T(8,128)(2,1)S(1)}, bf16[96,48,128]{2,1,0:T(8,128)(2,1)}, u32[]{:S(2)}) copy-start(bf16[96,48,128]{2,1,0:T(8,128)(2,1)} %pair_ref.5) | copy-start | bytes 3538948
  6.8 12.8 %copy-start.5 = (bf16[128,640]{1,0:T(8,128)(2,1)S(1)}, bf16[128,640]{1,0:T(8,128)(2,1)}, u32[]{:S(2)}) copy-start(bf16[128,640]{1,0:T(8,128)(2,1)} %weight_ref.4) | copy-start | bytes 491524
  6.8 12.8 %copy-start.12 = (f32[1,128]{1,0:T(1,128)S(1)}, f32[1,128]{1,0:T(1,128)}, u32[]{:S(2)}) copy-start(f32[1,128]{1,0:T(1,128)} %get-tuple-element.14.gain_ref) | copy-start | bytes 1540
  6.8 45.1 %all-to-all-start = ((bf16[128,72,128]{2,1,0:T(8,128)(2,1)}), bf16[128,72,128]{2,1,0:T(8,128)(2,1)}, u32[]{:S(2)}, u32[]{:S(2)}) async-start(bf16[128,72,128]{2,1,0:T(8,128)(2,1)} %get-tuple-element.13), calls=%async_computation | async-start | bytes 4718592 | tf_op jit(solution)/shard_map/all_to_all | solution.py:605
  19.6 10.4 %copy-start.3 = (bf16[192,128]{1,0:T(8,128)(2,1)S(1)}, bf16[192,128]{1,0:T(8,128)(2,1)}, u32[]{:S(2)}) copy-start(bf16[192,128]{1,0:T(8,128)(2,1)} %atoms_ref.1) | copy-start | bytes 147460
  23.9 1.4 %copy-start = (f32[96,48,128]{2,1,0:T(8,128)}, f32[96,48,128]{2,1,0:T(8,128)S(1)}, u32[]{:S(2)}) copy-start(f32[96,48,128]{2,1,0:T(8,128)S(1)} %get-tuple-element.17.gate_ref) | copy-start | bytes 7077892
  25.4 21.7 %collective-permute-start.2 = (f32[4,16,128]{2,1,0:T(8,128)S(1)}, f32[4,16,128]{2,1,0:T(8,128)S(1)}, u32[]{:S(2)}, u32[]{:S(2)}) collective-permute-start(f32[4,16,128]{2,1,0:T(8,128)S(1)} %get-tuple-element.28), channel_id=1, source_target_pairs={{0,4},{1,5},{2,6},{3,7},{4,0},{5,1},{6,2},{7,3},{8,12},{9,13},{10,... | collective-permute-start | bytes 98312 | tf_op jit(solution)/shard_map/ppermute | solution.py:627
  28.7 18.4 %collective-permute-start.3 = (f32[4,16,128]{2,1,0:T(8,128)S(1)}, f32[4,16,128]{2,1,0:T(8,128)S(1)}, u32[]{:S(2)}, u32[]{:S(2)}) collective-permute-start(f32[4,16,128]{2,1,0:T(8,128)S(1)} %get-tuple-element.27), channel_id=1, source_target_pairs={{0,8},{1,9},{2,10},{3,11},{4,12},{5,13},{6,14},{7,15},{8,0},{9,1},... | collective-permute-start | bytes 98312 | tf_op jit(solution)/shard_map/ppermute | solution.py:627
  30.0 17.8 %collective-permute-start.4 = (f32[4,16,128]{2,1,0:T(8,128)S(1)}, f32[4,16,128]{2,1,0:T(8,128)S(1)}, u32[]{:S(2)}, u32[]{:S(2)}) collective-permute-start(f32[4,16,128]{2,1,0:T(8,128)S(1)} %get-tuple-element.26), channel_id=1, source_target_pairs={{0,12},{1,13},{2,14},{3,15},{4,8},{5,9},{6,10},{7,11},{8,4},{9,5},... | collective-permute-start | bytes 98312 | tf_op jit(solution)/shard_map/ppermute | solution.py:627
  30.0 6.0 %collective-permute-start = (bf16[48,128]{1,0:T(8,128)(2,1)S(1)}, bf16[48,128]{1,0:T(8,128)(2,1)S(1)}, u32[]{:S(2)}, u32[]{:S(2)}) collective-permute-start(bf16[48,128]{1,0:T(8,128)(2,1)S(1)} %get-tuple-element.31), channel_id=1, source_target_pairs={{0,1},{1,2},{2,3},{3,4},{4,5},{5,6},{6,7},{7,8},{8,9},{9,10},{10,1... | collective-permute-start | bytes 36872 | tf_op jit(solution)/shard_map/ppermute | solution.py:632
  34.1 12.2 %collective-permute-start.1 = (bf16[48,128]{1,0:T(8,128)(2,1)S(1)}, bf16[48,128]{1,0:T(8,128)(2,1)S(1)}, u32[]{:S(2)}, u32[]{:S(2)}) collective-permute-start(bf16[48,128]{1,0:T(8,128)(2,1)S(1)} %get-tuple-element.30), channel_id=1, source_target_pairs={{1,0},{2,1},{3,2},{4,3},{5,4},{6,5},{7,6},{8,7},{9,8},{10,9},{11,1... | collective-permute-start | bytes 36872 | tf_op jit(solution)/shard_map/ppermute | solution.py:633
  57.2 17.1 %copy-start.6 = (bf16[128,512]{1,0:T(8,128)(2,1)S(1)}, bf16[128,512]{1,0:T(8,128)(2,1)}, u32[]{:S(2)}) copy-start(bf16[128,512]{1,0:T(8,128)(2,1)} %project_ref.1) | copy-start | bytes 393220
  57.2 17.0 %copy-start.7 = (bf16[128,512]{1,0:T(8,128)(2,1)S(1)}, bf16[128,512]{1,0:T(8,128)(2,1)}, u32[]{:S(2)}) copy-start(bf16[128,512]{1,0:T(8,128)(2,1)} %up_ref.1) | copy-start | bytes 393220
  57.2 17.0 %copy-start.8 = (bf16[256,128]{1,0:T(8,128)(2,1)S(1)}, bf16[256,128]{1,0:T(8,128)(2,1)}, u32[]{:S(2)}) copy-start(bf16[256,128]{1,0:T(8,128)(2,1)} %down_ref.1) | copy-start | bytes 196612
  57.2 17.0 %copy-start.9 = (bf16[128,128]{1,0:T(8,128)(2,1)S(1)}, bf16[128,128]{1,0:T(8,128)(2,1)}, u32[]{:S(2)}) copy-start(bf16[128,128]{1,0:T(8,128)(2,1)} %output_ref.1) | copy-start | bytes 98308
  57.2 17.0 %copy-start.10 = (f32[128]{0:T(128)S(1)}, f32[128]{0:T(128)}, u32[]{:S(2)}) copy-start(f32[128]{0:T(128)} %param.22) | copy-start | bytes 1540
  57.2 17.0 %copy-start.11 = (f32[128]{0:T(128)S(1)}, f32[128]{0:T(128)}, u32[]{:S(2)}) copy-start(f32[128]{0:T(128)} %param.25) | copy-start | bytes 1540
  57.2 26.9 %all-to-all-start.1 = ((bf16[128,9,4,128]{3,2,1,0:T(4,128)(2,1)}), bf16[128,9,4,128]{3,2,1,0:T(4,128)(2,1)S(1)}, u32[]{:S(2)}, u32[]{:S(2)}) async-start(bf16[128,9,4,128]{3,2,1,0:T(4,128)(2,1)} %bitcast.8), calls=%async_computation.1 | async-start | bytes 2359296 | tf_op jit(solution)/shard_map/all_to_all | solution.py:658
  65.2 4.6 %collective-permute-start.5 = (f32[1,16,128]{2,1,0:T(8,128)S(1)}, f32[1,16,128]{2,1,0:T(8,128)S(1)}, u32[]{:S(2)}, u32[]{:S(2)}) collective-permute-start(f32[1,16,128]{2,1,0:T(8,128)S(1)} %get-tuple-element.34), channel_id=1, source_target_pairs={{0,1},{1,0},{2,3},{3,2},{4,5},{5,4},{6,7},{7,6},{8,9},{9,8},{10,11... | collective-permute-start | bytes 24584 | tf_op jit(solution)/shard_map/ppermute | solution.py:627
  66.4 7.6 %collective-permute-start.6 = (f32[1,16,128]{2,1,0:T(8,128)S(1)}, f32[1,16,128]{2,1,0:T(8,128)S(1)}, u32[]{:S(2)}, u32[]{:S(2)}) collective-permute-start(f32[1,16,128]{2,1,0:T(8,128)S(1)} %get-tuple-element.33), channel_id=1, source_target_pairs={{0,2},{1,3},{2,0},{3,1},{4,6},{5,7},{6,4},{7,5},{8,10},{9,11},{10,... | collective-permute-start | bytes 24584 | tf_op jit(solution)/shard_map/ppermute | solution.py:627
  67.2 7.0 %collective-permute-start.7 = (f32[1,16,128]{2,1,0:T(8,128)S(1)}, f32[1,16,128]{2,1,0:T(8,128)S(1)}, u32[]{:S(2)}, u32[]{:S(2)}) collective-permute-start(f32[1,16,128]{2,1,0:T(8,128)S(1)} %get-tuple-element.32), channel_id=1, source_target_pairs={{0,3},{1,2},{2,1},{3,0},{4,7},{5,6},{6,5},{7,4},{8,11},{9,10},{10,... | collective-permute-start | bytes 24584 | tf_op jit(solution)/shard_map/ppermute | solution.py:627
  74.3 9.9 %copy-start.2 = (bf16[128,128]{1,0:T(8,128)(2,1)S(1)}, bf16[128,128]{1,0:T(8,128)(2,1)}, u32[]{:S(2)}) copy-start(bf16[128,128]{1,0:T(8,128)(2,1)} %weight_ref.5) | copy-start | bytes 98308
  74.3 9.8 %copy-start.4 = (f32[128]{0:T(128)S(1)}, f32[128]{0:T(128)}, u32[]{:S(2)}) copy-start(f32[128]{0:T(128)} %param.20) | copy-start | bytes 1540
